TPU v7x, 256 devices: a whole 4x4x8 slice. The times are simulated.
256 devices in a mesh: frame: 32 (over z, x_hi, core), band: 8 (over x_lo, y).
Axes of the slice: x: 4 (x_hi: 2, x_lo: 2; x = x_hi * 2 + x_lo), y: 4, z: 8, core: 2. Of those that a mesh axis runs over, the one named last changes fastest.
Arguments:
- frames: bfloat16 [256, 64, 16, 320], P('frame', 'band'), may hold values from -6 to 6
- control: bfloat16 [256, 64, 16, 320], P('frame', 'band'), may hold values from -4 to 4
- conv_first: bfloat16 [3, 3, 320, 320], replicated, may hold values from -0.109375 to 0.109375
- conv_second: bfloat16 [3, 3, 320, 320], replicated, may hold values from -0.109375 to 0.109375
- time_table: float32 [1000, 320], replicated, may hold values from -5 to 5
- step_index: int32 [1], replicated, may hold values from 0 to 999
- norm_gain: float32 [320], replicated, may hold values from 0.5 to 1.5
- w_query: bfloat16 [320, 320], replicated, as said below
- w_key: bfloat16 [320, 320], replicated, as said below
- w_value: bfloat16 [320, 320], replicated, may hold values from -0.3125 to 0.3125
- w_out: bfloat16 [320, 320], replicated, may hold values from -0.3125 to 0.3125
- rel_bias: float32 [8, 33], replicated, may hold values from -4 to 4
- reach: int32 [256], replicated, may hold values from 4 to 16, as said below
Outputs:
- section_out: float32 [256, 64, 16, 320], P('frame', 'band')
Inputs may be any that keep to these rules, and one draw needn't show every extreme that they name: Each frame attends within reach[f] frames on the loop; the first and last frame of each aligned block of 8 frames have reach 16. `w_query`: projection into 8 heads. `w_key`: projection into 8 heads.
All inputs are finite; a program needn't handle non-finite values.
Results may differ from a plain program's by a relative error of at most 0.012.
The roundings to bfloat16 on the way count: a program that leaves them out, or rounds other values in their place, can miss the bound.
Values may be sent and summed in bfloat16 or wider, within the bound.
No kernel may reach another device: no remote copies, remote signals or barrier semaphores. Data moves between devices by JAX's collectives and lax.ppermute only.
A program may use at most 128 MiB of HBM per device.

v0:
```python
import jax
import jax.numpy as jnp
from jax import lax
from jax.sharding import PartitionSpec as P


def with_halo(block, sides, width):
    for axis, dim in sides:
        count = lax.axis_size(axis)
        forward = [(i, i + 1) for i in range(count - 1)]
        backward = [(target, source) for source, target in forward]
        low = lax.ppermute(
            lax.slice_in_dim(block, block.shape[dim] - width, None, axis=dim), axis, forward
        )
        high = lax.ppermute(lax.slice_in_dim(block, 0, width, axis=dim), axis, backward)
        block = jnp.concatenate([low, block, high], axis=dim)
    return block


def passed_along(block, axis, distance):
    devices = range(lax.axis_size(axis))
    route = [((i - distance) % len(devices), i) for i in devices]
    return lax.ppermute(block, axis, route)


def conv_pass(field, weight):
    rimmed = with_halo(field, (("band", 1),), 1)
    return lax.conv_general_dilated(
        rimmed,
        weight,
        (1, 1),
        ((0, 0), (1, 1)),
        dimension_numbers=("NHWC", "HWIO", "NHWC"),
        preferred_element_type=jnp.float32,
    )


def attend(query, key, value, q_frames, k_frames, reach_q, rel_bias, total):
    heads = rel_bias.shape[0]
    span = (rel_bias.shape[1] - 1) // 2
    fq, pix, chans = query.shape
    fk = key.shape[0]
    dh = chans // heads
    q4 = query.reshape(fq, pix, heads, dh)
    k4 = key.reshape(fk, pix, heads, dh)
    v4 = value.reshape(fk, pix, heads, dh)
    scores = jnp.einsum("iphd,jphd->phij", q4, k4, preferred_element_type=jnp.float32) * dh ** (
        -0.5
    )
    delta = (k_frames[None, :] - q_frames[:, None] + total // 2) % total - total // 2
    table = (
        delta[:, :, None] + span == jnp.arange(2 * span + 1, dtype=jnp.int32)[None, None, :]
    ).astype(jnp.float32)
    bias = jnp.einsum("ijs,hs->hij", table, rel_bias, precision=lax.Precision.HIGHEST)
    allowed = jnp.abs(delta) <= reach_q[:, None]
    scores = jnp.where(allowed[None, None], scores + bias[None], -jnp.inf)
    top = jnp.max(scores, axis=-1, keepdims=True)
    expo = jnp.exp(scores - top)
    weights = (expo / jnp.sum(expo, axis=-1, keepdims=True)).astype(jnp.bfloat16)
    out = jnp.einsum("phij,jphd->iphd", weights, v4, preferred_element_type=jnp.float32)
    return out.astype(jnp.bfloat16).reshape(fq, pix, chans)


def shards(
    frames,
    control,
    conv_first,
    conv_second,
    time_table,
    step_index,
    norm_gain,
    w_query,
    w_key,
    w_value,
    w_out,
    rel_bias,
    reach,
):
    count, rows, cols, chans = frames.shape
    pixels = rows * cols
    members = lax.axis_size("frame")
    total = count * members
    start = lax.axis_index("frame") * count
    picker = (jnp.arange(time_table.shape[0], dtype=jnp.int32) == step_index[0]).astype(jnp.float32)
    embed = jnp.dot(picker, time_table, precision=lax.Precision.HIGHEST)
    merged = (frames.astype(jnp.float32) + control.astype(jnp.float32)).astype(jnp.bfloat16)
    activated = jax.nn.silu(conv_pass(merged, conv_first) + embed).astype(jnp.bfloat16)
    block_out = merged.astype(jnp.float32) + conv_pass(activated, conv_second)
    flat = block_out.reshape(count * pixels, chans)
    centre = flat - jnp.mean(flat, axis=1, keepdims=True)
    normed = (
        centre * lax.rsqrt(jnp.mean(centre * centre, axis=1, keepdims=True) + 1e-05) * norm_gain
    ).astype(jnp.bfloat16)
    query = (
        jnp.dot(normed, w_query, preferred_element_type=jnp.float32)
        .astype(jnp.bfloat16)
        .reshape(count, pixels, chans)
    )
    key = (
        jnp.dot(normed, w_key, preferred_element_type=jnp.float32)
        .astype(jnp.bfloat16)
        .reshape(count, pixels, chans)
    )
    value = (
        jnp.dot(normed, w_value, preferred_element_type=jnp.float32)
        .astype(jnp.bfloat16)
        .reshape(count, pixels, chans)
    )
    span = (rel_bias.shape[1] - 1) // 2
    hops = -(-span // count)
    stacked = jnp.stack((key, value))
    pieces = []
    key_frames = []
    for offset in list(range(hops, 0, -1)) + [0] + list(range(-1, -hops - 1, -1)):
        if offset == 0:
            pieces.append(stacked)
        else:
            pieces.append(passed_along(stacked, "frame", offset))
        key_frames.append((start - offset * count + jnp.arange(count, dtype=jnp.int32)) % total)
    window = jnp.concatenate(pieces, axis=1)
    q_frames = start + jnp.arange(count, dtype=jnp.int32)
    reach_q = lax.dynamic_slice_in_dim(reach, start, count)
    attended = attend(
        query, window[0], window[1], q_frames, jnp.concatenate(key_frames), reach_q, rel_bias, total
    )
    mixed = jnp.dot(
        attended.reshape(count * pixels, chans), w_out, preferred_element_type=jnp.float32
    )
    return (flat + mixed).reshape(count, rows, cols, chans)


def solution(mesh):
    in_specs = (
        P("frame", "band", None, None),
        P("frame", "band", None, None),
        P(),
        P(),
        P(),
        P(),
        P(),
        P(),
        P(),
        P(),
        P(),
        P(),
        P(),
    )
    out_specs = P("frame", "band", None, None)
    return jax.shard_map(shards, mesh=mesh, in_specs=in_specs, out_specs=out_specs, check_vma=False)
```

profile of v0, /device:TPU:24, one launch (start us, length us, event | category | flops | bytes accessed | tf_op | source)
XLA Modules:
  0.0 194.7 jit_solution(11722900516614865301)
XLA Ops:
  0.0 2.4 %add_convert_fusion = bf16[8,8,16,320]{3,0,2,1:T(8,128)(2,1)S(1)} fusion(bf16[8,8,16,320]{3,2,1,0:T(8,128)(2,1)} %param.14, bf16[8,8,16,320]{3,2,1,0:T(8,128)(2,1)} %param.13), kind=kLoop, calls=%fused_computation.16 | loop fusion | flops 1310720 | bytes 1966080 | tf_op jit(solution)/shard_map/convert_element_type | solution.py:86
  2.4 3.1 %collective-permute-start = (bf16[8,1,16,320]{3,0,2,1:T(8,128)(2,1)S(1)}, bf16[8,1,16,320]{3,0,2,1:T(8,128)(2,1)S(1)}, u32[]{:S(2)}, u32[]{:S(2)}) collective-permute-start(bf16[8,1,16,320]{3,0,2,1:T(8,128)(2,1)S(1)} %get-tuple-element.9), channel_id=1, source_target_pairs={{0,1},{1,2},{2,3},{3,4},{4,5},{5,6},{6,7},{8,9},{9,10},{10,11},{11... | collective-permute-start | bytes 245768 | tf_op jit(solution)/shard_map/ppermute | solution.py:12
  5.5 2.8 %collective-permute-start.1 = (bf16[8,1,16,320]{3,0,2,1:T(8,128)(2,1)S(1)}, bf16[8,1,16,320]{3,0,2,1:T(8,128)(2,1)S(1)}, u32[]{:S(2)}, u32[]{:S(2)}) collective-permute-start(bf16[8,1,16,320]{3,0,2,1:T(8,128)(2,1)S(1)} %get-tuple-element.10), channel_id=1, source_target_pairs={{1,0},{2,1},{3,2},{4,3},{5,4},{6,5},{7,6},{9,8},{10,9},{11,10},{12... | collective-permute-start | bytes 245768 | tf_op jit(solution)/shard_map/ppermute | solution.py:15
  9.0 0.0 copy-done.8
  9.0 0.7 convolution_reduce_fusion
  9.7 0.0 collective-permute-done
  9.7 4.4 %collective-permute-done.1 = bf16[8,1,16,320]{3,0,2,1:T(8,128)(2,1)S(1)} collective-permute-done((bf16[8,1,16,320]{3,0,2,1:T(8,128)(2,1)S(1)}, bf16[8,1,16,320]{3,0,2,1:T(8,128)(2,1)S(1)}, u32[]{:S(2)}, u32[]{:S(2)}) %collective-permute-start.1) | collective-permute-done | bytes 81952 | tf_op jit(solution)/shard_map/ppermute | solution.py:15
  14.1 3.5 %multiply_convert_fusion.1 = bf16[8,8,16,320]{3,0,2,1:T(8,128)(2,1)S(1)} fusion(bf16[3,3,320,320]{3,2,1,0:T(8,128)(2,1)S(1)} %copy-done.13, bf16[8,1,16,320]{3,0,2,1:T(8,128)(2,1)S(1)} %collective-permute-done.1, bf16[8,8,16,320]{3,0,2,1:T(8,128)(2,1)S(1)} %add_convert_fusion, bf16[8,1,16,320]{3,0,2,1:T(8,128)(2,1)S(1)} %collective-permute-done, ...), kind=kOutput, calls=%fused_computation.14 | convolution fusion | flops 1813217280 | bytes 3319040 | tf_op jit(solution)/shard_map/conv_general_dilated | solution.py:28
  17.6 1.9 collective-permute-start.2
  19.6 3.9 %collective-permute-start.3 = (bf16[8,1,16,320]{3,0,2,1:T(8,128)(2,1)S(1)}, bf16[8,1,16,320]{3,0,2,1:T(8,128)(2,1)S(1)}, u32[]{:S(2)}, u32[]{:S(2)}) collective-permute-start(bf16[8,1,16,320]{3,0,2,1:T(8,128)(2,1)S(1)} %get-tuple-element.8), channel_id=1, source_target_pairs={{1,0},{2,1},{3,2},{4,3},{5,4},{6,5},{7,6},{9,8},{10,9},{11,10},{12... | collective-permute-start | bytes 245768 | tf_op jit(solution)/shard_map/ppermute | solution.py:15
  23.5 0.7 collective-permute-done.2
  24.1 4.0 %collective-permute-done.3 = bf16[8,1,16,320]{3,0,2,1:T(8,128)(2,1)S(1)} collective-permute-done((bf16[8,1,16,320]{3,0,2,1:T(8,128)(2,1)S(1)}, bf16[8,1,16,320]{3,0,2,1:T(8,128)(2,1)S(1)}, u32[]{:S(2)}, u32[]{:S(2)}) %collective-permute-start.3) | collective-permute-done | bytes 81952 | tf_op jit(solution)/shard_map/ppermute | solution.py:15
  28.2 4.5 %fusion.39 = (f32[8,8,16]{0,2,1:T(8,128)S(1)}, f32[8,8,16,320]{3,0,2,1:T(8,128)}) fusion(bf16[3,3,320,320]{3,2,1,0:T(8,128)(2,1)S(1)} %copy-done, bf16[8,1,16,320]{3,0,2,1:T(8,128)(2,1)S(1)} %collective-permute-done.3, bf16[8,8,16,320]{3,0,2,1:T(8,128)(2,1)S(1)} %multiply_convert_fusion.1, bf16[8,1,16,320]{3,0,2,1:T(8,128)(2,1)S(1)} %collective-permute-done.2, ...), kind=kOutput, calls=%fused_computation.86 | convolution fusion | flops 1812233216 | bytes 4632576 | tf_op jit(solution)/shard_map/conv_general_dilated | solution.py:28
  32.7 0.1 copy.49
  32.8 0.1 copy.50
  32.9 0.1 div.22
  32.9 0.0 copy-start.12
  33.0 1.8 copy.48
  34.8 0.0 copy-done.3
  34.8 0.4 multiply_reduce_fusion
  35.2 0.1 copy.51
  35.3 0.1 rsqrt.12
  35.4 0.3 multiply_convert_fusion
  35.8 0.0 copy-start.10
  35.8 0.6 fusion.8
  36.4 0.1 copy.61
  36.5 0.9 copy-done.4
  37.4 0.9 copy_dynamic-update-slice_fusion.3
  38.3 0.0 copy-done.10
  38.3 0.6 fusion.9
  38.9 0.1 copy.62
  39.0 0.8 copy-done.6
  39.9 0.9 copy_dynamic-update-slice_fusion.1
  40.8 2.7 %collective-permute-start.4 = (bf16[2,8,128,320]{2,3,1,0:T(8,128)(2,1)}, bf16[2,8,128,320]{2,3,1,0:T(8,128)(2,1)}, u32[]{:S(2)}, u32[]{:S(2)}) collective-permute-start(bf16[2,8,128,320]{2,3,1,0:T(8,128)(2,1)} %copy_dynamic-update-slice_fusion.1), channel_id=1, source_target_pairs={{240,0},{248,8},{0,16},{8,24},{16,32},{24,40},{32,48},{40,56},{48,... | collective-permute-start | bytes 3932168 | tf_op jit(solution)/shard_map/ppermute | solution.py:23
  43.5 0.0 collective-permute-start.5
  43.6 0.1 concatenate.15
  43.7 0.1 fusion.26
  43.7 5.4 %collective-permute-start.6 = (bf16[2,8,128,320]{2,3,1,0:T(8,128)(2,1)}, bf16[2,8,128,320]{2,3,1,0:T(8,128)(2,1)}, u32[]{:S(2)}, u32[]{:S(2)}) collective-permute-start(bf16[2,8,128,320]{2,3,1,0:T(8,128)(2,1)} %copy_dynamic-update-slice_fusion.1), channel_id=1, source_target_pairs={{8,0},{16,8},{24,16},{32,24},{40,32},{48,40},{56,48},{64,56},{72,6... | collective-permute-start | bytes 3932168 | tf_op jit(solution)/shard_map/ppermute | solution.py:23
  49.1 0.4 convolution_bitcast_fusion
  49.6 0.1 dynamic_slice.3
  49.7 3.4 %collective-permute-start.7 = (bf16[2,8,128,320]{2,3,1,0:T(8,128)(2,1)}, bf16[2,8,128,320]{2,3,1,0:T(8,128)(2,1)}, u32[]{:S(2)}, u32[]{:S(2)}) collective-permute-start(bf16[2,8,128,320]{2,3,1,0:T(8,128)(2,1)} %copy_dynamic-update-slice_fusion.1), channel_id=1, source_target_pairs={{16,0},{24,8},{32,16},{40,24},{48,32},{56,40},{64,48},{72,56},{80,... | collective-permute-start | bytes 3932168 | tf_op jit(solution)/shard_map/ppermute | solution.py:23
  53.1 0.1 abs_compare_fusion
  53.2 0.6 fusion.10
  53.7 0.1 copy.63
  53.8 4.2 %copy.54 = bf16[8,128,8,40]{3,0,2,1:T(8,128)(2,1)} copy(bf16[8,128,8,40]{1,0,3,2:T(8,128)(2,1)S(1)} %bitcast.63) | data formatting | bytes 1310720 | tf_op jit(solution)/shard_map/reshape;reshape | solution.py:44
  58.0 0.4 copy.59
  58.5 56.7 %collective-permute-done.4 = bf16[2,8,128,320]{2,3,1,0:T(8,128)(2,1)} collective-permute-done((bf16[2,8,128,320]{2,3,1,0:T(8,128)(2,1)}, bf16[2,8,128,320]{2,3,1,0:T(8,128)(2,1)}, u32[]{:S(2)}, u32[]{:S(2)}) %collective-permute-start.4) | collective-permute-done | bytes 1310752 | tf_op jit(solution)/shard_map/ppermute | solution.py:23
  115.2 1.4 constant_dynamic-update-slice_fusion.3
  116.6 0.0 collective-permute-done.5
  116.6 1.6 constant_dynamic-update-slice_fusion.2
  118.2 0.1 copy_dynamic-update-slice_fusion.2
  118.4 0.1 copy_dynamic-update-slice_fusion
  118.5 0.0 collective-permute-done.6
  118.5 1.5 constant_dynamic-update-slice_fusion.1
  120.0 11.5 %collective-permute-done.7 = bf16[2,8,128,320]{2,3,1,0:T(8,128)(2,1)} collective-permute-done((bf16[2,8,128,320]{2,3,1,0:T(8,128)(2,1)}, bf16[2,8,128,320]{2,3,1,0:T(8,128)(2,1)}, u32[]{:S(2)}, u32[]{:S(2)}) %collective-permute-start.7) | collective-permute-done | bytes 1310752 | tf_op jit(solution)/shard_map/ppermute | solution.py:23
  131.5 1.5 constant_dynamic-update-slice_fusion
  133.0 3.1 %fusion.36 = (bf16[1,40,128,320]{2,3,1,0:T(8,128)(2,1)}, bf16[1,40,128,320]{2,3,1,0:T(8,128)(2,1)}) fusion(bf16[2,40,128,320]{2,3,1,0:T(8,128)(2,1)S(1)} %constant_dynamic-update-slice_fusion), kind=kLoop, calls=%fused_computation.83 | loop fusion | bytes 13107200 | tf_op jit(solution)/shard_map/slice | solution.py:124
  136.1 15.4 %copy.55 = bf16[40,128,8,40]{3,0,2,1:T(8,128)(2,1)} copy(bf16[40,128,8,40]{1,3,2,0:T(8,128)(2,1)} %bitcast.57) | data formatting | bytes 6553600 | tf_op jit(solution)/shard_map/reshape;squeeze | solution.py:45
  151.5 15.6 %copy.57 = bf16[40,128,8,40]{3,0,2,1:T(8,128)(2,1)} copy(bf16[40,128,8,40]{1,3,2,0:T(8,128)(2,1)} %bitcast.56) | data formatting | bytes 6553600 | tf_op jit(solution)/shard_map/reshape;squeeze | solution.py:46
  167.1 10.6 %fusion.40 = (f32[128,8,8]{2,1,0:T(8,128)}, f32[128,8,8,40]{3,2,1,0:T(8,128)}) fusion(f32[8,8,40]{2,1,0:T(8,128)S(1)} %copy.56, pred[8,40]{1,0:T(8,128)(4,1)S(1)} %abs_compare_fusion, bf16[8,128,8,40]{3,0,2,1:T(8,128)(2,1)S(1)} %copy-done.2, bf16[40,128,8,40]{3,0,2,1:T(8,128)(2,1)} %copy.55), kind=kOutput, calls=%fused_computation.87 | convolution fusion | flops 27852840 | bytes 5286208 | tf_op jit(solution)/shard_map/sub | solution.py:58
  177.6 8.2 %convert_bitcast_fusion = bf16[8,128,8,40]{3,0,2,1:T(8,128)(2,1)S(1)} fusion(bf16[40,128,8,40]{3,0,2,1:T(8,128)(2,1)} %copy.57, f32[128,8,8,40]{3,2,1,0:T(8,128)} %get-tuple-element.14, f32[128,8,8]{2,1,0:T(8,128)} %get-tuple-element.13), kind=kOutput, calls=%fused_computation.6 | convolution fusion | flops 27197440 | bytes 5275648 | tf_op jit(solution)/shard_map/phij,jphd->iphd/dot_general | solution.py:60
  185.8 3.0 %copy.58 = bf16[8,128,8,40]{1,0,3,2:T(8,128)(2,1)} copy(bf16[8,128,8,40]{3,0,2,1:T(8,128)(2,1)S(1)} %convert_bitcast_fusion) | data formatting | bytes 1310720 | tf_op jit(solution)/shard_map/convert_element_type | solution.py:61
  188.9 2.9 %convolution_add_fusion = f32[1024,320]{0,1:T(8,128)} fusion(f32[1024,320]{0,1:T(8,128)S(1)} %copy.59, bf16[320,320]{1,0:T(8,128)(2,1)} %param.23, bf16[40,8,8,128]{3,2,1,0:T(8,128)(2,1)} %bitcast.62), kind=kOutput, calls=%fused_computation.17 | convolution fusion | flops 210042880 | bytes 3481600 | tf_op jit(solution)/shard_map/dot_general | solution.py:126
  191.8 2.9 %copy.60 = f32[1024,320]{1,0:T(8,128)} copy(f32[1024,320]{0,1:T(8,128)} %convolution_add_fusion) | data formatting | bytes 2621440 | tf_op jit(solution)/shard_map/add | solution.py:129
  (35 shorter events, 0.2 us)
Async XLA Ops:
  0.0 28.2 %copy-start = (bf16[3,3,320,320]{3,2,1,0:T(8,128)(2,1)S(1)}, bf16[3,3,320,320]{3,2,1,0:T(8,128)(2,1)}, u32[]{:S(2)}) copy-start(bf16[3,3,320,320]{3,2,1,0:T(8,128)(2,1)} %param.16) | copy-start | bytes 5529604
  0.0 9.0 %copy-start.8 = (f32[1000,320]{0,1:T(8,128)S(1)}, f32[1000,320]{0,1:T(8,128)}, u32[]{:S(2)}) copy-start(f32[1000,320]{0,1:T(8,128)} %param.17) | copy-start | bytes 3840004
  0.0 14.1 %copy-start.13 = (bf16[3,3,320,320]{3,2,1,0:T(8,128)(2,1)S(1)}, bf16[3,3,320,320]{3,2,1,0:T(8,128)(2,1)}, u32[]{:S(2)}) copy-start(bf16[3,3,320,320]{3,2,1,0:T(8,128)(2,1)} %param.15) | copy-start | bytes 5529604
  2.4 7.3 %collective-permute-start = (bf16[8,1,16,320]{3,0,2,1:T(8,128)(2,1)S(1)}, bf16[8,1,16,320]{3,0,2,1:T(8,128)(2,1)S(1)}, u32[]{:S(2)}, u32[]{:S(2)}) collective-permute-start(bf16[8,1,16,320]{3,0,2,1:T(8,128)(2,1)S(1)} %get-tuple-element.9), channel_id=1, source_target_pairs={{0,1},{1,2},{2,3},{3,4},{4,5},{5,6},{6,7},{8,9},{9,10},{10,11},{11... | collective-permute-start | bytes 245768 | tf_op jit(solution)/shard_map/ppermute | solution.py:12
  5.5 8.6 %collective-permute-start.1 = (bf16[8,1,16,320]{3,0,2,1:T(8,128)(2,1)S(1)}, bf16[8,1,16,320]{3,0,2,1:T(8,128)(2,1)S(1)}, u32[]{:S(2)}, u32[]{:S(2)}) collective-permute-start(bf16[8,1,16,320]{3,0,2,1:T(8,128)(2,1)S(1)} %get-tuple-element.10), channel_id=1, source_target_pairs={{1,0},{2,1},{3,2},{4,3},{5,4},{6,5},{7,6},{9,8},{10,9},{11,10},{12... | collective-permute-start | bytes 245768 | tf_op jit(solution)/shard_map/ppermute | solution.py:15
  17.6 6.5 %collective-permute-start.2 = (bf16[8,1,16,320]{3,0,2,1:T(8,128)(2,1)S(1)}, bf16[8,1,16,320]{3,0,2,1:T(8,128)(2,1)S(1)}, u32[]{:S(2)}, u32[]{:S(2)}) collective-permute-start(bf16[8,1,16,320]{3,0,2,1:T(8,128)(2,1)S(1)} %get-tuple-element.7), channel_id=1, source_target_pairs={{0,1},{1,2},{2,3},{3,4},{4,5},{5,6},{6,7},{8,9},{9,10},{10,11},{11... | collective-permute-start | bytes 245768 | tf_op jit(solution)/shard_map/ppermute | solution.py:12
  19.6 8.6 %collective-permute-start.3 = (bf16[8,1,16,320]{3,0,2,1:T(8,128)(2,1)S(1)}, bf16[8,1,16,320]{3,0,2,1:T(8,128)(2,1)S(1)}, u32[]{:S(2)}, u32[]{:S(2)}) collective-permute-start(bf16[8,1,16,320]{3,0,2,1:T(8,128)(2,1)S(1)} %get-tuple-element.8), channel_id=1, source_target_pairs={{1,0},{2,1},{3,2},{4,3},{5,4},{6,5},{7,6},{9,8},{10,9},{11,10},{12... | collective-permute-start | bytes 245768 | tf_op jit(solution)/shard_map/ppermute | solution.py:15
  32.9 1.9 copy-start.3
  32.9 2.5 %copy-start.12 = (f32[320]{0:T(512)S(1)}, f32[320]{0:T(512)}, u32[]{:S(2)}) copy-start(f32[320]{0:T(512)} %param.19) | copy-start | bytes 3844
  34.8 0.9 copy-start.9
  35.8 2.5 %copy-start.10 = (bf16[320,320]{1,0:T(8,128)(2,1)S(1)}, bf16[320,320]{1,0:T(8,128)(2,1)}, u32[]{:S(2)}) copy-start(bf16[320,320]{1,0:T(8,128)(2,1)} %param.22) | copy-start | bytes 614404
  36.5 0.9 copy-start.4
  38.3 10.8 %copy-start.14 = (f32[8,33]{1,0:T(8,128)S(1)}, f32[8,33]{1,0:T(8,128)}, u32[]{:S(2)}) copy-start(f32[8,33]{1,0:T(8,128)} %param.24) | copy-start | bytes 3172
  38.3 11.3 %copy-start.15 = (s32[256]{0:T(256)S(1)}, s32[256]{0:T(256)}, u32[]{:S(2)}) copy-start(s32[256]{0:T(256)} %param.25) | copy-start | bytes 3076
  38.3 14.8 %copy-start.11 = (bf16[320,320]{1,0:T(8,128)(2,1)S(1)}, bf16[320,320]{1,0:T(8,128)(2,1)}, u32[]{:S(2)}) copy-start(bf16[320,320]{1,0:T(8,128)(2,1)} %param.20) | copy-start | bytes 614404
  39.0 0.8 copy-start.6
  40.8 74.4 %collective-permute-start.4 = (bf16[2,8,128,320]{2,3,1,0:T(8,128)(2,1)}, bf16[2,8,128,320]{2,3,1,0:T(8,128)(2,1)}, u32[]{:S(2)}, u32[]{:S(2)}) collective-permute-start(bf16[2,8,128,320]{2,3,1,0:T(8,128)(2,1)} %copy_dynamic-update-slice_fusion.1), channel_id=1, source_target_pairs={{240,0},{248,8},{0,16},{8,24},{16,32},{24,40},{32,48},{40,56},{48,... | collective-permute-start | bytes 3932168 | tf_op jit(solution)/shard_map/ppermute | solution.py:23
  43.5 73.1 %collective-permute-start.5 = (bf16[2,8,128,320]{2,3,1,0:T(8,128)(2,1)}, bf16[2,8,128,320]{2,3,1,0:T(8,128)(2,1)}, u32[]{:S(2)}, u32[]{:S(2)}) collective-permute-start(bf16[2,8,128,320]{2,3,1,0:T(8,128)(2,1)} %copy_dynamic-update-slice_fusion.1), channel_id=1, source_target_pairs={{248,0},{0,8},{8,16},{16,24},{24,32},{32,40},{40,48},{48,56},{56,6... | collective-permute-start | bytes 3932168 | tf_op jit(solution)/shard_map/ppermute | solution.py:23
  43.7 74.8 %collective-permute-start.6 = (bf16[2,8,128,320]{2,3,1,0:T(8,128)(2,1)}, bf16[2,8,128,320]{2,3,1,0:T(8,128)(2,1)}, u32[]{:S(2)}, u32[]{:S(2)}) collective-permute-start(bf16[2,8,128,320]{2,3,1,0:T(8,128)(2,1)} %copy_dynamic-update-slice_fusion.1), channel_id=1, source_target_pairs={{8,0},{16,8},{24,16},{32,24},{40,32},{48,40},{56,48},{64,56},{72,6... | collective-permute-start | bytes 3932168 | tf_op jit(solution)/shard_map/ppermute | solution.py:23
  49.7 81.9 %collective-permute-start.7 = (bf16[2,8,128,320]{2,3,1,0:T(8,128)(2,1)}, bf16[2,8,128,320]{2,3,1,0:T(8,128)(2,1)}, u32[]{:S(2)}, u32[]{:S(2)}) collective-permute-start(bf16[2,8,128,320]{2,3,1,0:T(8,128)(2,1)} %copy_dynamic-update-slice_fusion.1), channel_id=1, source_target_pairs={{16,0},{24,8},{32,16},{40,24},{48,32},{56,40},{64,48},{72,56},{80,... | collective-permute-start | bytes 3932168 | tf_op jit(solution)/shard_map/ppermute | solution.py:23
  58.5 59.7 %copy-start.5 = (bf16[40,8,8,128]{3,2,1,0:T(8,128)(2,1)S(1)}, bf16[40,8,8,128]{3,2,1,0:T(8,128)(2,1)}, u32[]{:S(2)}) copy-start(bf16[40,8,8,128]{3,2,1,0:T(8,128)(2,1)} %copy-done.4) | copy-start | bytes 1966084
  116.6 1.7 copy-start.7
  151.5 15.6 %copy-start.2 = (bf16[8,128,8,40]{3,0,2,1:T(8,128)(2,1)S(1)}, bf16[8,128,8,40]{3,0,2,1:T(8,128)(2,1)}, u32[]{:S(2)}) copy-start(bf16[8,128,8,40]{3,0,2,1:T(8,128)(2,1)} %copy.54) | copy-start | bytes 1966084
  188.9 5.9 %copy-start.1 = (bf16[3,3,320,320]{3,2,1,0:T(8,128)(2,1)S(1)}, bf16[3,3,320,320]{3,2,1,0:T(8,128)(2,1)}, u32[]{:S(2)}) copy-start(bf16[3,3,320,320]{3,2,1,0:T(8,128)(2,1)} %param.16) | copy-start | bytes 5529604
where the time goes:
time: 195 us
  waiting for transfers between devices  77.3 us (40%)
  local copies, waits for them, and re-layouts  57.4 us (29%)
  matrix products  32.4 us (17%)
  starting transfers between devices  23.2 us (12%)
  other arithmetic  3.37 us (2%)
    ppermute x4, waiting for transfers between devices, passed_along(): return lax.ppermute(block, axis, route)  68.2 us
    another operation x1, local copies, waits for them, and re-layouts, attend(): v4 = value.reshape(fk, pix, heads, dh)  15.6 us
    another operation x1, local copies, waits for them, and re-layouts, attend(): k4 = key.reshape(fk, pix, heads, dh)  15.4 us
    ppermute x4, starting transfers between devices, passed_along(): return lax.ppermute(block, axis, route)  11.5 us
    sub x1, matrix products, attend(): expo = jnp.exp(scores - top)  10.6 us
    ppermute x2, waiting for transfers between devices, with_halo(): lax.ppermute(lax.slice_in_dim(block, 0, width, axis=dim), axis, backward)  8.46 us
    dot_general x1, matrix products, attend(): jnp.einsum('phij,jphd->iphd', weights, v4, preferred_element_type=jnp.flo...  8.17 us
    conv_general_dilated x2, matrix products, conv_pass(): lax.conv_general_dilated(rimmed, weight, (1, 1), ((0, 0), (1, 1)), dimens...  7.97 us
  transfers between devices with their start and end apart: 8, of which 5 were waited for; matrix products, arithmetic and copies ran while one was open for 6% of the time, Pallas kernels for 0%

commit v1 on v0

v1 whole, which is shorter than its diff:
```python
import functools
import math

import jax
import jax.numpy as jnp
import numpy as np
from jax import lax
from jax.experimental import pallas as pl
from jax.experimental.pallas import tpu as pltpu
from jax.sharding import PartitionSpec as P

BF = jnp.bfloat16
F32 = jnp.float32
GROUP = 4
VMEM_BYTES = 52 * 1024 * 1024


def tapped(dst, row, tap, value):
    dst[row, :, tap * 256 : tap * 256 + 256] = value[:, :256]
    dst[row, :, 768 + tap * 64 : 832 + tap * 64] = value[:, 256:]


def arrange(dst, weight):
    for dy in range(3):
        for dx in range(3):
            w = weight[dy, dx]
            top = slice(dy * 256, dy * 256 + 256)
            low = slice(768 + dy * 64, 832 + dy * 64)
            left = slice(dx * 256, dx * 256 + 256)
            right = slice(768 + dx * 64, 832 + dx * 64)
            dst[top, left] = w[:256, :256]
            dst[top, right] = w[:256, 256:]
            dst[low, left] = w[256:, :256]
            dst[low, right] = w[256:, 256:]


def combine(prod, rows):
    def shifted(a, b, c):
        gap = jnp.zeros((8, a.shape[1]), F32)
        return (
            b
            + jnp.concatenate([gap, a[:-8]], axis=0)
            + jnp.concatenate([c[8:], gap], axis=0)
        )

    main = shifted(prod[rows, 0:256], prod[rows, 256:512], prod[rows, 512:768])
    rest = shifted(prod[rows, 768:832], prod[rows, 832:896], prod[rows, 896:960])
    return jnp.concatenate([main, rest], axis=1)


def conv_kernel(
    meta, frames, control, low, high, first, second, table, gain,
    out0, out1, out2, out3, flat,
    merged, taps1, taps2, wide1, wide2, prod, normed,
):
    me = meta[0]

    def put(row, f, value):
        value = value.astype(BF).astype(F32)
        rest = jnp.concatenate([value[:, 256:], jnp.zeros((16, 64), F32)], axis=1)
        for j, part in enumerate((value[:, :128], value[:, 128:256], rest)):
            merged[j, row, pl.ds(f, 16, stride=8), :] = part

    def taken(row):
        return jnp.concatenate([merged[0, row], merged[1, row], merged[2, row, :, :64]], axis=1)

    for f in range(8):
        for y in range(8):
            put(y + 2, f, frames[f, y].astype(F32) + control[f, y].astype(F32))
        for y in range(2):
            put(y, f, low[f, y].astype(F32))
            put(y + 10, f, high[f, y].astype(F32))
    for m in range(12):
        value = taken(m).astype(BF)
        for dy in range(3):
            if 0 <= m - dy < 10:
                tapped(taps1, m - dy, dy, value)
    arrange(wide1, first)
    arrange(wide2, second)
    embed = table[pl.ds(meta[3], 1), :]
    for part in range(2):
        prod[...] = jnp.dot(
            taps1[part * 5 : part * 5 + 5].reshape(640, 960), wide1[...],
            preferred_element_type=F32,
        )
        for i in range(5):
            row = part * 5 + i
            t = combine(prod, slice(i * 128, i * 128 + 128)) + embed
            act = t * (0.5 * jnp.tanh(0.5 * t) + 0.5)
            if row == 0:
                act = jnp.where(meta[1] == 1, 0.0, act)
            if row == 9:
                act = jnp.where(meta[2] == 1, 0.0, act)
            act = act.astype(BF)
            for dy in range(3):
                if 0 <= row - dy < 8:
                    tapped(taps2, row - dy, dy, act)
    for part in range(2):
        prod[0:512, :] = jnp.dot(
            taps2[part * 4 : part * 4 + 4].reshape(512, 960), wide2[...],
            preferred_element_type=F32,
        )
        for i in range(4):
            y = part * 4 + i
            block = combine(prod, slice(i * 128, i * 128 + 128)) + taken(y + 2)
            flat[y] = block
            mean = jnp.sum(block, axis=1, keepdims=True) * (1.0 / 320)
            centre = block - mean
            var = jnp.sum(centre * centre, axis=1, keepdims=True) * (1.0 / 320)
            normed[y] = (centre * lax.rsqrt(var + 1e-5) * gain[...]).astype(BF)
    for k, out in enumerate((out0, out1, out2, out3)):
        out[...] = normed[pl.ds(2 * (me ^ k), 2)].reshape(256, 320)


def attend_kernel(
    meta, own0, own1, own2, own3, halo0, halo1, halo2, halo3, wq, wk, wv, bias,
    out0, out1, out2, out3,
    field, wide, query, key, value, back,
):
    me = meta[0]
    for at, w in enumerate((wq, wk, wv)):
        wide[:, at * 256 : at * 256 + 256] = w[:, :256]
        wide[:, 768 + at * 64 : 832 + at * 64] = w[:, 256:]
    for k, own in enumerate((own0, own1, own2, own3)):
        at = pl.multiple_of(16 + 8 * (me ^ k), 8)
        field[:, pl.ds(at, 8), :] = own[...].astype(F32).reshape(32, 8, 320)
    for k, halo in enumerate((halo0, halo1, halo2, halo3)):
        block = me ^ k
        at = pl.multiple_of(jnp.where(block >= 2, 8 * block - 16, 48 + 8 * block), 8)
        field[:, pl.ds(at, 8), :] = halo[...].astype(F32).reshape(32, 8, 320)

    def project(lo, hi, with_query):
        n = hi - lo
        x = field[:, lo:hi, :].reshape(32 * n, 320).astype(BF)
        out = jnp.dot(x, wide[...], preferred_element_type=F32).astype(BF)
        if with_query:
            query[:, :, 0:256] = out[:, 0:256].reshape(32, n, 256)
            query[:, :, 256:320] = out[:, 768:832].reshape(32, n, 64)
        key[:, lo:hi, 0:256] = out[:, 256:512].reshape(32, n, 256)
        key[:, lo:hi, 256:320] = out[:, 832:896].reshape(32, n, 64)
        value[:, lo:hi, 0:256] = out[:, 512:768].reshape(32, n, 256)
        value[:, lo:hi, 256:320] = out[:, 896:960].reshape(32, n, 64)

    project(16, 48, True)
    project(0, 16, False)
    project(48, 64, False)

    lane = lax.broadcasted_iota(jnp.int32, (1, 1, 256), 2)
    head = lax.broadcasted_iota(jnp.int32, (6, 1, 1), 0)
    mask6 = (lane >= head * 40) & (lane < head * 40 + 40)
    lane = lax.broadcasted_iota(jnp.int32, (1, 1, 192), 2)
    head = lax.broadcasted_iota(jnp.int32, (2, 1, 1), 0)
    mask2 = (lane >= 112 + head * 40) & (lane < 152 + head * 40)
    ones6 = mask6.astype(F32)
    ones2 = mask2.astype(F32)
    spread6 = ones6.astype(BF)
    spread2 = ones2.astype(BF)
    scale = 40.0 ** -0.5 / math.log(2.0)
    across = (((1,), (1,)), ((), ()))

    def pixel(p):
        q = query[p]
        k = key[p]
        v = value[p]
        q6 = (q[None, :, 0:256] * spread6).reshape(192, 256)
        q2 = (q[None, :, 128:320] * spread2).reshape(64, 192)
        s = jnp.concatenate(
            [
                lax.dot_general(q6, k[:, 0:256], across, preferred_element_type=F32),
                lax.dot_general(q2, k[:, 128:320], across, preferred_element_type=F32),
            ],
            axis=0,
        )
        s = s * scale + bias[...]
        e = jnp.exp2(s - jnp.max(s, axis=1, keepdims=True))
        w = (e / jnp.sum(e, axis=1, keepdims=True)).astype(BF)
        o6 = jnp.dot(w[:192], v[:, 0:256], preferred_element_type=F32)
        o2 = jnp.dot(w[192:], v[:, 128:320], preferred_element_type=F32)
        a6 = jnp.sum(o6.reshape(6, 32, 256) * ones6, axis=0)
        a2 = jnp.sum(o2.reshape(2, 32, 192) * ones2, axis=0)
        att = jnp.concatenate(
            [a6[:, 0:128], a6[:, 128:256] + a2[:, 0:128], a2[:, 128:192]], axis=1
        )
        for b in range(4):
            back[b, p] = att[8 * b : 8 * b + 8]

    def some(i, carry):
        for j in range(4):
            pixel(i * 4 + j)
        return carry

    lax.fori_loop(0, 8, some, 0)
    for k, out in enumerate((out0, out1, out2, out3)):
        out[...] = back[me ^ k].reshape(256, 320).astype(BF)


def final_kernel(meta, a0, a1, a2, a3, w_out, flat, out, total):
    k = pl.program_id(0)
    for at, a in enumerate((a0, a1, a2, a3)):

        @pl.when(k == at)
        def _():
            mixed = jnp.dot(a[...], w_out[...], preferred_element_type=F32)
            mixed = flat[...].reshape(256, 320) + mixed
            total[0] = mixed[:, :128]
            total[1] = mixed[:, 128:256]
            total[2, :, :64] = mixed[:, 256:]

    for f in range(8):
        for y in range(2):
            for j, width in enumerate((128, 128, 64)):
                part = total[j, pl.ds(y * 128 + f, 16, stride=8), :]
                out[f, y, :, j * 128 : j * 128 + width] = part[:, :width]


def shards(
    frames, control, conv_first, conv_second, time_table, step_index, norm_gain,
    w_query, w_key, w_value, w_out, rel_bias, reach,
):
    count = lax.axis_size("frame")
    bands = lax.axis_size("band")
    planes = count // GROUP
    place = lax.axis_index("frame")
    band = lax.axis_index("band")
    me = place % GROUP
    step = step_index[0]
    meta = jnp.stack(
        [me, (band == 0).astype(jnp.int32), (band == bands - 1).astype(jnp.int32), step % 8, step // 8]
    ).astype(jnp.int32)

    up = [(i, i + 1) for i in range(bands - 1)]
    down = [(i + 1, i) for i in range(bands - 1)]

    def edge(rows):
        return (frames[:, rows].astype(F32) + control[:, rows].astype(F32)).astype(BF)

    low = lax.ppermute(edge(slice(6, 8)), "band", up)
    high = lax.ppermute(edge(slice(0, 2)), "band", down)

    delta = np.arange(64)[None, :] - 16 - np.arange(32)[:, None]
    picks = (delta[:, :, None] + 16 == np.arange(33)[None, None, :]).astype(np.float32)
    bias = jnp.einsum("hs,ijs->hij", rel_bias, picks, precision=lax.Precision.HIGHEST)
    reach_q = lax.dynamic_slice_in_dim(reach, (place // GROUP) * 32, 32)
    allowed = np.abs(delta) <= reach_q[:, None]
    bias = jnp.where(allowed[None], bias * (1.0 / math.log(2.0)), -jnp.inf).reshape(256, 64)

    whole = pl.BlockSpec(memory_space=pltpu.VMEM)
    smem = pl.BlockSpec(memory_space=pltpu.SMEM)
    params = pltpu.CompilerParams(vmem_limit_bytes=VMEM_BYTES)
    piece = jax.ShapeDtypeStruct((256, 320), BF)

    def at(shape):
        return pl.BlockSpec(shape, lambda i, m: (0,) * len(shape))

    n0, n1, n2, n3, flat = pl.pallas_call(
        conv_kernel,
        grid_spec=pltpu.PrefetchScalarGridSpec(
            num_scalar_prefetch=1,
            grid=(1,),
            in_specs=[
                at((8, 8, 16, 320)), at((8, 8, 16, 320)), at((8, 2, 16, 320)), at((8, 2, 16, 320)),
                at((3, 3, 320, 320)), at((3, 3, 320, 320)),
                pl.BlockSpec((8, 320), lambda i, m: (m[4], 0)),
                at((1, 320)),
            ],
            out_specs=[at((256, 320))] * 4 + [at((8, 128, 320))],
            scratch_shapes=[
                pltpu.VMEM((3, 12, 128, 128), F32),
                pltpu.VMEM((10, 128, 960), BF),
                pltpu.VMEM((8, 128, 960), BF),
                pltpu.VMEM((960, 960), BF),
                pltpu.VMEM((960, 960), BF),
                pltpu.VMEM((640, 960), F32),
                pltpu.VMEM((8, 128, 320), BF),
            ],
        ),
        out_shape=[piece] * 4 + [jax.ShapeDtypeStruct((8, 128, 320), F32)],
        compiler_params=params,
        name="conv_block",
    )(meta, frames, control, low, high, conv_first, conv_second, time_table, norm_gain[None])

    pieces = (n0, n1, n2, n3)

    def plane(i, k):
        return (i & ~3) | ((i & 3) ^ k)

    def exchange(x, k):
        return lax.ppermute(x, "frame", [(i, plane(i, k)) for i in range(count)])

    def beside(i, k):
        turn = 1 if i & 2 else -1
        return (((i >> 2) + turn) % planes) * GROUP + ((i & 3) ^ k)

    own = [n0] + [exchange(pieces[k], k) for k in (1, 2, 3)]
    halo = [
        lax.ppermute(pieces[k], "frame", [(i, beside(i, k)) for i in range(count)])
        for k in (0, 1)
    ]
    for k in (2, 3):
        route = [
            (i, (((i >> 2) + (1 if (i ^ k) & 2 else -1)) % planes) * GROUP + (i & 3))
            for i in range(count)
        ]
        halo.append(lax.ppermute(own[k], "frame", route))

    outs = pl.pallas_call(
        attend_kernel,
        in_specs=[smem] + [whole] * 12,
        out_specs=[whole] * 4,
        out_shape=[piece] * 4,
        scratch_shapes=[
            pltpu.VMEM((32, 64, 320), F32),
            pltpu.VMEM((320, 960), BF),
            pltpu.VMEM((32, 32, 320), BF),
            pltpu.VMEM((32, 64, 320), BF),
            pltpu.VMEM((32, 64, 320), BF),
            pltpu.VMEM((4, 32, 8, 320), F32),
        ],
        compiler_params=params,
        name="attend",
    )(meta, *own, *halo, w_query, w_key, w_value, bias)

    back = [outs[0]] + [exchange(outs[k], k) for k in (1, 2, 3)]

    return pl.pallas_call(
        final_kernel,
        grid_spec=pltpu.PrefetchScalarGridSpec(
            num_scalar_prefetch=1,
            grid=(4,),
            in_specs=[at((256, 320))] * 4
            + [at((320, 320)), pl.BlockSpec((2, 128, 320), lambda i, m: (m[0] ^ i, 0, 0))],
            out_specs=pl.BlockSpec((8, 2, 16, 320), lambda i, m: (0, m[0] ^ i, 0, 0)),
            scratch_shapes=[pltpu.VMEM((3, 256, 128), F32)],
        ),
        out_shape=jax.ShapeDtypeStruct((8, 8, 16, 320), F32),
        compiler_params=params,
        name="project_out",
    )(meta, *back, w_out, flat)


def solution(mesh):
    tiled = P("frame", "band", None, None)
    return jax.shard_map(
        shards, mesh=mesh, in_specs=(tiled, tiled) + (P(),) * 11, out_specs=tiled, check_vma=False
    )
```

time: 195 us -> 82.3 us (0.42)
  the two profiles are of different devices: /device:TPU:24 before, /device:TPU:1 now
where the time goes in v1:
time: 82.3 us; the launch traced here: 80.8 us
  Pallas kernels  31.2 us (38%)
  starting transfers between devices  23.7 us (29%)
  waiting for transfers between devices  19.4 us (24%)
  local copies, waits for them, and re-layouts  3.83 us (5%)
  other arithmetic  1.4 us (2%)
    pallas_call x1, Pallas kernels, shards(): pl.pallas_call(attend_kernel, in_specs=[smem] + [whole] * 12, out_specs=[...  15.9 us
    pallas_call x1, Pallas kernels, shards(): pl.pallas_call(conv_kernel, grid_spec=pltpu.PrefetchScalarGridSpec(num_sc...  10.6 us
    ppermute x6, starting transfers between devices, exchange(): return lax.ppermute(x, 'frame', [(i, plane(i, k)) for i in range(count)])  9.3 us
    ppermute x6, waiting for transfers between devices, exchange(): return lax.ppermute(x, 'frame', [(i, plane(i, k)) for i in range(count)])  8.17 us
    ppermute x2, starting transfers between devices, shards(): lax.ppermute(pieces[k], 'frame', [(i, beside(i, k)) for i in range(count)])  6.7 us
    ppermute x2, waiting for transfers between devices, shards(): lax.ppermute(pieces[k], 'frame', [(i, beside(i, k)) for i in range(count)])  5.12 us
    pallas_call x1, Pallas kernels, shards(): pl.pallas_call(final_kernel, grid_spec=pltpu.PrefetchScalarGridSpec(num_s...  4.75 us
    ppermute x1, starting transfers between devices, shards(): low = lax.ppermute(edge(slice(6, 8)), 'band', up)  4.17 us
  transfers between devices with their start and end apart: 12, of which 5 were waited for; matrix products, arithmetic and copies ran while one was open for 5% of the time, Pallas kernels for 0%

profile of v1, /device:TPU:1, one launch (start us, length us, event | category | flops | bytes accessed | tf_op | source)
XLA Modules:
  0.0 80.8 jit_solution(12157026455570143920)
XLA Ops:
  0.0 0.0 copy-start
  0.0 1.3 %add_convert_fusion = (bf16[8,2,16,320]{3,2,1,0:T(8,128)(2,1)S(1)}, bf16[8,2,16,320]{3,2,1,0:T(8,128)(2,1)S(1)}) fusion(bf16[8,8,16,320]{3,2,1,0:T(8,128)(2,1)} %control.1, bf16[8,8,16,320]{3,2,1,0:T(8,128)(2,1)} %frames.1), kind=kLoop, calls=%fused_computation.3 | loop fusion | flops 655360 | bytes 983040 | tf_op jit(solution)/shard_map/convert_element_type | solution.py:235
  1.3 0.0 copy-start.8
  1.3 0.0 copy-start.9
  1.4 0.0 copy-start.1
  1.4 4.2 %collective-permute-start = (bf16[8,2,16,320]{3,2,1,0:T(8,128)(2,1)S(1)}, bf16[8,2,16,320]{3,2,1,0:T(8,128)(2,1)S(1)}, u32[]{:S(2)}, u32[]{:S(2)}) collective-permute-start(bf16[8,2,16,320]{3,2,1,0:T(8,128)(2,1)S(1)} %get-tuple-element.24), channel_id=1, source_target_pairs={{0,1},{1,2},{2,3},{3,4},{4,5},{5,6},{6,7},{8,9},{9,10},{10,11},{11... | collective-permute-start | bytes 491528 | tf_op jit(solution)/shard_map/ppermute | solution.py:237
  5.6 1.3 %collective-permute-start.1 = (bf16[8,2,16,320]{3,2,1,0:T(8,128)(2,1)S(1)}, bf16[8,2,16,320]{3,2,1,0:T(8,128)(2,1)S(1)}, u32[]{:S(2)}, u32[]{:S(2)}) collective-permute-start(bf16[8,2,16,320]{3,2,1,0:T(8,128)(2,1)S(1)} %get-tuple-element.23), channel_id=1, source_target_pairs={{1,0},{2,1},{3,2},{4,3},{5,4},{6,5},{7,6},{9,8},{10,9},{11,10},{12... | collective-permute-start | bytes 491528 | tf_op jit(solution)/shard_map/ppermute | solution.py:238
  7.5 2.9 %copy.16.table = f32[1000,320]{1,0:T(8,128)} copy(f32[1000,320]{0,1:T(8,128)} %param.19) | data formatting | bytes 2560000 | tf_op args[4]
  10.5 0.0 copy-done.8
  10.5 0.0 copy-done.9
  10.5 0.1 dynamic_slice.3
  10.5 0.1 stack.31.meta
  10.6 0.0 copy-start.7
  10.6 0.0 copy-start.3
  10.6 0.0 collective-permute-done.low
  10.6 2.3 %collective-permute-done.1.high = bf16[8,2,16,320]{3,2,1,0:T(8,128)(2,1)S(1)} collective-permute-done((bf16[8,2,16,320]{3,2,1,0:T(8,128)(2,1)S(1)}, bf16[8,2,16,320]{3,2,1,0:T(8,128)(2,1)S(1)}, u32[]{:S(2)}, u32[]{:S(2)}) %collective-permute-start.1) | collective-permute-done | bytes 163872 | tf_op jit(solution)/shard_map/ppermute | solution.py:238
  12.9 0.0 copy-done.1
  12.9 10.6 %conv_block.1 = (bf16[256,320]{1,0:T(8,128)(2,1)S(1)}, bf16[256,320]{1,0:T(8,128)(2,1)S(1)}, bf16[256,320]{1,0:T(8,128)(2,1)S(1)}, bf16[256,320]{1,0:T(8,128)(2,1)S(1)}, f32[8,128,320]{2,1,0:T(8,128)}) custom-call(s32[5]{0:T(128)S(1)} %stack.31.meta, bf16[8,8,16,320]{3,2,1,0:T(8,128)(2,1)S(1)} %copy-done.1, bf16[8,8,16,320]{3,2,1,0:T(8,128)(2,1)} %control.1, ...), custom_call_target="tpu_custom_call" | custom-call | tf_op jit(solution)/shard_map/conv_block/pallas_call | solution.py:255
  23.5 2.7 %collective-permute-start.3 = (bf16[256,320]{1,0:T(8,128)(2,1)S(1)}, bf16[256,320]{1,0:T(8,128)(2,1)S(1)}, u32[]{:S(2)}, u32[]{:S(2)}) collective-permute-start(bf16[256,320]{1,0:T(8,128)(2,1)S(1)} %get-tuple-element.16), channel_id=1, source_target_pairs={{0,16},{8,24},{16,0},{24,8},{32,48},{40,56},{48,32},{56,40},{64,80... | collective-permute-start | bytes 491528 | tf_op jit(solution)/shard_map/ppermute | solution.py:288
  26.2 2.3 %collective-permute-start.4 = (bf16[256,320]{1,0:T(8,128)(2,1)S(1)}, bf16[256,320]{1,0:T(8,128)(2,1)S(1)}, u32[]{:S(2)}, u32[]{:S(2)}) collective-permute-start(bf16[256,320]{1,0:T(8,128)(2,1)S(1)} %get-tuple-element.17), channel_id=1, source_target_pairs={{0,24},{8,16},{16,8},{24,0},{32,56},{40,48},{48,40},{56,32},{64,88... | collective-permute-start | bytes 491528 | tf_op jit(solution)/shard_map/ppermute | solution.py:288
  28.5 0.0 copy-done.7
  28.5 0.1 broadcast_compare_fusion
  28.6 0.0 collective-permute-start.2
  28.6 6.0 %collective-permute-start.6 = (bf16[256,320]{1,0:T(8,128)(2,1)S(1)}, bf16[256,320]{1,0:T(8,128)(2,1)S(1)}, u32[]{:S(2)}, u32[]{:S(2)}) collective-permute-start(bf16[256,320]{1,0:T(8,128)(2,1)S(1)} %get-tuple-element.15), channel_id=1, source_target_pairs={{0,232},{8,224},{16,56},{24,48},{32,8},{40,0},{48,88},{56,80},{64,... | collective-permute-start | bytes 491528 | tf_op jit(solution)/shard_map/ppermute | solution.py:296
  34.6 0.0 copy-start.2
  34.6 0.7 collective-permute-start.5
  35.3 0.0 collective-permute-done.3.own2
  35.3 0.7 collective-permute-start.7
  36.0 0.0 collective-permute-done.4.own3
  36.0 1.5 %collective-permute-start.8 = (bf16[256,320]{1,0:T(8,128)(2,1)S(1)}, bf16[256,320]{1,0:T(8,128)(2,1)S(1)}, u32[]{:S(2)}, u32[]{:S(2)}) collective-permute-start(bf16[256,320]{1,0:T(8,128)(2,1)S(1)} %collective-permute-done.4.own3), channel_id=1, source_target_pairs={{0,32},{8,40},{16,240},{24,248},{32,64},{40,72},{48,16},{56,24},{6... | collective-permute-start | bytes 491528 | tf_op jit(solution)/shard_map/ppermute | solution.py:304
  37.6 0.0 copy-done
  37.6 0.0 copy-done.3
  37.6 0.5 fusion.1
  38.1 0.0 collective-permute-done.2.own1
  38.1 5.1 %collective-permute-done.5.halo0 = bf16[256,320]{1,0:T(8,128)(2,1)S(1)} collective-permute-done((bf16[256,320]{1,0:T(8,128)(2,1)S(1)}, bf16[256,320]{1,0:T(8,128)(2,1)S(1)}, u32[]{:S(2)}, u32[]{:S(2)}) %collective-permute-start.5) | collective-permute-done | bytes 163872 | tf_op jit(solution)/shard_map/ppermute | solution.py:296
  43.2 0.0 collective-permute-done.6.halo1
  43.2 0.0 copy-start.4
  43.2 0.0 collective-permute-done.7.halo2
  43.2 0.0 copy-start.5
  43.2 3.8 %collective-permute-done.8.halo3 = bf16[256,320]{1,0:T(8,128)(2,1)S(1)} collective-permute-done((bf16[256,320]{1,0:T(8,128)(2,1)S(1)}, bf16[256,320]{1,0:T(8,128)(2,1)S(1)}, u32[]{:S(2)}, u32[]{:S(2)}) %collective-permute-start.8) | collective-permute-done | bytes 163872 | tf_op jit(solution)/shard_map/ppermute | solution.py:304
  47.0 0.0 copy-start.6
  47.0 0.0 copy-done.4
  47.0 0.0 copy-done.5
  47.0 0.7 copy-done.6
  47.7 15.9 %attend.1 = (bf16[256,320]{1,0:T(8,128)(2,1)S(1)}, bf16[256,320]{1,0:T(8,128)(2,1)S(1)}, bf16[256,320]{1,0:T(8,128)(2,1)S(1)}, bf16[256,320]{1,0:T(8,128)(2,1)S(1)}) custom-call(s32[5]{0:T(128)S(1)} %stack.31.meta, bf16[256,320]{1,0:T(8,128)(2,1)S(1)} %get-tuple-element.14.own0, bf16[256,320]{1,0:T(8,128)(2,1)S(1)} %collective-permute-done.2.own1, ...), custom_call_target="tpu_custom_call" | custom-call | tf_op jit(solution)/shard_map/attend/pallas_call | solution.py:306
  63.6 2.1 %collective-permute-start.10 = (bf16[256,320]{1,0:T(8,128)(2,1)S(1)}, bf16[256,320]{1,0:T(8,128)(2,1)S(1)}, u32[]{:S(2)}, u32[]{:S(2)}) collective-permute-start(bf16[256,320]{1,0:T(8,128)(2,1)S(1)} %get-tuple-element.20), channel_id=1, source_target_pairs={{0,16},{8,24},{16,0},{24,8},{32,48},{40,56},{48,32},{56,40},{64,80... | collective-permute-start | bytes 491528 | tf_op jit(solution)/shard_map/ppermute | solution.py:288
  65.7 2.2 %collective-permute-start.11 = (bf16[256,320]{1,0:T(8,128)(2,1)S(1)}, bf16[256,320]{1,0:T(8,128)(2,1)S(1)}, u32[]{:S(2)}, u32[]{:S(2)}) collective-permute-start(bf16[256,320]{1,0:T(8,128)(2,1)S(1)} %get-tuple-element.21), channel_id=1, source_target_pairs={{0,24},{8,16},{16,8},{24,0},{32,56},{40,48},{48,40},{56,32},{64,88... | collective-permute-start | bytes 491528 | tf_op jit(solution)/shard_map/ppermute | solution.py:288
  67.9 0.0 collective-permute-start.9
  67.9 2.7 %collective-permute-done.10.a2 = bf16[256,320]{1,0:T(8,128)(2,1)S(1)} collective-permute-done((bf16[256,320]{1,0:T(8,128)(2,1)S(1)}, bf16[256,320]{1,0:T(8,128)(2,1)S(1)}, u32[]{:S(2)}, u32[]{:S(2)}) %collective-permute-start.10) | collective-permute-done | bytes 163872 | tf_op jit(solution)/shard_map/ppermute | solution.py:288
  70.6 5.5 %collective-permute-done.11.a3 = bf16[256,320]{1,0:T(8,128)(2,1)S(1)} collective-permute-done((bf16[256,320]{1,0:T(8,128)(2,1)S(1)}, bf16[256,320]{1,0:T(8,128)(2,1)S(1)}, u32[]{:S(2)}, u32[]{:S(2)}) %collective-permute-start.11) | collective-permute-done | bytes 163872 | tf_op jit(solution)/shard_map/ppermute | solution.py:288
  76.1 0.0 collective-permute-done.9.a1
  76.1 0.0 copy-done.2
  76.1 4.7 %project_out.1 = f32[8,8,16,320]{3,2,1,0:T(8,128)} custom-call(s32[5]{0:T(128)S(1)} %stack.31.meta, bf16[256,320]{1,0:T(8,128)(2,1)S(1)} %get-tuple-element.18.a0, bf16[256,320]{1,0:T(8,128)(2,1)S(1)} %collective-permute-done.9.a1, bf16[256,320]{1,0:T(8,128)(2,1)S(1)} %collective-permute-done.10.a2, bf16[256,320]{1,0:T(8,128)(2,1)S(1)} %collective-permute-done.11.a3, ...), custom_call_target="tpu_custom_call" | custom-call | tf_op jit(solution)/shard_map/project_out/pallas_call | solution.py:325
  (2 shorter events, 0.0 us)
Async XLA Ops:
  0.0 37.6 %copy-start = (f32[8,33]{1,0:T(8,128)S(1)}, f32[8,33]{1,0:T(8,128)}, u32[]{:S(2)}) copy-start(f32[8,33]{1,0:T(8,128)} %param.26) | copy-start | bytes 3172
  1.3 9.1 %copy-start.8 = (f32[320]{0:T(512)S(1)}, f32[320]{0:T(512)}, u32[]{:S(2)}) copy-start(f32[320]{0:T(512)} %param.21) | copy-start | bytes 3844
  1.3 9.1 %copy-start.9 = (s32[256]{0:T(256)S(1)}, s32[256]{0:T(256)}, u32[]{:S(2)}) copy-start(s32[256]{0:T(256)} %param.27) | copy-start | bytes 3076
  1.4 11.5 %copy-start.1 = (bf16[8,8,16,320]{3,2,1,0:T(8,128)(2,1)S(1)}, bf16[8,8,16,320]{3,2,1,0:T(8,128)(2,1)}, u32[]{:S(2)}) copy-start(bf16[8,8,16,320]{3,2,1,0:T(8,128)(2,1)} %frames.1) | copy-start | bytes 1966084
  1.4 9.3 %collective-permute-start = (bf16[8,2,16,320]{3,2,1,0:T(8,128)(2,1)S(1)}, bf16[8,2,16,320]{3,2,1,0:T(8,128)(2,1)S(1)}, u32[]{:S(2)}, u32[]{:S(2)}) collective-permute-start(bf16[8,2,16,320]{3,2,1,0:T(8,128)(2,1)S(1)} %get-tuple-element.24), channel_id=1, source_target_pairs={{0,1},{1,2},{2,3},{3,4},{4,5},{5,6},{6,7},{8,9},{9,10},{10,11},{11... | collective-permute-start | bytes 491528 | tf_op jit(solution)/shard_map/ppermute | solution.py:237
  5.6 7.3 %collective-permute-start.1 = (bf16[8,2,16,320]{3,2,1,0:T(8,128)(2,1)S(1)}, bf16[8,2,16,320]{3,2,1,0:T(8,128)(2,1)S(1)}, u32[]{:S(2)}, u32[]{:S(2)}) collective-permute-start(bf16[8,2,16,320]{3,2,1,0:T(8,128)(2,1)S(1)} %get-tuple-element.23), channel_id=1, source_target_pairs={{1,0},{2,1},{3,2},{4,3},{5,4},{6,5},{7,6},{9,8},{10,9},{11,10},{12... | collective-permute-start | bytes 491528 | tf_op jit(solution)/shard_map/ppermute | solution.py:238
  10.6 17.9 %copy-start.7 = (s32[32,64]{1,0:T(8,128)S(1)}, s32[32,64]{1,0:T(8,128)}, u32[]{:S(2)}) copy-start(s32[32,64]{1,0:T(8,128)} %constant.68.clone) | copy-start | bytes 24580
  10.6 26.9 %copy-start.3 = (f32[32,64,33]{1,2,0:T(8,128)S(1)}, f32[32,64,33]{1,2,0:T(8,128)}, u32[]{:S(2)}) copy-start(f32[32,64,33]{1,2,0:T(8,128)} %constant.67.clone) | copy-start | bytes 811012
  23.5 11.8 %collective-permute-start.3 = (bf16[256,320]{1,0:T(8,128)(2,1)S(1)}, bf16[256,320]{1,0:T(8,128)(2,1)S(1)}, u32[]{:S(2)}, u32[]{:S(2)}) collective-permute-start(bf16[256,320]{1,0:T(8,128)(2,1)S(1)} %get-tuple-element.16), channel_id=1, source_target_pairs={{0,16},{8,24},{16,0},{24,8},{32,48},{40,56},{48,32},{56,40},{64,80... | collective-permute-start | bytes 491528 | tf_op jit(solution)/shard_map/ppermute | solution.py:288
  26.2 9.8 %collective-permute-start.4 = (bf16[256,320]{1,0:T(8,128)(2,1)S(1)}, bf16[256,320]{1,0:T(8,128)(2,1)S(1)}, u32[]{:S(2)}, u32[]{:S(2)}) collective-permute-start(bf16[256,320]{1,0:T(8,128)(2,1)S(1)} %get-tuple-element.17), channel_id=1, source_target_pairs={{0,24},{8,16},{16,8},{24,0},{32,56},{40,48},{48,40},{56,32},{64,88... | collective-permute-start | bytes 491528 | tf_op jit(solution)/shard_map/ppermute | solution.py:288
  28.6 9.5 %collective-permute-start.2 = (bf16[256,320]{1,0:T(8,128)(2,1)S(1)}, bf16[256,320]{1,0:T(8,128)(2,1)S(1)}, u32[]{:S(2)}, u32[]{:S(2)}) collective-permute-start(bf16[256,320]{1,0:T(8,128)(2,1)S(1)} %get-tuple-element.15), channel_id=1, source_target_pairs={{0,8},{8,0},{16,24},{24,16},{32,40},{40,32},{48,56},{56,48},{64,72... | collective-permute-start | bytes 491528 | tf_op jit(solution)/shard_map/ppermute | solution.py:288
  28.6 14.6 %collective-permute-start.6 = (bf16[256,320]{1,0:T(8,128)(2,1)S(1)}, bf16[256,320]{1,0:T(8,128)(2,1)S(1)}, u32[]{:S(2)}, u32[]{:S(2)}) collective-permute-start(bf16[256,320]{1,0:T(8,128)(2,1)S(1)} %get-tuple-element.15), channel_id=1, source_target_pairs={{0,232},{8,224},{16,56},{24,48},{32,8},{40,0},{48,88},{56,80},{64,... | collective-permute-start | bytes 491528 | tf_op jit(solution)/shard_map/ppermute | solution.py:296
  34.6 41.5 %copy-start.2 = (bf16[320,320]{1,0:T(8,128)(2,1)S(1)}, bf16[320,320]{1,0:T(8,128)(2,1)}, u32[]{:S(2)}) copy-start(bf16[320,320]{1,0:T(8,128)(2,1)} %w_out.1) | copy-start | bytes 614404
  34.6 8.7 %collective-permute-start.5 = (bf16[256,320]{1,0:T(8,128)(2,1)S(1)}, bf16[256,320]{1,0:T(8,128)(2,1)S(1)}, u32[]{:S(2)}, u32[]{:S(2)}) collective-permute-start(bf16[256,320]{1,0:T(8,128)(2,1)S(1)} %get-tuple-element.14.own0), channel_id=1, source_target_pairs={{0,224},{8,232},{16,48},{24,56},{32,0},{40,8},{48,80},{56,88},{64,... | collective-permute-start | bytes 491528 | tf_op jit(solution)/shard_map/ppermute | solution.py:296
  35.3 7.9 %collective-permute-start.7 = (bf16[256,320]{1,0:T(8,128)(2,1)S(1)}, bf16[256,320]{1,0:T(8,128)(2,1)S(1)}, u32[]{:S(2)}, u32[]{:S(2)}) collective-permute-start(bf16[256,320]{1,0:T(8,128)(2,1)S(1)} %collective-permute-done.3.own2), channel_id=1, source_target_pairs={{0,32},{8,40},{16,240},{24,248},{32,64},{40,72},{48,16},{56,24},{6... | collective-permute-start | bytes 491528 | tf_op jit(solution)/shard_map/ppermute | solution.py:304
  36.0 11.0 %collective-permute-start.8 = (bf16[256,320]{1,0:T(8,128)(2,1)S(1)}, bf16[256,320]{1,0:T(8,128)(2,1)S(1)}, u32[]{:S(2)}, u32[]{:S(2)}) collective-permute-start(bf16[256,320]{1,0:T(8,128)(2,1)S(1)} %collective-permute-done.4.own3), channel_id=1, source_target_pairs={{0,32},{8,40},{16,240},{24,248},{32,64},{40,72},{48,16},{56,24},{6... | collective-permute-start | bytes 491528 | tf_op jit(solution)/shard_map/ppermute | solution.py:304
  43.2 3.8 %copy-start.4 = (bf16[256,320]{1,0:T(8,128)(2,1)}, bf16[256,320]{1,0:T(8,128)(2,1)S(1)}, u32[]{:S(2)}) copy-start(bf16[256,320]{1,0:T(8,128)(2,1)S(1)} %collective-permute-done.6.halo1) | copy-start | bytes 491524
  43.2 3.8 %copy-start.5 = (bf16[256,320]{1,0:T(8,128)(2,1)}, bf16[256,320]{1,0:T(8,128)(2,1)S(1)}, u32[]{:S(2)}) copy-start(bf16[256,320]{1,0:T(8,128)(2,1)S(1)} %collective-permute-done.7.halo2) | copy-start | bytes 491524
  47.0 0.7 copy-start.6
  63.6 6.9 %collective-permute-start.10 = (bf16[256,320]{1,0:T(8,128)(2,1)S(1)}, bf16[256,320]{1,0:T(8,128)(2,1)S(1)}, u32[]{:S(2)}, u32[]{:S(2)}) collective-permute-start(bf16[256,320]{1,0:T(8,128)(2,1)S(1)} %get-tuple-element.20), channel_id=1, source_target_pairs={{0,16},{8,24},{16,0},{24,8},{32,48},{40,56},{48,32},{56,40},{64,80... | collective-permute-start | bytes 491528 | tf_op jit(solution)/shard_map/ppermute | solution.py:288
  65.7 10.3 %collective-permute-start.11 = (bf16[256,320]{1,0:T(8,128)(2,1)S(1)}, bf16[256,320]{1,0:T(8,128)(2,1)S(1)}, u32[]{:S(2)}, u32[]{:S(2)}) collective-permute-start(bf16[256,320]{1,0:T(8,128)(2,1)S(1)} %get-tuple-element.21), channel_id=1, source_target_pairs={{0,24},{8,16},{16,8},{24,0},{32,56},{40,48},{48,40},{56,32},{64,88... | collective-permute-start | bytes 491528 | tf_op jit(solution)/shard_map/ppermute | solution.py:288
  67.9 8.2 %collective-permute-start.9 = (bf16[256,320]{1,0:T(8,128)(2,1)S(1)}, bf16[256,320]{1,0:T(8,128)(2,1)S(1)}, u32[]{:S(2)}, u32[]{:S(2)}) collective-permute-start(bf16[256,320]{1,0:T(8,128)(2,1)S(1)} %get-tuple-element.19), channel_id=1, source_target_pairs={{0,8},{8,0},{16,24},{24,16},{32,40},{40,32},{48,56},{56,48},{64,72... | collective-permute-start | bytes 491528 | tf_op jit(solution)/shard_map/ppermute | solution.py:288

commit v2 on v1

--- a/solution.py
+++ b/solution.py
@@ -12,7 +12,7 @@
 BF = jnp.bfloat16
 F32 = jnp.float32
 GROUP = 4
-VMEM_BYTES = 52 * 1024 * 1024
+VMEM_BYTES = 36 * 1024 * 1024
 
 
 def tapped(dst, row, tap, value):
@@ -77,7 +77,7 @@
                 tapped(taps1, m - dy, dy, value)
     arrange(wide1, first)
     arrange(wide2, second)
-    embed = table[pl.ds(meta[3], 1), :]
+    embed = table[...]
     for part in range(2):
         prod[...] = jnp.dot(
             taps1[part * 5 : part * 5 + 5].reshape(640, 960), wide1[...],
@@ -115,83 +115,88 @@
 def attend_kernel(
     meta, own0, own1, own2, own3, halo0, halo1, halo2, halo3, wq, wk, wv, bias,
     out0, out1, out2, out3,
-    field, wide, query, key, value, back,
+    field, query, key, value, score, prob, back,
 ):
     me = meta[0]
-    for at, w in enumerate((wq, wk, wv)):
-        wide[:, at * 256 : at * 256 + 256] = w[:, :256]
-        wide[:, 768 + at * 64 : 832 + at * 64] = w[:, 256:]
+    pixels = field.shape[0]
     for k, own in enumerate((own0, own1, own2, own3)):
         at = pl.multiple_of(16 + 8 * (me ^ k), 8)
-        field[:, pl.ds(at, 8), :] = own[...].astype(F32).reshape(32, 8, 320)
+        field[:, pl.ds(at, 8), :] = own[...].astype(F32).reshape(pixels, 8, 320)
     for k, halo in enumerate((halo0, halo1, halo2, halo3)):
         block = me ^ k
         at = pl.multiple_of(jnp.where(block >= 2, 8 * block - 16, 48 + 8 * block), 8)
-        field[:, pl.ds(at, 8), :] = halo[...].astype(F32).reshape(32, 8, 320)
-
-    def project(lo, hi, with_query):
-        n = hi - lo
-        x = field[:, lo:hi, :].reshape(32 * n, 320).astype(BF)
-        out = jnp.dot(x, wide[...], preferred_element_type=F32).astype(BF)
-        if with_query:
-            query[:, :, 0:256] = out[:, 0:256].reshape(32, n, 256)
-            query[:, :, 256:320] = out[:, 768:832].reshape(32, n, 64)
-        key[:, lo:hi, 0:256] = out[:, 256:512].reshape(32, n, 256)
-        key[:, lo:hi, 256:320] = out[:, 832:896].reshape(32, n, 64)
-        value[:, lo:hi, 0:256] = out[:, 512:768].reshape(32, n, 256)
-        value[:, lo:hi, 256:320] = out[:, 896:960].reshape(32, n, 64)
-
-    project(16, 48, True)
-    project(0, 16, False)
-    project(48, 64, False)
-
-    lane = lax.broadcasted_iota(jnp.int32, (1, 1, 256), 2)
-    head = lax.broadcasted_iota(jnp.int32, (6, 1, 1), 0)
-    mask6 = (lane >= head * 40) & (lane < head * 40 + 40)
-    lane = lax.broadcasted_iota(jnp.int32, (1, 1, 192), 2)
-    head = lax.broadcasted_iota(jnp.int32, (2, 1, 1), 0)
-    mask2 = (lane >= 112 + head * 40) & (lane < 152 + head * 40)
-    ones6 = mask6.astype(F32)
-    ones2 = mask2.astype(F32)
-    spread6 = ones6.astype(BF)
-    spread2 = ones2.astype(BF)
-    scale = 40.0 ** -0.5 / math.log(2.0)
+        field[:, pl.ds(at, 8), :] = halo[...].astype(F32).reshape(pixels, 8, 320)
+
+    def project(x, w):
+        return jnp.dot(x, w[...], preferred_element_type=F32).astype(BF)
+
+    x = field[...].reshape(pixels * 64, 320).astype(BF)
+    key[...] = project(x, wk).reshape(pixels, 64, 320)
+    value[...] = project(x, wv).reshape(pixels, 64, 320)
+    x = field[:, 16:48, :].reshape(pixels * 32, 320).astype(BF)
+    query[...] = project(x, wq).reshape(pixels, 32, 320)
+
+    def heads_at(lanes, base):
+        lane = lax.broadcasted_iota(jnp.int32, (4, 1, lanes), 2)
+        first = base + 40 * lax.broadcasted_iota(jnp.int32, (4, 1, lanes), 0)
+        return ((lane >= first) & (lane < first + 40)).astype(F32).astype(BF)
+
+    spread_low = heads_at(256, 0)
+    spread_high = heads_at(192, 32)
+    scale = 40.0**-0.5 / math.log(2.0)
     across = (((1,), (1,)), ((), ()))
 
-    def pixel(p):
+    def scores(p):
         q = query[p]
         k = key[p]
+        low = (q[None, :, 0:256] * spread_low).reshape(128, 256)
+        high = (q[None, :, 128:320] * spread_high).reshape(128, 192)
+        score[p, :, 0:128] = lax.dot_general(
+            k[:, 0:256], low, across, preferred_element_type=F32
+        )
+        score[p, :, 128:256] = lax.dot_general(
+            k[:, 128:320], high, across, preferred_element_type=F32
+        )
+
+    def softmax(p):
+        s = score[p] * scale + bias[...]
+        e = jnp.exp2(s - jnp.max(s, axis=0, keepdims=True))
+        prob[p] = (e * (1.0 / jnp.sum(e, axis=0, keepdims=True))).astype(BF)
+
+    def inside(h, lanes, base):
+        lane = lax.broadcasted_iota(jnp.int32, (1, lanes), 1) + base
+        return (lane >= 40 * h) & (lane < 40 * h + 40)
+
+    def attended(p):
+        w = prob[p].T
         v = value[p]
-        q6 = (q[None, :, 0:256] * spread6).reshape(192, 256)
-        q2 = (q[None, :, 128:320] * spread2).reshape(64, 192)
-        s = jnp.concatenate(
-            [
-                lax.dot_general(q6, k[:, 0:256], across, preferred_element_type=F32),
-                lax.dot_general(q2, k[:, 128:320], across, preferred_element_type=F32),
-            ],
-            axis=0,
-        )
-        s = s * scale + bias[...]
-        e = jnp.exp2(s - jnp.max(s, axis=1, keepdims=True))
-        w = (e / jnp.sum(e, axis=1, keepdims=True)).astype(BF)
-        o6 = jnp.dot(w[:192], v[:, 0:256], preferred_element_type=F32)
-        o2 = jnp.dot(w[192:], v[:, 128:320], preferred_element_type=F32)
-        a6 = jnp.sum(o6.reshape(6, 32, 256) * ones6, axis=0)
-        a2 = jnp.sum(o2.reshape(2, 32, 192) * ones2, axis=0)
-        att = jnp.concatenate(
-            [a6[:, 0:128], a6[:, 128:256] + a2[:, 0:128], a2[:, 128:192]], axis=1
-        )
+        low = jnp.dot(w[0:128], v[:, 0:256], preferred_element_type=F32)
+        high = jnp.dot(w[128:256], v[:, 128:320], preferred_element_type=F32)
+        left = low[0:32, 0:128]
+        for h in (1, 2, 3):
+            left = jnp.where(inside(h, 128, 0), low[32 * h : 32 * h + 32, 0:128], left)
+        middle = low[96:128, 128:256]
+        for h in (4, 5, 6):
+            at = 32 * h - 128
+            middle = jnp.where(inside(h, 128, 128), high[at : at + 32, 0:128], middle)
+        right = jnp.where(inside(7, 64, 256), high[96:128, 128:192], high[64:96, 128:192])
+        att = jnp.concatenate([left, middle, right], axis=1)
         for b in range(4):
             back[b, p] = att[8 * b : 8 * b + 8]
 
-    def some(i, carry):
-        for j in range(4):
-            pixel(i * 4 + j)
-        return carry
-
-    lax.fori_loop(0, 8, some, 0)
+    def each(step):
+        def some(i, carry):
+            for j in range(16):
+                step(i * 16 + j)
+            return carry
+
+        lax.fori_loop(0, pixels // 16, some, 0)
+
+    each(scores)
+    each(softmax)
+    each(attended)
     for k, out in enumerate((out0, out1, out2, out3)):
-        out[...] = back[me ^ k].reshape(256, 320).astype(BF)
+        out[...] = back[me ^ k].reshape(pixels * 8, 320).astype(BF)
 
 
 def final_kernel(meta, a0, a1, a2, a3, w_out, flat, out, total):
@@ -223,9 +228,8 @@
     place = lax.axis_index("frame")
     band = lax.axis_index("band")
     me = place % GROUP
-    step = step_index[0]
     meta = jnp.stack(
-        [me, (band == 0).astype(jnp.int32), (band == bands - 1).astype(jnp.int32), step % 8, step // 8]
+        [me, (band == 0).astype(jnp.int32), (band == bands - 1).astype(jnp.int32)]
     ).astype(jnp.int32)
 
     up = [(i, i + 1) for i in range(bands - 1)]
@@ -242,7 +246,7 @@
     bias = jnp.einsum("hs,ijs->hij", rel_bias, picks, precision=lax.Precision.HIGHEST)
     reach_q = lax.dynamic_slice_in_dim(reach, (place // GROUP) * 32, 32)
     allowed = np.abs(delta) <= reach_q[:, None]
-    bias = jnp.where(allowed[None], bias * (1.0 / math.log(2.0)), -jnp.inf).reshape(256, 64)
+    bias = jnp.where(allowed[None], bias * (1.0 / math.log(2.0)), -jnp.inf).reshape(256, 64).T
 
     whole = pl.BlockSpec(memory_space=pltpu.VMEM)
     smem = pl.BlockSpec(memory_space=pltpu.SMEM)
@@ -252,32 +256,24 @@
     def at(shape):
         return pl.BlockSpec(shape, lambda i, m: (0,) * len(shape))
 
+    embed = lax.dynamic_slice_in_dim(time_table, step_index[0], 1)
     n0, n1, n2, n3, flat = pl.pallas_call(
         conv_kernel,
-        grid_spec=pltpu.PrefetchScalarGridSpec(
-            num_scalar_prefetch=1,
-            grid=(1,),
-            in_specs=[
-                at((8, 8, 16, 320)), at((8, 8, 16, 320)), at((8, 2, 16, 320)), at((8, 2, 16, 320)),
-                at((3, 3, 320, 320)), at((3, 3, 320, 320)),
-                pl.BlockSpec((8, 320), lambda i, m: (m[4], 0)),
-                at((1, 320)),
-            ],
-            out_specs=[at((256, 320))] * 4 + [at((8, 128, 320))],
-            scratch_shapes=[
-                pltpu.VMEM((3, 12, 128, 128), F32),
-                pltpu.VMEM((10, 128, 960), BF),
-                pltpu.VMEM((8, 128, 960), BF),
-                pltpu.VMEM((960, 960), BF),
-                pltpu.VMEM((960, 960), BF),
-                pltpu.VMEM((640, 960), F32),
-                pltpu.VMEM((8, 128, 320), BF),
-            ],
-        ),
+        in_specs=[smem] + [whole] * 8,
+        out_specs=[whole] * 5,
+        scratch_shapes=[
+            pltpu.VMEM((3, 12, 128, 128), F32),
+            pltpu.VMEM((10, 128, 960), BF),
+            pltpu.VMEM((8, 128, 960), BF),
+            pltpu.VMEM((960, 960), BF),
+            pltpu.VMEM((960, 960), BF),
+            pltpu.VMEM((640, 960), F32),
+            pltpu.VMEM((8, 128, 320), BF),
+        ],
         out_shape=[piece] * 4 + [jax.ShapeDtypeStruct((8, 128, 320), F32)],
         compiler_params=params,
         name="conv_block",
-    )(meta, frames, control, low, high, conv_first, conv_second, time_table, norm_gain[None])
+    )(meta, frames, control, low, high, conv_first, conv_second, embed, norm_gain[None])
 
     pieces = (n0, n1, n2, n3)
 
@@ -310,10 +306,11 @@
         out_shape=[piece] * 4,
         scratch_shapes=[
             pltpu.VMEM((32, 64, 320), F32),
-            pltpu.VMEM((320, 960), BF),
             pltpu.VMEM((32, 32, 320), BF),
             pltpu.VMEM((32, 64, 320), BF),
             pltpu.VMEM((32, 64, 320), BF),
+            pltpu.VMEM((32, 64, 256), F32),
+            pltpu.VMEM((32, 64, 256), BF),
             pltpu.VMEM((4, 32, 8, 320), F32),
         ],
         compiler_params=params,

time: 82.3 us -> 81.1 us (0.985)
  the two profiles are of different devices: /device:TPU:1 before, /device:TPU:3 now
where the time goes in v2:
time: 81.1 us; the launch traced here: 80.8 us
  starting transfers between devices  24.6 us (30%)
  waiting for transfers between devices  23.6 us (29%)
  Pallas kernels  19.1 us (24%)
  local copies, waits for them, and re-layouts  9.87 us (12%)
  other arithmetic  2.35 us (3%)
  between operations  0.82 us (1%)
    ppermute x6, starting transfers between devices, exchange(): return lax.ppermute(x, 'frame', [(i, plane(i, k)) for i in range(count)])  10.2 us
    ppermute x6, waiting for transfers between devices, exchange(): return lax.ppermute(x, 'frame', [(i, plane(i, k)) for i in range(count)])  9.36 us
    pallas_call x1, Pallas kernels, shards(): pl.pallas_call(attend_kernel, in_specs=[smem] + [whole] * 12, out_specs=[...  8.16 us
    unnamed x37, local copies, waits for them, and re-layouts  8.01 us
    pallas_call x1, Pallas kernels, shards(): pl.pallas_call(conv_kernel, in_specs=[smem] + [whole] * 8, out_specs=[who...  7.79 us
    ppermute x2, waiting for transfers between devices, shards(): halo.append(lax.ppermute(own[k], 'frame', route))  6.26 us
    ppermute x1, waiting for transfers between devices, shards(): low = lax.ppermute(edge(slice(6, 8)), 'band', up)  5.8 us
    ppermute x2, starting transfers between devices, shards(): lax.ppermute(pieces[k], 'frame', [(i, beside(i, k)) for i in range(count)])  5.48 us
  transfers between devices with their start and end apart: 12, of which 8 were waited for; matrix products, arithmetic and copies ran while one was open for 3% of the time, Pallas kernels for 0%

profile of v2, /device:TPU:3, one launch (start us, length us, event | category | flops | bytes accessed | tf_op | source)
XLA Modules:
  0.0 80.8 jit_solution(2796905468840255260)
XLA Ops:
  0.0 0.0 copy-start
  0.0 0.0 copy-start.4
  0.0 0.0 copy-start.3
  0.0 0.0 copy-start.16
  0.0 0.0 copy-start.17
  0.0 2.2 %add_convert_fusion = (bf16[8,2,16,320]{3,2,1,0:T(8,128)(2,1)}, bf16[8,2,16,320]{3,2,1,0:T(8,128)(2,1)}) fusion(bf16[8,8,16,320]{3,2,1,0:T(8,128)(2,1)} %control.1, bf16[8,8,16,320]{3,2,1,0:T(8,128)(2,1)} %frames.1), kind=kLoop, calls=%fused_computation.3 | loop fusion | flops 655360 | bytes 983040 | tf_op jit(solution)/shard_map/convert_element_type | solution.py:239
  2.2 4.6 %collective-permute-start.1 = (bf16[8,2,16,320]{3,2,1,0:T(8,128)(2,1)}, bf16[8,2,16,320]{3,2,1,0:T(8,128)(2,1)S(1)}, u32[]{:S(2)}, u32[]{:S(2)}) collective-permute-start(bf16[8,2,16,320]{3,2,1,0:T(8,128)(2,1)} %get-tuple-element.23), channel_id=1, source_target_pairs={{1,0},{2,1},{3,2},{4,3},{5,4},{6,5},{7,6},{9,8},{10,9},{11,10},{12... | collective-permute-start | bytes 491528 | tf_op jit(solution)/shard_map/ppermute | solution.py:242
  6.8 1.9 %collective-permute-start = (bf16[8,2,16,320]{3,2,1,0:T(8,128)(2,1)}, bf16[8,2,16,320]{3,2,1,0:T(8,128)(2,1)S(1)}, u32[]{:S(2)}, u32[]{:S(2)}) collective-permute-start(bf16[8,2,16,320]{3,2,1,0:T(8,128)(2,1)} %get-tuple-element.24), channel_id=1, source_target_pairs={{0,1},{1,2},{2,3},{3,4},{4,5},{5,6},{6,7},{8,9},{9,10},{10,11},{11... | collective-permute-start | bytes 491528 | tf_op jit(solution)/shard_map/ppermute | solution.py:241
  9.4 0.0 copy-done
  9.4 0.1 constant_dynamic-slice_fusion
  9.6 0.0 copy-done.16
  9.6 0.1 copy.21.table
  9.7 0.0 copy-done.17
  9.7 0.1 dynamic_slice.7
  9.8 0.1 pad_add_fusion.meta
  9.9 0.8 %collective-permute-done.1.high = bf16[8,2,16,320]{3,2,1,0:T(8,128)(2,1)S(1)} collective-permute-done((bf16[8,2,16,320]{3,2,1,0:T(8,128)(2,1)}, bf16[8,2,16,320]{3,2,1,0:T(8,128)(2,1)S(1)}, u32[]{:S(2)}, u32[]{:S(2)}) %collective-permute-start.1) | collective-permute-done | bytes 163872 | tf_op jit(solution)/shard_map/ppermute | solution.py:242
  10.7 5.8 %collective-permute-done.low = bf16[8,2,16,320]{3,2,1,0:T(8,128)(2,1)S(1)} collective-permute-done((bf16[8,2,16,320]{3,2,1,0:T(8,128)(2,1)}, bf16[8,2,16,320]{3,2,1,0:T(8,128)(2,1)S(1)}, u32[]{:S(2)}, u32[]{:S(2)}) %collective-permute-start) | collective-permute-done | bytes 163872 | tf_op jit(solution)/shard_map/ppermute | solution.py:241
  16.5 0.0 copy-start.11
  16.5 0.7 copy-done.11
  17.2 0.0 copy-done.4
  17.2 0.0 copy-done.3
  17.2 0.0 copy-start.1
  17.2 1.6 %copy-done.1 = bf16[3,3,320,320]{3,2,1,0:T(8,128)(2,1)S(1)} copy-done((bf16[3,3,320,320]{3,2,1,0:T(8,128)(2,1)S(1)}, bf16[3,3,320,320]{3,2,1,0:T(8,128)(2,1)}, u32[]{:S(2)}) %copy-start.1) | copy-done | bytes 1843224
  18.8 0.0 copy-start.2
  18.8 1.6 %copy-done.2 = bf16[3,3,320,320]{3,2,1,0:T(8,128)(2,1)S(1)} copy-done((bf16[3,3,320,320]{3,2,1,0:T(8,128)(2,1)S(1)}, bf16[3,3,320,320]{3,2,1,0:T(8,128)(2,1)}, u32[]{:S(2)}) %copy-start.2) | copy-done | bytes 1843224
  20.4 0.9 %copy-done.12 = bf16[8,2,16,320]{3,2,1,0:T(8,128)(2,1)S(1)} copy-done((bf16[8,2,16,320]{3,2,1,0:T(8,128)(2,1)S(1)}, bf16[8,2,16,320]{3,2,1,0:T(8,128)(2,1)}, u32[]{:S(2)}) %copy-start.12) | copy-done | bytes 163864
  21.4 7.8 %conv_block.1 = (bf16[256,320]{1,0:T(8,128)(2,1)}, bf16[256,320]{1,0:T(8,128)(2,1)}, bf16[256,320]{1,0:T(8,128)(2,1)S(1)}, bf16[256,320]{1,0:T(8,128)(2,1)S(1)}, f32[8,128,320]{2,1,0:T(8,128)S(1)}) custom-call(s32[3]{0:T(128)S(1)} %pad_add_fusion.meta, bf16[8,8,16,320]{3,2,1,0:T(8,128)(2,1)S(1)} %copy-done.3, bf16[8,8,16,320]{3,2,1,0:T(8,128)(2,1)S(1)} %copy-done.4, ...), custom_call_target="tpu_custom_call" | custom-call | tf_op jit(solution)/shard_map/conv_block/pallas_call | solution.py:260
  29.2 1.1 %copy-done.5 = f32[8,128,320]{2,1,0:T(8,128)} copy-done((f32[8,128,320]{2,1,0:T(8,128)}, f32[8,128,320]{2,1,0:T(8,128)S(1)}, u32[]{:S(2)}) %copy-start.5) | copy-done | bytes 1310744
  30.3 2.2 %collective-permute-start.3 = (bf16[256,320]{1,0:T(8,128)(2,1)S(1)}, bf16[256,320]{1,0:T(8,128)(2,1)}, u32[]{:S(2)}, u32[]{:S(2)}) collective-permute-start(bf16[256,320]{1,0:T(8,128)(2,1)S(1)} %get-tuple-element.16), channel_id=1, source_target_pairs={{0,16},{8,24},{16,0},{24,8},{32,48},{40,56},{48,32},{56,40},{64,80... | collective-permute-start | bytes 491528 | tf_op jit(solution)/shard_map/ppermute | solution.py:284
  32.5 2.9 %collective-permute-start.4 = (bf16[256,320]{1,0:T(8,128)(2,1)S(1)}, bf16[256,320]{1,0:T(8,128)(2,1)}, u32[]{:S(2)}, u32[]{:S(2)}) collective-permute-start(bf16[256,320]{1,0:T(8,128)(2,1)S(1)} %get-tuple-element.17), channel_id=1, source_target_pairs={{0,24},{8,16},{16,8},{24,0},{32,56},{40,48},{48,40},{56,32},{64,88... | collective-permute-start | bytes 491528 | tf_op jit(solution)/shard_map/ppermute | solution.py:284
  35.3 0.0 copy-done.14
  35.3 0.1 broadcast_compare_fusion
  35.4 4.7 %collective-permute-start.6 = (bf16[256,320]{1,0:T(8,128)(2,1)}, bf16[256,320]{1,0:T(8,128)(2,1)}, u32[]{:S(2)}, u32[]{:S(2)}) collective-permute-start(bf16[256,320]{1,0:T(8,128)(2,1)} %get-tuple-element.15), channel_id=1, source_target_pairs={{0,232},{8,224},{16,56},{24,48},{32,8},{40,0},{48,88},{56,80},{64,... | collective-permute-start | bytes 491528 | tf_op jit(solution)/shard_map/ppermute | solution.py:292
  40.2 1.2 %collective-permute-start.2 = (bf16[256,320]{1,0:T(8,128)(2,1)}, bf16[256,320]{1,0:T(8,128)(2,1)}, u32[]{:S(2)}, u32[]{:S(2)}) collective-permute-start(bf16[256,320]{1,0:T(8,128)(2,1)} %get-tuple-element.15), channel_id=1, source_target_pairs={{0,8},{8,0},{16,24},{24,16},{32,40},{40,32},{48,56},{56,48},{64,72... | collective-permute-start | bytes 491528 | tf_op jit(solution)/shard_map/ppermute | solution.py:284
  41.4 0.7 collective-permute-start.5
  42.1 0.0 collective-permute-done.3.own2
  42.1 0.7 collective-permute-start.7
  42.9 0.2 collective-permute-done.4.own3
  43.1 1.6 %collective-permute-start.8 = (bf16[256,320]{1,0:T(8,128)(2,1)}, bf16[256,320]{1,0:T(8,128)(2,1)}, u32[]{:S(2)}, u32[]{:S(2)}) collective-permute-start(bf16[256,320]{1,0:T(8,128)(2,1)} %collective-permute-done.4.own3), channel_id=1, source_target_pairs={{0,32},{8,40},{16,240},{24,248},{32,64},{40,72},{48,16},{56,24},{6... | collective-permute-start | bytes 491528 | tf_op jit(solution)/shard_map/ppermute | solution.py:300
  44.7 0.0 copy-done.13
  44.7 0.0 copy-done.15
  44.7 0.5 fusion.1
  45.2 0.0 copy-start.6
  45.2 0.0 copy-start.7
  45.2 0.7 copy.19
  45.9 1.0 %copy.20 = f32[256,64]{0,1:T(8,128)S(1)} copy(f32[256,64]{1,0:T(8,128)} %bitcast.16) | data formatting | bytes 131072 | tf_op jit(solution)/shard_map/reshape | solution.py:249
  46.9 1.4 %collective-permute-done.5.halo0 = bf16[256,320]{1,0:T(8,128)(2,1)} collective-permute-done((bf16[256,320]{1,0:T(8,128)(2,1)}, bf16[256,320]{1,0:T(8,128)(2,1)}, u32[]{:S(2)}, u32[]{:S(2)}) %collective-permute-start.5) | collective-permute-done | bytes 163872 | tf_op jit(solution)/shard_map/ppermute | solution.py:292
  48.2 0.0 collective-permute-done.6.halo1
  48.2 0.0 collective-permute-done.2.own1
  48.2 1.6 %collective-permute-done.7.halo2 = bf16[256,320]{1,0:T(8,128)(2,1)} collective-permute-done((bf16[256,320]{1,0:T(8,128)(2,1)}, bf16[256,320]{1,0:T(8,128)(2,1)}, u32[]{:S(2)}, u32[]{:S(2)}) %collective-permute-start.7) | collective-permute-done | bytes 163872 | tf_op jit(solution)/shard_map/ppermute | solution.py:300
  49.9 4.6 %collective-permute-done.8.halo3 = bf16[256,320]{1,0:T(8,128)(2,1)} collective-permute-done((bf16[256,320]{1,0:T(8,128)(2,1)}, bf16[256,320]{1,0:T(8,128)(2,1)}, u32[]{:S(2)}, u32[]{:S(2)}) %collective-permute-start.8) | collective-permute-done | bytes 163872 | tf_op jit(solution)/shard_map/ppermute | solution.py:300
  54.5 0.0 copy-done.8
  54.5 0.9 %copy-done.9 = bf16[320,320]{1,0:T(8,128)(2,1)S(1)} copy-done((bf16[320,320]{1,0:T(8,128)(2,1)S(1)}, bf16[320,320]{1,0:T(8,128)(2,1)}, u32[]{:S(2)}) %copy-start.9) | copy-done | bytes 204824
  55.4 0.9 %copy-done.10 = bf16[320,320]{1,0:T(8,128)(2,1)S(1)} copy-done((bf16[320,320]{1,0:T(8,128)(2,1)S(1)}, bf16[320,320]{1,0:T(8,128)(2,1)}, u32[]{:S(2)}) %copy-start.10) | copy-done | bytes 204824
  56.4 8.2 %attend.1 = (bf16[256,320]{1,0:T(8,128)(2,1)S(1)}, bf16[256,320]{1,0:T(8,128)(2,1)S(1)}, bf16[256,320]{1,0:T(8,128)(2,1)S(1)}, bf16[256,320]{1,0:T(8,128)(2,1)S(1)}) custom-call(s32[3]{0:T(128)S(1)} %pad_add_fusion.meta, bf16[256,320]{1,0:T(8,128)(2,1)} %get-tuple-element.14.own0, bf16[256,320]{1,0:T(8,128)(2,1)} %collective-permute-done.2.own1, ...), custom_call_target="tpu_custom_call" | custom-call | tf_op jit(solution)/shard_map/attend/pallas_call | solution.py:302
  64.6 0.8 collective-permute-start.9
  65.3 1.6 %collective-permute-start.10 = (bf16[256,320]{1,0:T(8,128)(2,1)S(1)}, bf16[256,320]{1,0:T(8,128)(2,1)S(1)}, u32[]{:S(2)}, u32[]{:S(2)}) collective-permute-start(bf16[256,320]{1,0:T(8,128)(2,1)S(1)} %get-tuple-element.20), channel_id=1, source_target_pairs={{0,16},{8,24},{16,0},{24,8},{32,48},{40,56},{48,32},{56,40},{64,80... | collective-permute-start | bytes 491528 | tf_op jit(solution)/shard_map/ppermute | solution.py:284
  67.0 1.6 %collective-permute-start.11 = (bf16[256,320]{1,0:T(8,128)(2,1)S(1)}, bf16[256,320]{1,0:T(8,128)(2,1)S(1)}, u32[]{:S(2)}, u32[]{:S(2)}) collective-permute-start(bf16[256,320]{1,0:T(8,128)(2,1)S(1)} %get-tuple-element.21), channel_id=1, source_target_pairs={{0,24},{8,16},{16,8},{24,0},{32,56},{40,48},{48,40},{56,32},{64,88... | collective-permute-start | bytes 491528 | tf_op jit(solution)/shard_map/ppermute | solution.py:284
  68.6 0.0 collective-permute-done.9.a1
  68.6 4.7 %collective-permute-done.10.a2 = bf16[256,320]{1,0:T(8,128)(2,1)S(1)} collective-permute-done((bf16[256,320]{1,0:T(8,128)(2,1)S(1)}, bf16[256,320]{1,0:T(8,128)(2,1)S(1)}, u32[]{:S(2)}, u32[]{:S(2)}) %collective-permute-start.10) | collective-permute-done | bytes 163872 | tf_op jit(solution)/shard_map/ppermute | solution.py:284
  73.3 4.4 %collective-permute-done.11.a3 = bf16[256,320]{1,0:T(8,128)(2,1)S(1)} collective-permute-done((bf16[256,320]{1,0:T(8,128)(2,1)S(1)}, bf16[256,320]{1,0:T(8,128)(2,1)S(1)}, u32[]{:S(2)}, u32[]{:S(2)}) %collective-permute-start.11) | collective-permute-done | bytes 163872 | tf_op jit(solution)/shard_map/ppermute | solution.py:284
  77.7 0.0 copy-done.6
  77.7 0.0 copy-done.7
  77.7 3.1 %project_out.1 = f32[8,8,16,320]{3,2,1,0:T(8,128)} custom-call(s32[3]{0:T(128)S(1)} %pad_add_fusion.meta, bf16[256,320]{1,0:T(8,128)(2,1)S(1)} %get-tuple-element.18.a0, bf16[256,320]{1,0:T(8,128)(2,1)S(1)} %collective-permute-done.9.a1, bf16[256,320]{1,0:T(8,128)(2,1)S(1)} %collective-permute-done.10.a2, bf16[256,320]{1,0:T(8,128)(2,1)S(1)} %collective-permute-done.11.a3, ...), custom_call_target="tpu_custom_call" | custom-call | tf_op jit(solution)/shard_map/project_out/pallas_call | solution.py:322
  (9 shorter events, 0.0 us)
Async XLA Ops:
  0.0 9.4 %copy-start = (f32[1000,320]{0,1:T(8,128)S(1)}, f32[1000,320]{0,1:T(8,128)}, u32[]{:S(2)}) copy-start(f32[1000,320]{0,1:T(8,128)} %param.19) | copy-start | bytes 3840004
  0.0 17.2 %copy-start.4 = (bf16[8,8,16,320]{3,2,1,0:T(8,128)(2,1)S(1)}, bf16[8,8,16,320]{3,2,1,0:T(8,128)(2,1)}, u32[]{:S(2)}) copy-start(bf16[8,8,16,320]{3,2,1,0:T(8,128)(2,1)} %control.1) | copy-start | bytes 1966084
  0.0 17.2 %copy-start.3 = (bf16[8,8,16,320]{3,2,1,0:T(8,128)(2,1)S(1)}, bf16[8,8,16,320]{3,2,1,0:T(8,128)(2,1)}, u32[]{:S(2)}) copy-start(bf16[8,8,16,320]{3,2,1,0:T(8,128)(2,1)} %frames.1) | copy-start | bytes 1966084
  0.0 9.6 %copy-start.16 = (f32[320]{0:T(512)S(1)}, f32[320]{0:T(512)}, u32[]{:S(2)}) copy-start(f32[320]{0:T(512)} %param.21) | copy-start | bytes 3844
  0.0 9.7 %copy-start.17 = (s32[256]{0:T(256)S(1)}, s32[256]{0:T(256)}, u32[]{:S(2)}) copy-start(s32[256]{0:T(256)} %param.27) | copy-start | bytes 3076
  2.2 8.5 %collective-permute-start.1 = (bf16[8,2,16,320]{3,2,1,0:T(8,128)(2,1)}, bf16[8,2,16,320]{3,2,1,0:T(8,128)(2,1)S(1)}, u32[]{:S(2)}, u32[]{:S(2)}) collective-permute-start(bf16[8,2,16,320]{3,2,1,0:T(8,128)(2,1)} %get-tuple-element.23), channel_id=1, source_target_pairs={{1,0},{2,1},{3,2},{4,3},{5,4},{6,5},{7,6},{9,8},{10,9},{11,10},{12... | collective-permute-start | bytes 491528 | tf_op jit(solution)/shard_map/ppermute | solution.py:242
  6.8 9.7 %collective-permute-start = (bf16[8,2,16,320]{3,2,1,0:T(8,128)(2,1)}, bf16[8,2,16,320]{3,2,1,0:T(8,128)(2,1)S(1)}, u32[]{:S(2)}, u32[]{:S(2)}) collective-permute-start(bf16[8,2,16,320]{3,2,1,0:T(8,128)(2,1)} %get-tuple-element.24), channel_id=1, source_target_pairs={{0,1},{1,2},{2,3},{3,4},{4,5},{5,6},{6,7},{8,9},{9,10},{10,11},{11... | collective-permute-start | bytes 491528 | tf_op jit(solution)/shard_map/ppermute | solution.py:241
  16.5 0.7 copy-start.11
  17.2 1.6 %copy-start.1 = (bf16[3,3,320,320]{3,2,1,0:T(8,128)(2,1)S(1)}, bf16[3,3,320,320]{3,2,1,0:T(8,128)(2,1)}, u32[]{:S(2)}) copy-start(bf16[3,3,320,320]{3,2,1,0:T(8,128)(2,1)} %first.1) | copy-start | bytes 5529604
  18.8 1.6 %copy-start.2 = (bf16[3,3,320,320]{3,2,1,0:T(8,128)(2,1)S(1)}, bf16[3,3,320,320]{3,2,1,0:T(8,128)(2,1)}, u32[]{:S(2)}) copy-start(bf16[3,3,320,320]{3,2,1,0:T(8,128)(2,1)} %second.1) | copy-start | bytes 5529604
  20.4 0.9 %copy-start.12 = (bf16[8,2,16,320]{3,2,1,0:T(8,128)(2,1)S(1)}, bf16[8,2,16,320]{3,2,1,0:T(8,128)(2,1)}, u32[]{:S(2)}) copy-start(bf16[8,2,16,320]{3,2,1,0:T(8,128)(2,1)} %copy-done.11) | copy-start | bytes 491524
  21.4 14.0 %copy-start.14 = (s32[32,64]{1,0:T(8,128)S(1)}, s32[32,64]{1,0:T(8,128)}, u32[]{:S(2)}) copy-start(s32[32,64]{1,0:T(8,128)} %constant.53.clone) | copy-start | bytes 24580
  21.4 23.3 %copy-start.13 = (f32[32,64,33]{1,2,0:T(8,128)S(1)}, f32[32,64,33]{1,2,0:T(8,128)}, u32[]{:S(2)}) copy-start(f32[32,64,33]{1,2,0:T(8,128)} %constant.52.clone) | copy-start | bytes 811012
  21.4 23.3 %copy-start.15 = (f32[8,33]{1,0:T(8,128)S(1)}, f32[8,33]{1,0:T(8,128)}, u32[]{:S(2)}) copy-start(f32[8,33]{1,0:T(8,128)} %param.26) | copy-start | bytes 3172
  21.4 33.1 %copy-start.8 = (bf16[320,320]{1,0:T(8,128)(2,1)S(1)}, bf16[320,320]{1,0:T(8,128)(2,1)}, u32[]{:S(2)}) copy-start(bf16[320,320]{1,0:T(8,128)(2,1)} %wq.1) | copy-start | bytes 614404
  29.2 1.1 %copy-start.5 = (f32[8,128,320]{2,1,0:T(8,128)}, f32[8,128,320]{2,1,0:T(8,128)S(1)}, u32[]{:S(2)}) copy-start(f32[8,128,320]{2,1,0:T(8,128)S(1)} %get-tuple-element.22.flat) | copy-start | bytes 3932164
  30.3 11.8 %collective-permute-start.3 = (bf16[256,320]{1,0:T(8,128)(2,1)S(1)}, bf16[256,320]{1,0:T(8,128)(2,1)}, u32[]{:S(2)}, u32[]{:S(2)}) collective-permute-start(bf16[256,320]{1,0:T(8,128)(2,1)S(1)} %get-tuple-element.16), channel_id=1, source_target_pairs={{0,16},{8,24},{16,0},{24,8},{32,48},{40,56},{48,32},{56,40},{64,80... | collective-permute-start | bytes 491528 | tf_op jit(solution)/shard_map/ppermute | solution.py:284
  32.5 10.6 %collective-permute-start.4 = (bf16[256,320]{1,0:T(8,128)(2,1)S(1)}, bf16[256,320]{1,0:T(8,128)(2,1)}, u32[]{:S(2)}, u32[]{:S(2)}) collective-permute-start(bf16[256,320]{1,0:T(8,128)(2,1)S(1)} %get-tuple-element.17), channel_id=1, source_target_pairs={{0,24},{8,16},{16,8},{24,0},{32,56},{40,48},{48,40},{56,32},{64,88... | collective-permute-start | bytes 491528 | tf_op jit(solution)/shard_map/ppermute | solution.py:284
  35.4 12.8 %collective-permute-start.6 = (bf16[256,320]{1,0:T(8,128)(2,1)}, bf16[256,320]{1,0:T(8,128)(2,1)}, u32[]{:S(2)}, u32[]{:S(2)}) collective-permute-start(bf16[256,320]{1,0:T(8,128)(2,1)} %get-tuple-element.15), channel_id=1, source_target_pairs={{0,232},{8,224},{16,56},{24,48},{32,8},{40,0},{48,88},{56,80},{64,... | collective-permute-start | bytes 491528 | tf_op jit(solution)/shard_map/ppermute | solution.py:292
  40.2 8.1 %collective-permute-start.2 = (bf16[256,320]{1,0:T(8,128)(2,1)}, bf16[256,320]{1,0:T(8,128)(2,1)}, u32[]{:S(2)}, u32[]{:S(2)}) collective-permute-start(bf16[256,320]{1,0:T(8,128)(2,1)} %get-tuple-element.15), channel_id=1, source_target_pairs={{0,8},{8,0},{16,24},{24,16},{32,40},{40,32},{48,56},{56,48},{64,72... | collective-permute-start | bytes 491528 | tf_op jit(solution)/shard_map/ppermute | solution.py:284
  41.4 6.8 %collective-permute-start.5 = (bf16[256,320]{1,0:T(8,128)(2,1)}, bf16[256,320]{1,0:T(8,128)(2,1)}, u32[]{:S(2)}, u32[]{:S(2)}) collective-permute-start(bf16[256,320]{1,0:T(8,128)(2,1)} %get-tuple-element.14.own0), channel_id=1, source_target_pairs={{0,224},{8,232},{16,48},{24,56},{32,0},{40,8},{48,80},{56,88},{64,... | collective-permute-start | bytes 491528 | tf_op jit(solution)/shard_map/ppermute | solution.py:292
  42.1 7.7 %collective-permute-start.7 = (bf16[256,320]{1,0:T(8,128)(2,1)}, bf16[256,320]{1,0:T(8,128)(2,1)}, u32[]{:S(2)}, u32[]{:S(2)}) collective-permute-start(bf16[256,320]{1,0:T(8,128)(2,1)} %collective-permute-done.3.own2), channel_id=1, source_target_pairs={{0,32},{8,40},{16,240},{24,248},{32,64},{40,72},{48,16},{56,24},{6... | collective-permute-start | bytes 491528 | tf_op jit(solution)/shard_map/ppermute | solution.py:300
  43.1 11.4 %collective-permute-start.8 = (bf16[256,320]{1,0:T(8,128)(2,1)}, bf16[256,320]{1,0:T(8,128)(2,1)}, u32[]{:S(2)}, u32[]{:S(2)}) collective-permute-start(bf16[256,320]{1,0:T(8,128)(2,1)} %collective-permute-done.4.own3), channel_id=1, source_target_pairs={{0,32},{8,40},{16,240},{24,248},{32,64},{40,72},{48,16},{56,24},{6... | collective-permute-start | bytes 491528 | tf_op jit(solution)/shard_map/ppermute | solution.py:300
  45.2 32.5 %copy-start.6 = (f32[8,128,320]{2,1,0:T(8,128)S(1)}, f32[8,128,320]{2,1,0:T(8,128)}, u32[]{:S(2)}) copy-start(f32[8,128,320]{2,1,0:T(8,128)} %copy-done.5) | copy-start | bytes 3932164
  45.2 32.5 %copy-start.7 = (bf16[320,320]{1,0:T(8,128)(2,1)S(1)}, bf16[320,320]{1,0:T(8,128)(2,1)}, u32[]{:S(2)}) copy-start(bf16[320,320]{1,0:T(8,128)(2,1)} %w_out.1) | copy-start | bytes 614404
  54.5 0.9 %copy-start.9 = (bf16[320,320]{1,0:T(8,128)(2,1)S(1)}, bf16[320,320]{1,0:T(8,128)(2,1)}, u32[]{:S(2)}) copy-start(bf16[320,320]{1,0:T(8,128)(2,1)} %wk.1) | copy-start | bytes 614404
  55.4 0.9 %copy-start.10 = (bf16[320,320]{1,0:T(8,128)(2,1)S(1)}, bf16[320,320]{1,0:T(8,128)(2,1)}, u32[]{:S(2)}) copy-start(bf16[320,320]{1,0:T(8,128)(2,1)} %wv.1) | copy-start | bytes 614404
  64.6 4.0 %collective-permute-start.9 = (bf16[256,320]{1,0:T(8,128)(2,1)S(1)}, bf16[256,320]{1,0:T(8,128)(2,1)S(1)}, u32[]{:S(2)}, u32[]{:S(2)}) collective-permute-start(bf16[256,320]{1,0:T(8,128)(2,1)S(1)} %get-tuple-element.19), channel_id=1, source_target_pairs={{0,8},{8,0},{16,24},{24,16},{32,40},{40,32},{48,56},{56,48},{64,72... | collective-permute-start | bytes 491528 | tf_op jit(solution)/shard_map/ppermute | solution.py:284
  65.3 8.0 %collective-permute-start.10 = (bf16[256,320]{1,0:T(8,128)(2,1)S(1)}, bf16[256,320]{1,0:T(8,128)(2,1)S(1)}, u32[]{:S(2)}, u32[]{:S(2)}) collective-permute-start(bf16[256,320]{1,0:T(8,128)(2,1)S(1)} %get-tuple-element.20), channel_id=1, source_target_pairs={{0,16},{8,24},{16,0},{24,8},{32,48},{40,56},{48,32},{56,40},{64,80... | collective-permute-start | bytes 491528 | tf_op jit(solution)/shard_map/ppermute | solution.py:284
  67.0 10.7 %collective-permute-start.11 = (bf16[256,320]{1,0:T(8,128)(2,1)S(1)}, bf16[256,320]{1,0:T(8,128)(2,1)S(1)}, u32[]{:S(2)}, u32[]{:S(2)}) collective-permute-start(bf16[256,320]{1,0:T(8,128)(2,1)S(1)} %get-tuple-element.21), channel_id=1, source_target_pairs={{0,24},{8,16},{16,8},{24,0},{32,56},{40,48},{48,40},{56,32},{64,88... | collective-permute-start | bytes 491528 | tf_op jit(solution)/shard_map/ppermute | solution.py:284

commit v3 on v2

v3 whole, which is shorter than its diff:
```python
import math

import jax
import jax.numpy as jnp
from jax import lax
from jax.experimental import pallas as pl
from jax.experimental.pallas import tpu as pltpu
from jax.sharding import PartitionSpec as P

BF = jnp.bfloat16
F32 = jnp.float32
GROUP = 4
MIB = 1024 * 1024


def tapped(dst, row, tap, value):
    dst[row, :, tap * 256 : tap * 256 + 256] = value[:, :256]
    dst[row, :, 768 + tap * 64 : 832 + tap * 64] = value[:, 256:]


def arrange(dst, weight):
    for dy in range(3):
        for dx in range(3):
            w = weight[dy, dx]
            top = slice(dy * 256, dy * 256 + 256)
            low = slice(768 + dy * 64, 832 + dy * 64)
            left = slice(dx * 256, dx * 256 + 256)
            right = slice(768 + dx * 64, 832 + dx * 64)
            dst[top, left] = w[:256, :256]
            dst[top, right] = w[:256, 256:]
            dst[low, left] = w[256:, :256]
            dst[low, right] = w[256:, 256:]


def combine(prod, row):
    rows = slice(row * 128, row * 128 + 128)

    def shifted(a, b, c):
        gap = jnp.zeros((8, a.shape[1]), F32)
        return (
            b
            + jnp.concatenate([gap, a[:-8]], axis=0)
            + jnp.concatenate([c[8:], gap], axis=0)
        )

    main = shifted(prod[rows, 0:256], prod[rows, 256:512], prod[rows, 512:768])
    rest = shifted(prod[rows, 768:832], prod[rows, 832:896], prod[rows, 896:960])
    return jnp.concatenate([main, rest], axis=1)


def put(merged, row, f, value):
    value = value.astype(BF).astype(F32)
    rest = jnp.concatenate([value[:, 256:], jnp.zeros((16, 64), F32)], axis=1)
    for j, part in enumerate((value[:, :128], value[:, 128:256], rest)):
        merged[j, row, pl.ds(f, 16, stride=8), :] = part


def taken(merged, row):
    return jnp.concatenate([merged[0, row], merged[1, row], merged[2, row, :, :64]], axis=1)


def multiply(prod, taps, wide, count):
    prod[0 : count * 128, :] = jnp.dot(
        taps[...].reshape(count * 128, 960), wide[...], preferred_element_type=F32
    )


def silu(t):
    return t * (0.5 * jnp.tanh(0.5 * t) + 0.5)


def layer_norm(block, gain):
    mean = jnp.sum(block, axis=1, keepdims=True) * (1.0 / 320)
    centre = block - mean
    var = jnp.sum(centre * centre, axis=1, keepdims=True) * (1.0 / 320)
    return (centre * lax.rsqrt(var + 1e-5) * gain).astype(BF)


def hand_out(me, normed, keep, give):
    keep[0] = normed[me]
    keep[1] = normed[me ^ 2]
    give[0] = normed[me ^ 1]
    give[1] = normed[me ^ 3]


def in_group():
    return lax.axis_index("frame") % GROUP


def edges_kernel(frames, control, top, bottom, fbuf, cbuf, sems):
    loads = []
    for i, (src, dst) in enumerate(((frames, fbuf), (control, cbuf))):
        for j in range(2):
            loads.append(
                pltpu.make_async_copy(src.at[:, pl.ds(6 * j, 2)], dst.at[j], sems.at[2 * j + i])
            )
    for load in loads:
        load.start()
    for j, out in ((1, bottom), (0, top)):
        loads[j].wait()
        loads[2 + j].wait()
        out[...] = (fbuf[j].astype(F32) + cbuf[j].astype(F32)).astype(BF)


def inner_kernel(
    step, frames, control, first, second, table, gain,
    keep, give, flat, edge, rim, wide1, wide2, vectors,
    column, tail, row, fbuf, cbuf, buf1, buf2, merged, taps1, taps2, prod, normed, sems,
):
    loads = [
        pltpu.make_async_copy(src, dst, sems.at[i])
        for i, (src, dst) in enumerate(
            ((frames, fbuf), (control, cbuf), (first, buf1), (second, buf2))
        )
    ]
    for load in loads[:3]:
        load.start()
    me = in_group()
    block = step[0] // 128
    whole_block = pltpu.make_async_copy(
        table.at[:, pl.ds(pl.multiple_of(jnp.minimum(block, 6) * 128, 128), 128)],
        column, sems.at[4],
    )
    last_block = pltpu.make_async_copy(
        table.at[:, pl.ds(896, 104)], tail, sems.at[4]
    )

    @pl.when(block < 7)
    def _():
        whole_block.start()
        whole_block.wait()
        row[...] = column[...].T

    @pl.when(block >= 7)
    def _():
        last_block.start()
        last_block.wait()
        row[0:104] = tail[...].T

    embed = row[pl.ds(step[0] % 128, 1), :]
    vectors[0:1] = embed
    vectors[1:2] = gain[...].reshape(1, 320)
    gain = vectors[1:2]
    loads[0].wait()
    loads[1].wait()
    loads[3].start()
    for m in range(8):
        for f in range(8):
            put(merged, m, f, fbuf[f, m].astype(F32) + cbuf[f, m].astype(F32))
        value = taken(merged, m).astype(BF)
        if m in (0, 1, 6, 7):
            rim[(0, 1, None, None, None, None, 2, 3)[m]] = value
        for dy in range(3):
            if 0 <= m - dy < 6:
                tapped(taps1, m - dy, dy, value)
    loads[2].wait()
    arrange(wide1, buf1)
    multiply(prod, taps1, wide1, 6)
    for r in range(6):
        act = silu(combine(prod, r) + embed).astype(BF)
        for dy in range(3):
            if 0 <= r - dy < 4:
                tapped(taps2, r - dy, dy, act)
        if r in (0, 1, 4, 5):
            edge[(0, 1, None, None, 2, 3)[r]] = act
    loads[3].wait()
    arrange(wide2, buf2)
    multiply(prod, taps2, wide2, 4)
    for y in range(4):
        value = combine(prod, y) + taken(merged, y + 2)
        flat[y] = value
        normed[y] = layer_norm(value, gain)
    hand_out(me, normed, keep, give)


def outer_kernel(
    low, high, rim, edge, wide1, wide2, vectors,
    keep, give, flat,
    merged, taps1, taps2, prod, normed,
):
    me = in_group()
    band = lax.axis_index("band")
    embed = vectors[0:1]
    gain = vectors[1:2]
    for f in range(8):
        for y in range(2):
            put(merged, y, f, low[f, y].astype(F32))
            put(merged, 2 + y, f, high[f, y].astype(F32))
    rows = [taken(merged, i).astype(BF) for i in range(4)]
    rows = [rows[0], rows[1], rim[0], rim[1], rim[2], rim[3], rows[2], rows[3]]
    starts = (0, 1, 4, 5)
    for m in range(8):
        for r in range(4):
            if 0 <= m - starts[r] < 3:
                tapped(taps1, r, m - starts[r], rows[m])
    multiply(prod, taps1, wide1, 4)
    act = [silu(combine(prod, r) + embed) for r in range(4)]
    act[0] = jnp.where(band == 0, 0.0, act[0])
    act[3] = jnp.where(band == lax.axis_size("band") - 1, 0.0, act[3])
    act = [a.astype(BF) for a in act]
    lines = ((act[0], act[1], edge[0], edge[1]), (edge[2], edge[3], act[2], act[3]))
    for side in range(2):
        for i in range(4):
            for dy in range(3):
                if 0 <= i - dy < 2:
                    tapped(taps2, 2 * side + i - dy, dy, lines[side][i])
    multiply(prod, taps2, wide2, 4)
    for y in range(4):
        value = combine(prod, y) + rim[y].astype(F32)
        flat[y] = value
        normed[y] = layer_norm(value, gain)
    hand_out(me, normed, keep, give)


def pack_kernel(keep, got, near, far):
    near[0] = keep[0]
    near[1] = got[0]
    far[0] = keep[1]
    far[1] = got[1]


def attend_kernel(
    reach, near, across_x, near_z, across_z, wq, wk, wv, w_out, rel_bias,
    out0, out1, out2, out3,
    weights, field, query, key, value, score, prob, back, bias, sems,
):
    loads = [
        pltpu.make_async_copy(w, weights.at[i], sems.at[i])
        for i, w in enumerate((wq, wk, wv, w_out))
    ]
    for load in loads:
        load.start()
    place = lax.axis_index("frame")
    me = place % GROUP
    pixels = field.shape[0]

    line = lax.broadcasted_iota(jnp.int32, (64, 128), 0)
    lane = lax.broadcasted_iota(jnp.int32, (64, 128), 1) % 32
    limit = jnp.zeros((1, 128), jnp.int32)
    for i in range(32):
        limit = jnp.where(lane[0:1] == i, reach[(place // GROUP) * 32 + i], limit)
    allowed = jnp.abs(line - 16 - lane) <= limit
    padded = jnp.concatenate([rel_bias[...], jnp.zeros((8, 95), F32)], axis=1)
    for half in range(2):
        table = []
        for h in range(4 * half, 4 * half + 4):
            wide = jnp.broadcast_to(padded[h : h + 1], (32, 128))
            table.append(pltpu.roll(wide, 0, 1, stride=1, stride_axis=0))
        table = jnp.concatenate(table, axis=0).T[0:64]
        bias[:, half * 128 : half * 128 + 128] = jnp.where(
            allowed, table * (1.0 / math.log(2.0)), -jnp.inf
        )

    for k in range(4):
        block = me ^ k
        own = (near, across_x)[k // 2]
        at = pl.multiple_of(16 + 8 * block, 8)
        field[:, pl.ds(at, 8), :] = own[k % 2].astype(F32).reshape(pixels, 8, 320)
        halo = (near_z, across_z)[k // 2]
        at = pl.multiple_of(jnp.where(block >= 2, 8 * block - 16, 48 + 8 * block), 8)
        field[:, pl.ds(at, 8), :] = halo[k % 2].astype(F32).reshape(pixels, 8, 320)
    for load in loads[:3]:
        load.wait()

    def project(x, i):
        return jnp.dot(x, weights[i], preferred_element_type=F32).astype(BF)

    x = field[...].reshape(pixels * 64, 320).astype(BF)
    key[...] = project(x, 1).reshape(pixels, 64, 320)
    value[...] = project(x, 2).reshape(pixels, 64, 320)
    x = field[:, 16:48, :].reshape(pixels * 32, 320).astype(BF)
    query[...] = project(x, 0).reshape(pixels, 32, 320)

    def heads_at(lanes, base):
        lane = lax.broadcasted_iota(jnp.int32, (4, 1, lanes), 2)
        first = base + 40 * lax.broadcasted_iota(jnp.int32, (4, 1, lanes), 0)
        return ((lane >= first) & (lane < first + 40)).astype(F32).astype(BF)

    spread_low = heads_at(256, 0)
    spread_high = heads_at(192, 32)
    scale = 40.0**-0.5 / math.log(2.0)
    across = (((1,), (1,)), ((), ()))

    def scores(p):
        q = query[p]
        k = key[p]
        low = (q[None, :, 0:256] * spread_low).reshape(128, 256)
        high = (q[None, :, 128:320] * spread_high).reshape(128, 192)
        score[p, :, 0:128] = lax.dot_general(
            k[:, 0:256], low, across, preferred_element_type=F32
        )
        score[p, :, 128:256] = lax.dot_general(
            k[:, 128:320], high, across, preferred_element_type=F32
        )

    def softmax(p):
        s = score[p] * scale + bias[...]
        e = jnp.exp2(s - jnp.max(s, axis=0, keepdims=True))
        prob[p] = (e * (1.0 / jnp.sum(e, axis=0, keepdims=True))).astype(BF)

    def inside(h, lanes, base):
        lane = lax.broadcasted_iota(jnp.int32, (1, lanes), 1) + base
        return (lane >= 40 * h) & (lane < 40 * h + 40)

    def attended(p):
        w = prob[p].T
        v = value[p]
        low = jnp.dot(w[0:128], v[:, 0:256], preferred_element_type=F32)
        high = jnp.dot(w[128:256], v[:, 128:320], preferred_element_type=F32)
        left = low[0:32, 0:128]
        for h in (1, 2, 3):
            left = jnp.where(inside(h, 128, 0), low[32 * h : 32 * h + 32, 0:128], left)
        middle = low[96:128, 128:256]
        for h in (4, 5, 6):
            at = 32 * h - 128
            middle = jnp.where(inside(h, 128, 128), high[at : at + 32, 0:128], middle)
        right = jnp.where(inside(7, 64, 256), high[96:128, 128:192], high[64:96, 128:192])
        att = jnp.concatenate([left, middle, right], axis=1)
        for b in range(4):
            back[b, p] = att[8 * b : 8 * b + 8]

    def each(step):
        def some(i, carry):
            for j in range(16):
                step(i * 16 + j)
            return carry

        lax.fori_loop(0, pixels // 16, some, 0)

    each(scores)
    each(softmax)
    each(attended)
    loads[3].wait()
    for k, out in enumerate((out0, out1, out2, out3)):
        out[...] = project(back[me ^ k].reshape(pixels * 8, 320).astype(BF), 3)


def final_kernel(first_row, second_row, *refs):
    a0, a1, a2, a3, flat = refs[:5]
    me = in_group()
    out, total, done, sems = refs[-4:]
    stores = []
    for k, a in enumerate((a0, a1, a2, a3)):
        q = me ^ k
        row = jnp.where(q >= 2, second_row + q - 2, first_row + q)
        value = a[...].astype(F32) + flat[q]
        rest = jnp.concatenate([value[:, 256:], jnp.zeros((128, 64), F32)], axis=1)
        for j, part in enumerate((value[:, :128], value[:, 128:256], rest)):
            total[k, j] = part
        for f in range(8):
            for j, width in enumerate((128, 128, 64)):
                part = total[k, j, pl.ds(f, 16, stride=8), :]
                done[k, f, :, j * 128 : j * 128 + width] = part[:, :width]
        store = pltpu.make_async_copy(done.at[k], out.at[:, row], sems.at[k])
        store.start()
        stores.append(store)
    for store in stores:
        store.wait()


def shards(
    frames, control, conv_first, conv_second, time_table, step_index, norm_gain,
    w_query, w_key, w_value, w_out, rel_bias, reach,
):
    count = lax.axis_size("frame")
    bands = lax.axis_size("band")
    planes = count // GROUP
    up = [(i, i + 1) for i in range(bands - 1)]
    down = [(i + 1, i) for i in range(bands - 1)]

    def plane(i, k):
        return (i & ~3) | ((i & 3) ^ k)

    def beside(i, k):
        turn = 1 if i & 2 else -1
        return (((i >> 2) + turn) % planes) * GROUP + ((i & 3) ^ k)

    def exchange(x, to, k):
        return lax.ppermute(x, "frame", [(i, to(i, k)) for i in range(count)])

    vmem = pl.BlockSpec(memory_space=pltpu.VMEM)
    smem = pl.BlockSpec(memory_space=pltpu.SMEM)
    anywhere = pl.BlockSpec(memory_space=pltpu.HBM)

    def params(mebibytes):
        return pltpu.CompilerParams(vmem_limit_bytes=mebibytes * MIB)
    pair = jax.ShapeDtypeStruct((2, 128, 320), BF)
    chunk = pltpu.VMEM((4, 128, 320), F32)
    wide = pltpu.VMEM((960, 960), BF)
    rows = pltpu.VMEM((4, 128, 320), BF)

    def cost(flops):
        return pl.CostEstimate(flops=flops, bytes_accessed=4_000_000, transcendentals=0)

    def stay(*arrays):
        return [pltpu.with_memory_space_constraint(x, pltpu.HBM) for x in arrays]

    def near_by(*arrays):
        return [pltpu.with_memory_space_constraint(x, pltpu.VMEM) for x in arrays]

    rows_scratch = [
        pltpu.VMEM((4, 128, 960), BF),
        pltpu.VMEM((768, 960), F32),
        pltpu.VMEM((4, 128, 320), BF),
    ]
    margin = jax.ShapeDtypeStruct((8, 2, 16, 320), BF)
    top, bottom = pl.pallas_call(
        edges_kernel,
        in_specs=[anywhere] * 2,
        out_specs=[vmem] * 2,
        out_shape=[margin] * 2,
        scratch_shapes=[
            pltpu.VMEM((2, 8, 2, 16, 320), BF),
            pltpu.VMEM((2, 8, 2, 16, 320), BF),
            pltpu.SemaphoreType.DMA((4,)),
        ],
        compiler_params=params(4),
        name="edges",
    )(*stay(frames, control))
    top, bottom, step_index = lax.optimization_barrier((top, bottom, step_index))
    low = lax.ppermute(bottom, "band", up)
    high = lax.ppermute(top, "band", down)

    keep, give, flat_in, edge, rim, wide1, wide2, vectors = pl.pallas_call(
        inner_kernel,
        in_specs=[smem] + [anywhere] * 5 + [vmem],
        out_specs=[vmem] * 8,
        out_shape=[pair, pair, chunk, rows, rows, wide, wide, pltpu.VMEM((2, 320), F32)],
        scratch_shapes=[
            pltpu.VMEM((320, 128), F32),
            pltpu.VMEM((320, 104), F32),
            pltpu.VMEM((128, 320), F32),
            pltpu.VMEM((8, 8, 16, 320), BF),
            pltpu.VMEM((8, 8, 16, 320), BF),
            pltpu.VMEM((3, 3, 320, 320), BF),
            pltpu.VMEM((3, 3, 320, 320), BF),
            pltpu.VMEM((3, 8, 128, 128), F32),
            pltpu.VMEM((6, 128, 960), BF),
        ]
        + rows_scratch
        + [pltpu.SemaphoreType.DMA((5,))],
        compiler_params=params(22),
        name="inner_rows",
    )(step_index, *stay(frames, control, conv_first, conv_second, time_table.T), norm_gain)

    keep, give, low, high = lax.optimization_barrier((keep, give, low, high))

    def packed(keep, give):
        got = exchange(give, plane, 1)
        return pl.pallas_call(
            pack_kernel,
            in_specs=[vmem] * 2,
            out_specs=[vmem] * 2,
            out_shape=[pair] * 2,
            compiler_params=params(2),
            name="pack",
        )(keep, got)

    def onward(i, k):
        turn = 1 if (i ^ 2) & 2 else -1
        return (((i >> 2) + turn) % planes) * GROUP + (i & 3)

    near_in, far = packed(keep, give)
    x_in = exchange(far, plane, 2)
    z_in = exchange(near_in, beside, 0)
    near_in, edge = lax.optimization_barrier((near_in, edge))

    keep, give, flat_out = pl.pallas_call(
        outer_kernel,
        in_specs=[vmem] * 7,
        out_specs=[vmem] * 3,
        out_shape=[pair, pair, chunk],
        scratch_shapes=[
            pltpu.VMEM((3, 4, 128, 128), F32),
            pltpu.VMEM((4, 128, 960), BF),
        ]
        + rows_scratch,
        compiler_params=params(12),
        name="outer_rows",
    )(low, high, *near_by(rim, edge, wide1, wide2, vectors))

    give, x_in, z_in = lax.optimization_barrier((give, x_in, z_in))
    xz_in = exchange(x_in, onward, 0)
    near_out, far = packed(keep, give)
    x_out = exchange(far, plane, 2)
    xz_out = exchange(far, beside, 2)
    z_out = exchange(near_out, beside, 0)

    def attend(fields):
        piece = jax.ShapeDtypeStruct((128, 320), BF)
        outs = pl.pallas_call(
            attend_kernel,
            in_specs=[smem] + [vmem] * 4 + [anywhere] * 4 + [vmem],
            out_specs=[vmem] * 4,
            out_shape=[piece] * 4,
            scratch_shapes=[
                pltpu.VMEM((4, 320, 320), BF),
                pltpu.VMEM((16, 64, 320), F32),
                pltpu.VMEM((16, 32, 320), BF),
                pltpu.VMEM((16, 64, 320), BF),
                pltpu.VMEM((16, 64, 320), BF),
                pltpu.VMEM((16, 64, 256), F32),
                pltpu.VMEM((16, 64, 256), BF),
                pltpu.VMEM((4, 16, 8, 320), F32),
                pltpu.VMEM((64, 256), F32),
                pltpu.SemaphoreType.DMA((4,)),
            ],
            compiler_params=params(14),
            name="attend",
        )(reach, *fields, *stay(w_query, w_key, w_value, w_out), rel_bias)
        return [outs[0]] + [exchange(outs[k], plane, k) for k in (2, 3, 1)], outs[0]

    near_out, near_in = lax.optimization_barrier((near_out, near_in))
    (b0, b2, b3, b1), _ = attend((near_in, x_in, z_in, xz_in))
    back_in = [b0, b1, b2, b3]
    (b0, b2, b3, b1), mark = attend((near_out, x_out, z_out, xz_out))
    back_out = [b0, b1, b2, b3]

    def finish(first_row, second_row, back, flat, *before):
        def body(*refs):
            final_kernel(first_row, second_row, *refs)

        return pl.pallas_call(
            body,
            in_specs=[vmem] * 5 + [anywhere] * len(before),
            out_specs=anywhere,
            out_shape=jax.ShapeDtypeStruct(frames.shape, F32),
            input_output_aliases={5: 0} if before else {},
            scratch_shapes=[
                pltpu.VMEM((4, 3, 128, 128), F32),
                pltpu.VMEM((4, 8, 16, 320), F32),
                pltpu.SemaphoreType.DMA((4,)),
            ],
            compiler_params=params(6),
            name="project_out",
        )(*back, *near_by(flat), *before)

    back_in[0], mark = lax.optimization_barrier((back_in[0], mark))
    out = finish(2, 4, back_in, flat_in)
    return finish(0, 6, back_out, flat_out, out)


def solution(mesh):
    tiled = P("frame", "band", None, None)
    return jax.shard_map(
        shards, mesh=mesh, in_specs=(tiled, tiled) + (P(),) * 11, out_specs=tiled, check_vma=False
    )
```

time: 81.1 us -> 66.4 us (0.82)
  waiting for transfers between devices: 23.6 us -> 9.26 us
  local copies, waits for them, and re-layouts: 9.87 us -> 0.68 us
  starting transfers between devices: 24.6 us -> 31.8 us
  Pallas kernels: 19.1 us -> 23.5 us
  other arithmetic: 2.35 us -> 0 us
    ppermute x12 -> x16, waiting for transfers between devices: 23.6 us -> 9.26 us  [the longest x14 9.25 us: exchange(): return lax.ppermute(x, 'frame', [(i, to(i, k)) for i in range(count)])]
    unnamed x37 -> x6, local copies, waits for them, and re-layouts: 8.01 us -> 0.68 us
    ppermute x12 -> x16, starting transfers between devices: 24.6 us -> 31.8 us  [the longest x14 24.4 us: exchange(): return lax.ppermute(x, 'frame', [(i, to(i, k)) for i in range(count)])]
    pallas_call x3 -> x9, Pallas kernels: 19.1 us -> 23.5 us  [the longest x2 9.71 us: attend(): pl.pallas_call(attend_kernel, in_specs=[smem] + [vmem] * 4 + [anywhere] *...]
    convert_element_type x1 -> x0, other arithmetic: 2.2 us -> none  [edge(): (frames[:, rows].astype(F32) + control[:, rows].astype(F32)).astype(BF)]
    reshape x1 -> x0, local copies, waits for them, and re-layouts: 0.98 us -> none  [shards(): jnp.where(allowed[None], bias * (1.0 / math.log(2.0)), -jnp.inf)]
  transfers between devices with their start and end apart: 12 -> 16, of which waited for: 8 -> 7; matrix products, arithmetic and copies ran while one was open for 3% -> 0% of each run, Pallas kernels for 0% -> 32%
where the time goes in v3:
time: 66.4 us; the launch traced here: 66.1 us
  starting transfers between devices  31.8 us (48%)
  Pallas kernels  23.5 us (35%)
  waiting for transfers between devices  9.26 us (14%)
  between operations  0.93 us (1%)
  local copies, waits for them, and re-layouts  0.68 us (1%)
    ppermute x14, starting transfers between devices, exchange(): return lax.ppermute(x, 'frame', [(i, to(i, k)) for i in range(count)])  24.4 us
    pallas_call x2, Pallas kernels, attend(): pl.pallas_call(attend_kernel, in_specs=[smem] + [vmem] * 4 + [anywhere] *...  9.71 us
    ppermute x14, waiting for transfers between devices, exchange(): return lax.ppermute(x, 'frame', [(i, to(i, k)) for i in range(count)])  9.25 us
    pallas_call x1, Pallas kernels, shards(): pl.pallas_call(inner_kernel, in_specs=[smem] + [anywhere] * 5 + [vmem], o...  7.11 us
    ppermute x1, starting transfers between devices, shards(): high = lax.ppermute(top, 'band', down)  4.19 us
    pallas_call x1, Pallas kernels, shards(): pl.pallas_call(outer_kernel, in_specs=[vmem] * 7, out_specs=[vmem] * 3, o...  3.28 us
    ppermute x1, starting transfers between devices, shards(): low = lax.ppermute(bottom, 'band', up)  3.2 us
    pallas_call x2, Pallas kernels, finish(): pl.pallas_call(body, in_specs=[vmem] * 5 + [anywhere] * len(before), out_...  1.94 us
  transfers between devices with their start and end apart: 16, of which 7 were waited for; matrix products, arithmetic and copies ran while one was open for 0% of the time, Pallas kernels for 32%

profile of v3, /device:TPU:3, one launch (start us, length us, event | category | flops | bytes accessed | tf_op | source)
XLA Modules:
  0.0 66.1 jit_solution(5484135656590217014)
XLA Ops:
  0.0 1.4 %edges.1 = (bf16[8,2,16,320]{3,2,1,0:T(8,128)(2,1)S(1)}, bf16[8,2,16,320]{3,2,1,0:T(8,128)(2,1)S(1)}) custom-call(bf16[8,8,16,320]{3,2,1,0:T(8,128)(2,1)} %frames.3, bf16[8,8,16,320]{3,2,1,0:T(8,128)(2,1)} %control.3), custom_call_target="tpu_custom_call" | custom-call | tf_op jit(solution)/shard_map/edges/pallas_call | solution.py:407
  1.4 3.2 %collective-permute-start = (bf16[8,2,16,320]{3,2,1,0:T(8,128)(2,1)S(1)}, bf16[8,2,16,320]{3,2,1,0:T(8,128)(2,1)S(1)}, u32[]{:S(2)}, u32[]{:S(2)}) collective-permute-start(bf16[8,2,16,320]{3,2,1,0:T(8,128)(2,1)S(1)} %get-tuple-element.50), channel_id=1, source_target_pairs={{0,1},{1,2},{2,3},{3,4},{4,5},{5,6},{6,7},{8,9},{9,10},{10,11},{11... | collective-permute-start | bytes 491528 | tf_op jit(solution)/shard_map/ppermute | solution.py:421
  4.6 4.2 %collective-permute-start.1 = (bf16[8,2,16,320]{3,2,1,0:T(8,128)(2,1)S(1)}, bf16[8,2,16,320]{3,2,1,0:T(8,128)(2,1)S(1)}, u32[]{:S(2)}, u32[]{:S(2)}) collective-permute-start(bf16[8,2,16,320]{3,2,1,0:T(8,128)(2,1)S(1)} %get-tuple-element.51), channel_id=1, source_target_pairs={{1,0},{2,1},{3,2},{4,3},{5,4},{6,5},{7,6},{9,8},{10,9},{11,10},{12... | collective-permute-start | bytes 491528 | tf_op jit(solution)/shard_map/ppermute | solution.py:422
  9.4 0.0 copy-start.2
  9.4 0.7 %copy-done.2 = f32[320]{0:T(512)S(1)} copy-done((f32[320]{0:T(512)S(1)}, f32[320]{0:T(512)}, u32[]{:S(2)}) %copy-start.2) | copy-done | bytes 1304
  10.1 7.1 %inner_rows.1 = (bf16[2,128,320]{2,1,0:T(8,128)(2,1)S(1)}, bf16[2,128,320]{2,1,0:T(8,128)(2,1)S(1)}, f32[4,128,320]{2,1,0:T(8,128)S(1)}, bf16[4,128,320]{2,1,0:T...) custom-call(s32[1]{0:T(128)S(6)} %copy.16.step, ...), custom_call_target="tpu_custom_call" | custom-call | tf_op jit(solution)/shard_map/inner_rows/pallas_call | solution.py:424
  17.2 0.0 collective-permute-done.low
  17.2 0.0 collective-permute-done.1.high
  17.2 1.3 %collective-permute-start.2 = (bf16[2,128,320]{2,1,0:T(8,128)(2,1)S(1)}, bf16[2,128,320]{2,1,0:T(8,128)(2,1)S(1)}, u32[]{:S(2)}, u32[]{:S(2)}) collective-permute-start(bf16[2,128,320]{2,1,0:T(8,128)(2,1)S(1)} %get-tuple-element.56), channel_id=1, source_target_pairs={{0,8},{8,0},{16,24},{24,16},{32,40},{40,32},{48,56},{56,48},{64,72... | collective-permute-start | bytes 491528 | tf_op jit(solution)/shard_map/ppermute | solution.py:379
  18.6 1.1 %collective-permute-done.2.got = bf16[2,128,320]{2,1,0:T(8,128)(2,1)S(1)} collective-permute-done((bf16[2,128,320]{2,1,0:T(8,128)(2,1)S(1)}, bf16[2,128,320]{2,1,0:T(8,128)(2,1)S(1)}, u32[]{:S(2)}, u32[]{:S(2)}) %collective-permute-start.2) | collective-permute-done | bytes 163872 | tf_op jit(solution)/shard_map/ppermute | solution.py:379
  19.7 1.9 %collective-permute-start.3 = (bf16[2,128,320]{2,1,0:T(8,128)(2,1)S(1)}, bf16[2,128,320]{2,1,0:T(8,128)(2,1)S(1)}, u32[]{:S(2)}, u32[]{:S(2)}) collective-permute-start(bf16[2,128,320]{2,1,0:T(8,128)(2,1)S(1)} %get-tuple-element.65), channel_id=1, source_target_pairs={{0,16},{8,24},{16,0},{24,8},{32,48},{40,56},{48,32},{56,40},{64,80... | collective-permute-start | bytes 491528 | tf_op jit(solution)/shard_map/ppermute | solution.py:379
  21.6 5.6 %collective-permute-start.4 = (bf16[2,128,320]{2,1,0:T(8,128)(2,1)S(1)}, bf16[2,128,320]{2,1,0:T(8,128)(2,1)S(1)}, u32[]{:S(2)}, u32[]{:S(2)}) collective-permute-start(bf16[2,128,320]{2,1,0:T(8,128)(2,1)S(1)} %get-tuple-element.76.near), channel_id=1, source_target_pairs={{0,224},{8,232},{16,48},{24,56},{32,0},{40,8},{48,80},{56,88},{64,... | collective-permute-start | bytes 491528 | tf_op jit(solution)/shard_map/ppermute | solution.py:379
  27.2 0.0 copy-start
  27.2 0.0 copy-start.1
  27.2 3.3 %outer_rows.1 = (bf16[2,128,320]{2,1,0:T(8,128)(2,1)S(1)}, bf16[2,128,320]{2,1,0:T(8,128)(2,1)S(1)}, f32[4,128,320]{2,1,0:T(8,128)S(1)}) custom-call(bf16[8,2,16,320]{3,2,1,0:T(8,128)(2,1)S(1)} %collective-permute-done.low, bf16[8,2,16,320]{3,2,1,0:T(8,128)(2,1)S(1)} %collective-permute-done.1.high, bf16[4,128,320]{2,1,0:T(8,128)(2,1)S(1)} %get-tuple-element.54.rim, ...), custom_call_target="tpu_custom_call" | custom-call | tf_op jit(solution)/shard_map/outer_rows/pallas_call | solution.py:468
  30.5 0.0 collective-permute-done.3.across_x
  30.5 0.3 collective-permute-done.4.near_z
  30.8 1.5 %collective-permute-start.5 = (bf16[2,128,320]{2,1,0:T(8,128)(2,1)S(1)}, bf16[2,128,320]{2,1,0:T(8,128)(2,1)S(1)}, u32[]{:S(2)}, u32[]{:S(2)}) collective-permute-start(bf16[2,128,320]{2,1,0:T(8,128)(2,1)S(1)} %get-tuple-element.66), channel_id=1, source_target_pairs={{0,8},{8,0},{16,24},{24,16},{32,40},{40,32},{48,56},{56,48},{64,72... | collective-permute-start | bytes 491528 | tf_op jit(solution)/shard_map/ppermute | solution.py:379
  32.3 0.0 collective-permute-start.12
  32.3 1.1 %collective-permute-done.5.got = bf16[2,128,320]{2,1,0:T(8,128)(2,1)S(1)} collective-permute-done((bf16[2,128,320]{2,1,0:T(8,128)(2,1)S(1)}, bf16[2,128,320]{2,1,0:T(8,128)(2,1)S(1)}, u32[]{:S(2)}, u32[]{:S(2)}) %collective-permute-start.5) | collective-permute-done | bytes 163872 | tf_op jit(solution)/shard_map/ppermute | solution.py:379
  33.4 3.5 %collective-permute-start.7 = (bf16[2,128,320]{2,1,0:T(8,128)(2,1)S(1)}, bf16[2,128,320]{2,1,0:T(8,128)(2,1)S(1)}, u32[]{:S(2)}, u32[]{:S(2)}) collective-permute-start(bf16[2,128,320]{2,1,0:T(8,128)(2,1)S(1)} %get-tuple-element.69.near), channel_id=1, source_target_pairs={{0,224},{8,232},{16,48},{24,56},{32,0},{40,8},{48,80},{56,88},{64,... | collective-permute-start | bytes 491528 | tf_op jit(solution)/shard_map/ppermute | solution.py:379
  36.9 1.6 %collective-permute-start.8 = (bf16[2,128,320]{2,1,0:T(8,128)(2,1)S(1)}, bf16[2,128,320]{2,1,0:T(8,128)(2,1)S(1)}, u32[]{:S(2)}, u32[]{:S(2)}) collective-permute-start(bf16[2,128,320]{2,1,0:T(8,128)(2,1)S(1)} %get-tuple-element.70), channel_id=1, source_target_pairs={{0,240},{8,248},{16,32},{24,40},{32,16},{40,24},{48,64},{56,72},{6... | collective-permute-start | bytes 491528 | tf_op jit(solution)/shard_map/ppermute | solution.py:379
  38.5 0.0 collective-permute-start.6
  38.5 2.5 %collective-permute-done.12.across_z = bf16[2,128,320]{2,1,0:T(8,128)(2,1)S(1)} collective-permute-done((bf16[2,128,320]{2,1,0:T(8,128)(2,1)S(1)}, bf16[2,128,320]{2,1,0:T(8,128)(2,1)S(1)}, u32[]{:S(2)}, u32[]{:S(2)}) %collective-permute-start.12) | collective-permute-done | bytes 163872 | tf_op jit(solution)/shard_map/ppermute | solution.py:379
  41.0 0.0 copy-done
  41.0 0.0 copy-done.1
  41.0 4.9 %attend.3 = (bf16[128,320]{1,0:T(8,128)(2,1)S(1)}, bf16[128,320]{1,0:T(8,128)(2,1)S(1)}, bf16[128,320]{1,0:T(8,128)(2,1)S(1)}, bf16[128,320]{1,0:T(8,128)(2,1)S(1)}) custom-call(s32[256]{0:T(256)S(1)} %copy-done.1, bf16[2,128,320]{2,1,0:T(8,128)(2,1)S(1)} %get-tuple-element.76.near, bf16[2,128,320]{2,1,0:T(8,128)(2,1)S(1)} %collective-permute-done.3.across_x, ...), custom_call_target="tpu_custom_call" | custom-call | tf_op jit(solution)/shard_map/attend/pallas_call | solution.py:491
  45.9 0.7 %collective-permute-start.13 = (bf16[128,320]{1,0:T(8,128)(2,1)S(1)}, bf16[128,320]{1,0:T(8,128)(2,1)S(1)}, u32[]{:S(2)}, u32[]{:S(2)}) collective-permute-start(bf16[128,320]{1,0:T(8,128)(2,1)S(1)} %get-tuple-element.81), channel_id=1, source_target_pairs={{0,8},{8,0},{16,24},{24,16},{32,40},{40,32},{48,56},{56,48},{64,72... | collective-permute-start | bytes 245768 | tf_op jit(solution)/shard_map/ppermute | solution.py:379
  46.5 1.1 %collective-permute-start.14 = (bf16[128,320]{1,0:T(8,128)(2,1)S(1)}, bf16[128,320]{1,0:T(8,128)(2,1)S(1)}, u32[]{:S(2)}, u32[]{:S(2)}) collective-permute-start(bf16[128,320]{1,0:T(8,128)(2,1)S(1)} %get-tuple-element.82), channel_id=1, source_target_pairs={{0,16},{8,24},{16,0},{24,8},{32,48},{40,56},{48,32},{56,40},{64,80... | collective-permute-start | bytes 245768 | tf_op jit(solution)/shard_map/ppermute | solution.py:379
  47.6 0.0 collective-permute-done.7.near_z
  47.6 2.2 %collective-permute-start.15 = (bf16[128,320]{1,0:T(8,128)(2,1)S(1)}, bf16[128,320]{1,0:T(8,128)(2,1)S(1)}, u32[]{:S(2)}, u32[]{:S(2)}) collective-permute-start(bf16[128,320]{1,0:T(8,128)(2,1)S(1)} %get-tuple-element.83), channel_id=1, source_target_pairs={{0,24},{8,16},{16,8},{24,0},{32,56},{40,48},{48,40},{56,32},{64,88... | collective-permute-start | bytes 245768 | tf_op jit(solution)/shard_map/ppermute | solution.py:379
  49.8 0.0 collective-permute-done.8.across_z
  49.8 0.4 collective-permute-done.6.across_x
  50.2 4.9 %attend.2 = (bf16[128,320]{1,0:T(8,128)(2,1)S(1)}, bf16[128,320]{1,0:T(8,128)(2,1)S(1)}, bf16[128,320]{1,0:T(8,128)(2,1)S(1)}, bf16[128,320]{1,0:T(8,128)(2,1)S(1)}) custom-call(s32[256]{0:T(256)S(1)} %copy-done.1, bf16[2,128,320]{2,1,0:T(8,128)(2,1)S(1)} %get-tuple-element.69.near, bf16[2,128,320]{2,1,0:T(8,128)(2,1)S(1)} %collective-permute-done.6.across_x, ...), custom_call_target="tpu_custom_call" | custom-call | tf_op jit(solution)/shard_map/attend/pallas_call | solution.py:491
  55.1 1.8 %collective-permute-start.9 = (bf16[128,320]{1,0:T(8,128)(2,1)S(1)}, bf16[128,320]{1,0:T(8,128)(2,1)S(1)}, u32[]{:S(2)}, u32[]{:S(2)}) collective-permute-start(bf16[128,320]{1,0:T(8,128)(2,1)S(1)} %get-tuple-element.72), channel_id=1, source_target_pairs={{0,8},{8,0},{16,24},{24,16},{32,40},{40,32},{48,56},{56,48},{64,72... | collective-permute-start | bytes 245768 | tf_op jit(solution)/shard_map/ppermute | solution.py:379
  56.9 0.0 collective-permute-start.10
  56.9 0.0 collective-permute-done.13.refs_1_
  56.9 3.2 %collective-permute-start.11 = (bf16[128,320]{1,0:T(8,128)(2,1)S(1)}, bf16[128,320]{1,0:T(8,128)(2,1)S(1)}, u32[]{:S(2)}, u32[]{:S(2)}) collective-permute-start(bf16[128,320]{1,0:T(8,128)(2,1)S(1)} %get-tuple-element.74), channel_id=1, source_target_pairs={{0,24},{8,16},{16,8},{24,0},{32,56},{40,48},{48,40},{56,32},{64,88... | collective-permute-start | bytes 245768 | tf_op jit(solution)/shard_map/ppermute | solution.py:379
  60.1 0.0 collective-permute-done.14.refs_2_
  60.1 0.0 collective-permute-done.15.refs_3_
  60.1 1.0 %project_out.2.refs_5_ = f32[8,8,16,320]{3,2,1,0:T(8,128)} custom-call(bf16[128,320]{1,0:T(8,128)(2,1)S(1)} %get-tuple-element.80.refs_0_, bf16[128,320]{1,0:T(8,128)(2,1)S(1)} %collective-permute-done.13.refs_1_, bf16[128,320]{1,0:T(8,128)(2,1)S(1)} %collective-permute-done.14.refs_2_, bf16[128,320]{1,0:T(8,128)(2,1)S(1)} %collective-permute-done.15.refs_3_, ...), custom_call_target="tpu_custom_call" | custom-call | tf_op jit(solution)/shard_map/project_out/pallas_call | solution.py:523
  61.1 0.0 collective-permute-done.9.refs_1_
  61.1 1.6 %collective-permute-done.10.refs_2_ = bf16[128,320]{1,0:T(8,128)(2,1)S(1)} collective-permute-done((bf16[128,320]{1,0:T(8,128)(2,1)S(1)}, bf16[128,320]{1,0:T(8,128)(2,1)S(1)}, u32[]{:S(2)}, u32[]{:S(2)}) %collective-permute-start.10) | collective-permute-done | bytes 81952 | tf_op jit(solution)/shard_map/ppermute | solution.py:379
  62.7 2.3 %collective-permute-done.11.refs_3_ = bf16[128,320]{1,0:T(8,128)(2,1)S(1)} collective-permute-done((bf16[128,320]{1,0:T(8,128)(2,1)S(1)}, bf16[128,320]{1,0:T(8,128)(2,1)S(1)}, u32[]{:S(2)}, u32[]{:S(2)}) %collective-permute-start.11) | collective-permute-done | bytes 81952 | tf_op jit(solution)/shard_map/ppermute | solution.py:379
  65.0 1.0 %project_out.3 = f32[8,8,16,320]{3,2,1,0:T(8,128)} custom-call(bf16[128,320]{1,0:T(8,128)(2,1)S(1)} %get-tuple-element.71.refs_0_, bf16[128,320]{1,0:T(8,128)(2,1)S(1)} %collective-permute-done.9.refs_1_, bf16[128,320]{1,0:T(8,128)(2,1)S(1)} %collective-permute-done.10.refs_2_, ...), custom_call_target="tpu_custom_call", output_to_operand_aliasing={{}: (5, {})} | custom-call | tf_op jit(solution)/shard_map/project_out/pallas_call | solution.py:523
  (2 shorter events, 0.1 us)
Async XLA Ops:
  1.4 15.9 %collective-permute-start = (bf16[8,2,16,320]{3,2,1,0:T(8,128)(2,1)S(1)}, bf16[8,2,16,320]{3,2,1,0:T(8,128)(2,1)S(1)}, u32[]{:S(2)}, u32[]{:S(2)}) collective-permute-start(bf16[8,2,16,320]{3,2,1,0:T(8,128)(2,1)S(1)} %get-tuple-element.50), channel_id=1, source_target_pairs={{0,1},{1,2},{2,3},{3,4},{4,5},{5,6},{6,7},{8,9},{9,10},{10,11},{11... | collective-permute-start | bytes 491528 | tf_op jit(solution)/shard_map/ppermute | solution.py:421
  4.6 12.7 %collective-permute-start.1 = (bf16[8,2,16,320]{3,2,1,0:T(8,128)(2,1)S(1)}, bf16[8,2,16,320]{3,2,1,0:T(8,128)(2,1)S(1)}, u32[]{:S(2)}, u32[]{:S(2)}) collective-permute-start(bf16[8,2,16,320]{3,2,1,0:T(8,128)(2,1)S(1)} %get-tuple-element.51), channel_id=1, source_target_pairs={{1,0},{2,1},{3,2},{4,3},{5,4},{6,5},{7,6},{9,8},{10,9},{11,10},{12... | collective-permute-start | bytes 491528 | tf_op jit(solution)/shard_map/ppermute | solution.py:422
  9.4 0.7 %copy-start.2 = (f32[320]{0:T(512)S(1)}, f32[320]{0:T(512)}, u32[]{:S(2)}) copy-start(f32[320]{0:T(512)} %gain.1) | copy-start | bytes 3844
  17.2 2.4 %collective-permute-start.2 = (bf16[2,128,320]{2,1,0:T(8,128)(2,1)S(1)}, bf16[2,128,320]{2,1,0:T(8,128)(2,1)S(1)}, u32[]{:S(2)}, u32[]{:S(2)}) collective-permute-start(bf16[2,128,320]{2,1,0:T(8,128)(2,1)S(1)} %get-tuple-element.56), channel_id=1, source_target_pairs={{0,8},{8,0},{16,24},{24,16},{32,40},{40,32},{48,56},{56,48},{64,72... | collective-permute-start | bytes 491528 | tf_op jit(solution)/shard_map/ppermute | solution.py:379
  19.7 10.8 %collective-permute-start.3 = (bf16[2,128,320]{2,1,0:T(8,128)(2,1)S(1)}, bf16[2,128,320]{2,1,0:T(8,128)(2,1)S(1)}, u32[]{:S(2)}, u32[]{:S(2)}) collective-permute-start(bf16[2,128,320]{2,1,0:T(8,128)(2,1)S(1)} %get-tuple-element.65), channel_id=1, source_target_pairs={{0,16},{8,24},{16,0},{24,8},{32,48},{40,56},{48,32},{56,40},{64,80... | collective-permute-start | bytes 491528 | tf_op jit(solution)/shard_map/ppermute | solution.py:379
  21.6 9.2 %collective-permute-start.4 = (bf16[2,128,320]{2,1,0:T(8,128)(2,1)S(1)}, bf16[2,128,320]{2,1,0:T(8,128)(2,1)S(1)}, u32[]{:S(2)}, u32[]{:S(2)}) collective-permute-start(bf16[2,128,320]{2,1,0:T(8,128)(2,1)S(1)} %get-tuple-element.76.near), channel_id=1, source_target_pairs={{0,224},{8,232},{16,48},{24,56},{32,0},{40,8},{48,80},{56,88},{64,... | collective-permute-start | bytes 491528 | tf_op jit(solution)/shard_map/ppermute | solution.py:379
  27.2 13.8 %copy-start = (f32[8,33]{1,0:T(8,128)S(1)}, f32[8,33]{1,0:T(8,128)}, u32[]{:S(2)}) copy-start(f32[8,33]{1,0:T(8,128)} %rel_bias.3) | copy-start | bytes 3172
  27.2 13.8 %copy-start.1 = (s32[256]{0:T(256)S(1)}, s32[256]{0:T(256)}, u32[]{:S(2)}) copy-start(s32[256]{0:T(256)} %reach.3) | copy-start | bytes 3076
  30.8 2.6 %collective-permute-start.5 = (bf16[2,128,320]{2,1,0:T(8,128)(2,1)S(1)}, bf16[2,128,320]{2,1,0:T(8,128)(2,1)S(1)}, u32[]{:S(2)}, u32[]{:S(2)}) collective-permute-start(bf16[2,128,320]{2,1,0:T(8,128)(2,1)S(1)} %get-tuple-element.66), channel_id=1, source_target_pairs={{0,8},{8,0},{16,24},{24,16},{32,40},{40,32},{48,56},{56,48},{64,72... | collective-permute-start | bytes 491528 | tf_op jit(solution)/shard_map/ppermute | solution.py:379
  32.3 8.7 %collective-permute-start.12 = (bf16[2,128,320]{2,1,0:T(8,128)(2,1)S(1)}, bf16[2,128,320]{2,1,0:T(8,128)(2,1)S(1)}, u32[]{:S(2)}, u32[]{:S(2)}) collective-permute-start(bf16[2,128,320]{2,1,0:T(8,128)(2,1)S(1)} %collective-permute-done.3.across_x), channel_id=1, source_target_pairs={{0,32},{8,40},{16,240},{24,248},{32,64},{40,72},{48,16},{56,24},{6... | collective-permute-start | bytes 491528 | tf_op jit(solution)/shard_map/ppermute | solution.py:379
  33.4 14.2 %collective-permute-start.7 = (bf16[2,128,320]{2,1,0:T(8,128)(2,1)S(1)}, bf16[2,128,320]{2,1,0:T(8,128)(2,1)S(1)}, u32[]{:S(2)}, u32[]{:S(2)}) collective-permute-start(bf16[2,128,320]{2,1,0:T(8,128)(2,1)S(1)} %get-tuple-element.69.near), channel_id=1, source_target_pairs={{0,224},{8,232},{16,48},{24,56},{32,0},{40,8},{48,80},{56,88},{64,... | collective-permute-start | bytes 491528 | tf_op jit(solution)/shard_map/ppermute | solution.py:379
  36.9 12.9 %collective-permute-start.8 = (bf16[2,128,320]{2,1,0:T(8,128)(2,1)S(1)}, bf16[2,128,320]{2,1,0:T(8,128)(2,1)S(1)}, u32[]{:S(2)}, u32[]{:S(2)}) collective-permute-start(bf16[2,128,320]{2,1,0:T(8,128)(2,1)S(1)} %get-tuple-element.70), channel_id=1, source_target_pairs={{0,240},{8,248},{16,32},{24,40},{32,16},{40,24},{48,64},{56,72},{6... | collective-permute-start | bytes 491528 | tf_op jit(solution)/shard_map/ppermute | solution.py:379
  38.5 11.7 %collective-permute-start.6 = (bf16[2,128,320]{2,1,0:T(8,128)(2,1)S(1)}, bf16[2,128,320]{2,1,0:T(8,128)(2,1)S(1)}, u32[]{:S(2)}, u32[]{:S(2)}) collective-permute-start(bf16[2,128,320]{2,1,0:T(8,128)(2,1)S(1)} %get-tuple-element.70), channel_id=1, source_target_pairs={{0,16},{8,24},{16,0},{24,8},{32,48},{40,56},{48,32},{56,40},{64,80... | collective-permute-start | bytes 491528 | tf_op jit(solution)/shard_map/ppermute | solution.py:379
  45.9 11.0 %collective-permute-start.13 = (bf16[128,320]{1,0:T(8,128)(2,1)S(1)}, bf16[128,320]{1,0:T(8,128)(2,1)S(1)}, u32[]{:S(2)}, u32[]{:S(2)}) collective-permute-start(bf16[128,320]{1,0:T(8,128)(2,1)S(1)} %get-tuple-element.81), channel_id=1, source_target_pairs={{0,8},{8,0},{16,24},{24,16},{32,40},{40,32},{48,56},{56,48},{64,72... | collective-permute-start | bytes 245768 | tf_op jit(solution)/shard_map/ppermute | solution.py:379
  46.5 13.6 %collective-permute-start.14 = (bf16[128,320]{1,0:T(8,128)(2,1)S(1)}, bf16[128,320]{1,0:T(8,128)(2,1)S(1)}, u32[]{:S(2)}, u32[]{:S(2)}) collective-permute-start(bf16[128,320]{1,0:T(8,128)(2,1)S(1)} %get-tuple-element.82), channel_id=1, source_target_pairs={{0,16},{8,24},{16,0},{24,8},{32,48},{40,56},{48,32},{56,40},{64,80... | collective-permute-start | bytes 245768 | tf_op jit(solution)/shard_map/ppermute | solution.py:379
  47.6 12.5 %collective-permute-start.15 = (bf16[128,320]{1,0:T(8,128)(2,1)S(1)}, bf16[128,320]{1,0:T(8,128)(2,1)S(1)}, u32[]{:S(2)}, u32[]{:S(2)}) collective-permute-start(bf16[128,320]{1,0:T(8,128)(2,1)S(1)} %get-tuple-element.83), channel_id=1, source_target_pairs={{0,24},{8,16},{16,8},{24,0},{32,56},{40,48},{48,40},{56,32},{64,88... | collective-permute-start | bytes 245768 | tf_op jit(solution)/shard_map/ppermute | solution.py:379
  55.1 6.0 %collective-permute-start.9 = (bf16[128,320]{1,0:T(8,128)(2,1)S(1)}, bf16[128,320]{1,0:T(8,128)(2,1)S(1)}, u32[]{:S(2)}, u32[]{:S(2)}) collective-permute-start(bf16[128,320]{1,0:T(8,128)(2,1)S(1)} %get-tuple-element.72), channel_id=1, source_target_pairs={{0,8},{8,0},{16,24},{24,16},{32,40},{40,32},{48,56},{56,48},{64,72... | collective-permute-start | bytes 245768 | tf_op jit(solution)/shard_map/ppermute | solution.py:379
  56.9 5.9 %collective-permute-start.10 = (bf16[128,320]{1,0:T(8,128)(2,1)S(1)}, bf16[128,320]{1,0:T(8,128)(2,1)S(1)}, u32[]{:S(2)}, u32[]{:S(2)}) collective-permute-start(bf16[128,320]{1,0:T(8,128)(2,1)S(1)} %get-tuple-element.73), channel_id=1, source_target_pairs={{0,16},{8,24},{16,0},{24,8},{32,48},{40,56},{48,32},{56,40},{64,80... | collective-permute-start | bytes 245768 | tf_op jit(solution)/shard_map/ppermute | solution.py:379
  56.9 8.1 %collective-permute-start.11 = (bf16[128,320]{1,0:T(8,128)(2,1)S(1)}, bf16[128,320]{1,0:T(8,128)(2,1)S(1)}, u32[]{:S(2)}, u32[]{:S(2)}) collective-permute-start(bf16[128,320]{1,0:T(8,128)(2,1)S(1)} %get-tuple-element.74), channel_id=1, source_target_pairs={{0,24},{8,16},{16,8},{24,0},{32,56},{40,48},{48,40},{56,32},{64,88... | collective-permute-start | bytes 245768 | tf_op jit(solution)/shard_map/ppermute | solution.py:379

commit v4 on v3

--- a/solution.py
+++ b/solution.py
@@ -76,6 +76,26 @@
     return (centre * lax.rsqrt(var + 1e-5) * gain).astype(BF)
 
 
+def bias_table(bias, rel_bias, reach):
+    plane = lax.axis_index("frame") // GROUP
+    line = lax.broadcasted_iota(jnp.int32, (64, 128), 0)
+    lane = lax.broadcasted_iota(jnp.int32, (64, 128), 1) % 32
+    limit = jnp.zeros((1, 128), jnp.int32)
+    for i in range(32):
+        limit = jnp.where(lane[0:1] == i, reach[plane * 32 + i], limit)
+    allowed = jnp.abs(line - 16 - lane) <= limit
+    padded = jnp.concatenate([rel_bias[...], jnp.zeros((8, 95), F32)], axis=1)
+    for half in range(2):
+        table = []
+        for h in range(4 * half, 4 * half + 4):
+            wide = jnp.broadcast_to(padded[h : h + 1], (32, 128))
+            table.append(pltpu.roll(wide, 0, 1, stride=1, stride_axis=0))
+        table = jnp.concatenate(table, axis=0).T[0:64]
+        bias[:, half * 128 : half * 128 + 128] = jnp.where(
+            allowed, table * (1.0 / math.log(2.0)), -jnp.inf
+        )
+
+
 def hand_out(me, normed, keep, give):
     keep[0] = normed[me]
     keep[1] = normed[me ^ 2]
@@ -87,34 +107,39 @@
     return lax.axis_index("frame") % GROUP
 
 
-def edges_kernel(frames, control, top, bottom, fbuf, cbuf, sems):
-    loads = []
-    for i, (src, dst) in enumerate(((frames, fbuf), (control, cbuf))):
-        for j in range(2):
-            loads.append(
-                pltpu.make_async_copy(src.at[:, pl.ds(6 * j, 2)], dst.at[j], sems.at[2 * j + i])
-            )
-    for load in loads:
-        load.start()
-    for j, out in ((1, bottom), (0, top)):
-        loads[j].wait()
-        loads[2 + j].wait()
-        out[...] = (fbuf[j].astype(F32) + cbuf[j].astype(F32)).astype(BF)
-
-
-def inner_kernel(
-    step, frames, control, first, second, table, gain,
-    keep, give, flat, edge, rim, wide1, wide2, vectors,
-    column, tail, row, fbuf, cbuf, buf1, buf2, merged, taps1, taps2, prod, normed, sems,
+def odd_band():
+    return lax.axis_index("band") % 2 == 1
+
+
+def merge_kernel(
+    frames, control, first, one, two, rows, wide, fbuf, cbuf, buf, merged, sems
 ):
     loads = [
         pltpu.make_async_copy(src, dst, sems.at[i])
-        for i, (src, dst) in enumerate(
-            ((frames, fbuf), (control, cbuf), (first, buf1), (second, buf2))
-        )
+        for i, (src, dst) in enumerate(((frames, fbuf), (control, cbuf), (first, buf)))
     ]
-    for load in loads[:3]:
+    for load in loads:
         load.start()
+    loads[0].wait()
+    loads[1].wait()
+    for m in range(8):
+        for f in range(8):
+            put(merged, m, f, fbuf[f, m].astype(F32) + cbuf[f, m].astype(F32))
+        rows[m] = taken(merged, m).astype(BF)
+    facing = jnp.where(odd_band(), 6, 0)
+    one[...] = rows[pl.ds(facing, 2)]
+    two[...] = rows[pl.ds(6 - facing, 2)]
+    loads[2].wait()
+    arrange(wide, buf)
+
+
+def inner_kernel(
+    step, rows, wide1, second, table, gain,
+    keep, give, flat, edge, wide2, vectors,
+    line, column, tail, row, buf, taps1, taps2, prod, normed, sems,
+):
+    loads = [pltpu.make_async_copy(second.at[i], buf.at[i], sems.at[i]) for i in range(3)]
+    load_gain = pltpu.make_async_copy(gain, line, sems.at[3])
     me = in_group()
     block = step[0] // 128
     whole_block = pltpu.make_async_copy(
@@ -128,34 +153,36 @@
     @pl.when(block < 7)
     def _():
         whole_block.start()
-        whole_block.wait()
-        row[...] = column[...].T
 
     @pl.when(block >= 7)
     def _():
         last_block.start()
-        last_block.wait()
-        row[0:104] = tail[...].T
-
-    embed = row[pl.ds(step[0] % 128, 1), :]
-    vectors[0:1] = embed
-    vectors[1:2] = gain[...].reshape(1, 320)
-    gain = vectors[1:2]
-    loads[0].wait()
-    loads[1].wait()
-    loads[3].start()
+
+    load_gain.start()
+    for load in loads:
+        load.start()
     for m in range(8):
-        for f in range(8):
-            put(merged, m, f, fbuf[f, m].astype(F32) + cbuf[f, m].astype(F32))
-        value = taken(merged, m).astype(BF)
-        if m in (0, 1, 6, 7):
-            rim[(0, 1, None, None, None, None, 2, 3)[m]] = value
+        value = rows[m]
         for dy in range(3):
             if 0 <= m - dy < 6:
                 tapped(taps1, m - dy, dy, value)
-    loads[2].wait()
-    arrange(wide1, buf1)
     multiply(prod, taps1, wide1, 6)
+
+    @pl.when(block < 7)
+    def _():
+        whole_block.wait()
+        row[...] = column[...].T
+
+    @pl.when(block >= 7)
+    def _():
+        last_block.wait()
+        row[0:104] = tail[...].T
+
+    embed = row[pl.ds(step[0] % 128, 1), :]
+    vectors[0:1] = embed
+    load_gain.wait()
+    vectors[1:2] = line[...].reshape(1, 320)
+    gain = vectors[1:2]
     for r in range(6):
         act = silu(combine(prod, r) + embed).astype(BF)
         for dy in range(3):
@@ -163,31 +190,36 @@
                 tapped(taps2, r - dy, dy, act)
         if r in (0, 1, 4, 5):
             edge[(0, 1, None, None, 2, 3)[r]] = act
-    loads[3].wait()
-    arrange(wide2, buf2)
+    for load in loads:
+        load.wait()
+    arrange(wide2, buf)
     multiply(prod, taps2, wide2, 4)
     for y in range(4):
-        value = combine(prod, y) + taken(merged, y + 2)
+        value = combine(prod, y) + rows[y + 2].astype(F32)
         flat[y] = value
         normed[y] = layer_norm(value, gain)
     hand_out(me, normed, keep, give)
 
 
 def outer_kernel(
-    low, high, rim, edge, wide1, wide2, vectors,
-    keep, give, flat,
-    merged, taps1, taps2, prod, normed,
+    reach, one, two, merged, edge, wide1, wide2, vectors, rel_bias, wq, wk, wv, w_out,
+    keep, give, flat, weights, bias,
+    taps1, taps2, prod, normed, sems,
 ):
+    loads = [
+        pltpu.make_async_copy(w, weights.at[i], sems.at[i])
+        for i, w in enumerate((wq, wk, wv, w_out))
+    ]
+    for load in loads:
+        load.start()
     me = in_group()
     band = lax.axis_index("band")
+    odd = odd_band()
     embed = vectors[0:1]
     gain = vectors[1:2]
-    for f in range(8):
-        for y in range(2):
-            put(merged, y, f, low[f, y].astype(F32))
-            put(merged, 2 + y, f, high[f, y].astype(F32))
-    rows = [taken(merged, i).astype(BF) for i in range(4)]
-    rows = [rows[0], rows[1], rim[0], rim[1], rim[2], rim[3], rows[2], rows[3]]
+    low = [jnp.where(odd, two[y], one[y]) for y in range(2)]
+    high = [jnp.where(odd, one[y], two[y]) for y in range(2)]
+    rows = low + [merged[0], merged[1], merged[6], merged[7]] + high
     starts = (0, 1, 4, 5)
     for m in range(8):
         for r in range(4):
@@ -206,10 +238,13 @@
                     tapped(taps2, 2 * side + i - dy, dy, lines[side][i])
     multiply(prod, taps2, wide2, 4)
     for y in range(4):
-        value = combine(prod, y) + rim[y].astype(F32)
+        value = combine(prod, y) + merged[(0, 1, 6, 7)[y]].astype(F32)
         flat[y] = value
         normed[y] = layer_norm(value, gain)
     hand_out(me, normed, keep, give)
+    bias_table(bias, rel_bias, reach)
+    for load in loads:
+        load.wait()
 
 
 def pack_kernel(keep, got, near, far):
@@ -220,36 +255,12 @@
 
 
 def attend_kernel(
-    reach, near, across_x, near_z, across_z, wq, wk, wv, w_out, rel_bias,
+    near, across_x, near_z, across_z, weights, bias,
     out0, out1, out2, out3,
-    weights, field, query, key, value, score, prob, back, bias, sems,
+    field, query, key, value, score, prob, back,
 ):
-    loads = [
-        pltpu.make_async_copy(w, weights.at[i], sems.at[i])
-        for i, w in enumerate((wq, wk, wv, w_out))
-    ]
-    for load in loads:
-        load.start()
-    place = lax.axis_index("frame")
-    me = place % GROUP
+    me = in_group()
     pixels = field.shape[0]
-
-    line = lax.broadcasted_iota(jnp.int32, (64, 128), 0)
-    lane = lax.broadcasted_iota(jnp.int32, (64, 128), 1) % 32
-    limit = jnp.zeros((1, 128), jnp.int32)
-    for i in range(32):
-        limit = jnp.where(lane[0:1] == i, reach[(place // GROUP) * 32 + i], limit)
-    allowed = jnp.abs(line - 16 - lane) <= limit
-    padded = jnp.concatenate([rel_bias[...], jnp.zeros((8, 95), F32)], axis=1)
-    for half in range(2):
-        table = []
-        for h in range(4 * half, 4 * half + 4):
-            wide = jnp.broadcast_to(padded[h : h + 1], (32, 128))
-            table.append(pltpu.roll(wide, 0, 1, stride=1, stride_axis=0))
-        table = jnp.concatenate(table, axis=0).T[0:64]
-        bias[:, half * 128 : half * 128 + 128] = jnp.where(
-            allowed, table * (1.0 / math.log(2.0)), -jnp.inf
-        )
 
     for k in range(4):
         block = me ^ k
@@ -259,8 +270,6 @@
         halo = (near_z, across_z)[k // 2]
         at = pl.multiple_of(jnp.where(block >= 2, 8 * block - 16, 48 + 8 * block), 8)
         field[:, pl.ds(at, 8), :] = halo[k % 2].astype(F32).reshape(pixels, 8, 320)
-    for load in loads[:3]:
-        load.wait()
 
     def project(x, i):
         return jnp.dot(x, weights[i], preferred_element_type=F32).astype(BF)
@@ -330,7 +339,6 @@
     each(scores)
     each(softmax)
     each(attended)
-    loads[3].wait()
     for k, out in enumerate((out0, out1, out2, out3)):
         out[...] = project(back[me ^ k].reshape(pixels * 8, 320).astype(BF), 3)
 
@@ -365,8 +373,9 @@
     count = lax.axis_size("frame")
     bands = lax.axis_size("band")
     planes = count // GROUP
-    up = [(i, i + 1) for i in range(bands - 1)]
-    down = [(i + 1, i) for i in range(bands - 1)]
+    def swaps(first):
+        pairs = [(i, i + 1) for i in range(first, bands - 1, 2)]
+        return pairs + [(j, i) for i, j in pairs]
 
     def plane(i, k):
         return (i & ~3) | ((i & 3) ^ k)
@@ -386,8 +395,6 @@
         return pltpu.CompilerParams(vmem_limit_bytes=mebibytes * MIB)
     pair = jax.ShapeDtypeStruct((2, 128, 320), BF)
     chunk = pltpu.VMEM((4, 128, 320), F32)
-    wide = pltpu.VMEM((960, 960), BF)
-    rows = pltpu.VMEM((4, 128, 320), BF)
 
     def cost(flops):
         return pl.CostEstimate(flops=flops, bytes_accessed=4_000_000, transcendentals=0)
@@ -403,47 +410,48 @@
         pltpu.VMEM((768, 960), F32),
         pltpu.VMEM((4, 128, 320), BF),
     ]
-    margin = jax.ShapeDtypeStruct((8, 2, 16, 320), BF)
-    top, bottom = pl.pallas_call(
-        edges_kernel,
-        in_specs=[anywhere] * 2,
-        out_specs=[vmem] * 2,
-        out_shape=[margin] * 2,
+    wide = pltpu.VMEM((960, 960), BF)
+    one, two, merged, wide1 = pl.pallas_call(
+        merge_kernel,
+        in_specs=[anywhere] * 3,
+        out_specs=[vmem] * 4,
+        out_shape=[pair, pair, pltpu.VMEM((8, 128, 320), BF), wide],
         scratch_shapes=[
-            pltpu.VMEM((2, 8, 2, 16, 320), BF),
-            pltpu.VMEM((2, 8, 2, 16, 320), BF),
-            pltpu.SemaphoreType.DMA((4,)),
+            pltpu.VMEM((8, 8, 16, 320), BF),
+            pltpu.VMEM((8, 8, 16, 320), BF),
+            pltpu.VMEM((3, 3, 320, 320), BF),
+            pltpu.VMEM((3, 8, 128, 128), F32),
+            pltpu.SemaphoreType.DMA((3,)),
         ],
-        compiler_params=params(4),
-        name="edges",
-    )(*stay(frames, control))
-    top, bottom, step_index = lax.optimization_barrier((top, bottom, step_index))
-    low = lax.ppermute(bottom, "band", up)
-    high = lax.ppermute(top, "band", down)
-
-    keep, give, flat_in, edge, rim, wide1, wide2, vectors = pl.pallas_call(
+        compiler_params=params(8),
+        name="merge",
+    )(*stay(frames, control, conv_first))
+    one, two, step_index = lax.optimization_barrier((one, two, step_index))
+    one = lax.ppermute(one, "band", swaps(1))
+    two = lax.ppermute(two, "band", swaps(0))
+
+    keep, give, flat_in, edge, wide2, vectors = pl.pallas_call(
         inner_kernel,
-        in_specs=[smem] + [anywhere] * 5 + [vmem],
-        out_specs=[vmem] * 8,
-        out_shape=[pair, pair, chunk, rows, rows, wide, wide, pltpu.VMEM((2, 320), F32)],
+        in_specs=[smem] + [vmem] * 2 + [anywhere] * 3,
+        out_specs=[vmem] * 6,
+        out_shape=[
+            pair, pair, chunk, pltpu.VMEM((4, 128, 320), BF), wide, pltpu.VMEM((2, 320), F32)
+        ],
         scratch_shapes=[
+            pltpu.VMEM((320,), F32),
             pltpu.VMEM((320, 128), F32),
             pltpu.VMEM((320, 104), F32),
             pltpu.VMEM((128, 320), F32),
-            pltpu.VMEM((8, 8, 16, 320), BF),
-            pltpu.VMEM((8, 8, 16, 320), BF),
             pltpu.VMEM((3, 3, 320, 320), BF),
-            pltpu.VMEM((3, 3, 320, 320), BF),
-            pltpu.VMEM((3, 8, 128, 128), F32),
             pltpu.VMEM((6, 128, 960), BF),
         ]
         + rows_scratch
         + [pltpu.SemaphoreType.DMA((5,))],
-        compiler_params=params(22),
+        compiler_params=params(16),
         name="inner_rows",
-    )(step_index, *stay(frames, control, conv_first, conv_second, time_table.T), norm_gain)
-
-    keep, give, low, high = lax.optimization_barrier((keep, give, low, high))
+    )(step_index, *near_by(merged, wide1), *stay(conv_second, time_table.T, norm_gain))
+
+    keep, give, one, two = lax.optimization_barrier((keep, give, one, two))
 
     def packed(keep, give):
         got = exchange(give, plane, 1)
@@ -465,19 +473,24 @@
     z_in = exchange(near_in, beside, 0)
     near_in, edge = lax.optimization_barrier((near_in, edge))
 
-    keep, give, flat_out = pl.pallas_call(
+    keep, give, flat_out, weights, bias = pl.pallas_call(
         outer_kernel,
-        in_specs=[vmem] * 7,
-        out_specs=[vmem] * 3,
-        out_shape=[pair, pair, chunk],
+        in_specs=[smem] + [vmem] * 8 + [anywhere] * 4,
+        out_specs=[vmem] * 5,
+        out_shape=[
+            pair, pair, chunk, pltpu.VMEM((4, 320, 320), BF), pltpu.VMEM((64, 256), F32)
+        ],
         scratch_shapes=[
-            pltpu.VMEM((3, 4, 128, 128), F32),
             pltpu.VMEM((4, 128, 960), BF),
         ]
-        + rows_scratch,
+        + rows_scratch
+        + [pltpu.SemaphoreType.DMA((4,))],
         compiler_params=params(12),
         name="outer_rows",
-    )(low, high, *near_by(rim, edge, wide1, wide2, vectors))
+    )(
+        reach, one, two, *near_by(merged, edge, wide1, wide2, vectors), rel_bias,
+        *stay(w_query, w_key, w_value, w_out),
+    )
 
     give, x_in, z_in = lax.optimization_barrier((give, x_in, z_in))
     xz_in = exchange(x_in, onward, 0)
@@ -490,11 +503,10 @@
         piece = jax.ShapeDtypeStruct((128, 320), BF)
         outs = pl.pallas_call(
             attend_kernel,
-            in_specs=[smem] + [vmem] * 4 + [anywhere] * 4 + [vmem],
+            in_specs=[vmem] * 6,
             out_specs=[vmem] * 4,
             out_shape=[piece] * 4,
             scratch_shapes=[
-                pltpu.VMEM((4, 320, 320), BF),
                 pltpu.VMEM((16, 64, 320), F32),
                 pltpu.VMEM((16, 32, 320), BF),
                 pltpu.VMEM((16, 64, 320), BF),
@@ -502,12 +514,10 @@
                 pltpu.VMEM((16, 64, 256), F32),
                 pltpu.VMEM((16, 64, 256), BF),
                 pltpu.VMEM((4, 16, 8, 320), F32),
-                pltpu.VMEM((64, 256), F32),
-                pltpu.SemaphoreType.DMA((4,)),
             ],
             compiler_params=params(14),
             name="attend",
-        )(reach, *fields, *stay(w_query, w_key, w_value, w_out), rel_bias)
+        )(*fields, *near_by(weights, bias))
         return [outs[0]] + [exchange(outs[k], plane, k) for k in (2, 3, 1)], outs[0]
 
     near_out, near_in = lax.optimization_barrier((near_out, near_in))

time: 66.4 us -> 63.1 us (0.950)
  the two profiles are of different devices: /device:TPU:3 before, /device:TPU:1 now
where the time goes in v4:
time: 63.1 us; the launch traced here: 62.9 us
  starting transfers between devices  30.2 us (48%)
  Pallas kernels  21.3 us (34%)
  waiting for transfers between devices  10.4 us (16%)
  between operations  0.94 us (1%)
    ppermute x14, starting transfers between devices, exchange(): return lax.ppermute(x, 'frame', [(i, to(i, k)) for i in range(count)])  24.8 us
    ppermute x14, waiting for transfers between devices, exchange(): return lax.ppermute(x, 'frame', [(i, to(i, k)) for i in range(count)])  10.4 us
    pallas_call x2, Pallas kernels, attend(): pl.pallas_call(attend_kernel, in_specs=[vmem] * 6, out_specs=[vmem] * 4,...  6.28 us
    pallas_call x1, Pallas kernels, shards(): pl.pallas_call(inner_kernel, in_specs=[smem] + [vmem] * 2 + [anywhere] *...  5.56 us
    pallas_call x1, Pallas kernels, shards(): pl.pallas_call(outer_kernel, in_specs=[smem] + [vmem] * 8 + [anywhere] *...  4.93 us
    ppermute x1, starting transfers between devices, shards(): two = lax.ppermute(two, 'band', swaps(0))  4.74 us
    pallas_call x1, Pallas kernels, shards(): pl.pallas_call(merge_kernel, in_specs=[anywhere] * 3, out_specs=[vmem] *...  2.55 us
    pallas_call x2, Pallas kernels, finish(): pl.pallas_call(body, in_specs=[vmem] * 5 + [anywhere] * len(before), out_...  1.94 us
  transfers between devices with their start and end apart: 16, of which 6 were waited for; matrix products, arithmetic and copies ran while one was open for 0% of the time, Pallas kernels for 28%

profile of v4, /device:TPU:1, one launch (start us, length us, event | category | flops | bytes accessed | tf_op | source)
XLA Modules:
  0.0 62.9 jit_solution(15614679788862678379)
XLA Ops:
  0.0 2.5 %merge.1 = (bf16[2,128,320]{2,1,0:T(8,128)(2,1)S(1)}, bf16[2,128,320]{2,1,0:T(8,128)(2,1)S(1)}, bf16[8,128,320]{2,1,0:T(8,128)(2,1)S(1)}, bf16[960,960]{1,0:T(8,128)(2,1)S(1)}) custom-call(bf16[8,8,16,320]{3,2,1,0:T(8,128)(2,1)} %frames.1, bf16[8,8,16,320]{3,2,1,0:T(8,128)(2,1)} %control.1, bf16[3,3,320,320]{3,2,1,0:T(8,128)(2,1)} %first.1), custom_call_target="tpu_custom_call" | custom-call | tf_op jit(solution)/shard_map/merge/pallas_call | solution.py:414
  2.6 0.7 %collective-permute-start = (bf16[2,128,320]{2,1,0:T(8,128)(2,1)S(1)}, bf16[2,128,320]{2,1,0:T(8,128)(2,1)S(1)}, u32[]{:S(2)}, u32[]{:S(2)}) collective-permute-start(bf16[2,128,320]{2,1,0:T(8,128)(2,1)S(1)} %get-tuple-element.54), channel_id=1, source_target_pairs={{1,2},{3,4},{5,6},{2,1},{4,3},{6,5},{9,10},{11,12},{13,14},{10,9},... | collective-permute-start | bytes 491528 | tf_op jit(solution)/shard_map/ppermute | solution.py:430
  3.2 4.7 %collective-permute-start.1 = (bf16[2,128,320]{2,1,0:T(8,128)(2,1)S(1)}, bf16[2,128,320]{2,1,0:T(8,128)(2,1)S(1)}, u32[]{:S(2)}, u32[]{:S(2)}) collective-permute-start(bf16[2,128,320]{2,1,0:T(8,128)(2,1)S(1)} %get-tuple-element.55), channel_id=1, source_target_pairs={{0,1},{2,3},{4,5},{6,7},{1,0},{3,2},{5,4},{7,6},{8,9},{10,11},{12,... | collective-permute-start | bytes 491528 | tf_op jit(solution)/shard_map/ppermute | solution.py:431
  8.6 0.0 copy-start
  8.6 0.0 copy-start.1
  8.7 5.6 %inner_rows.1 = (bf16[2,128,320]{2,1,0:T(8,128)(2,1)S(1)}, bf16[2,128,320]{2,1,0:T(8,128)(2,1)S(1)}, f32[4,128,320]{2,1,0:T(8,128)S(1)}, bf16[4,128,320]{2,1,0:T...) custom-call(s32[1]{0:T(128)S(6)} %copy.16.step, ...), custom_call_target="tpu_custom_call" | custom-call | tf_op jit(solution)/shard_map/inner_rows/pallas_call | solution.py:433
  14.2 0.0 collective-permute-done.one
  14.2 0.0 collective-permute-done.1.two
  14.2 1.3 %collective-permute-start.2 = (bf16[2,128,320]{2,1,0:T(8,128)(2,1)S(1)}, bf16[2,128,320]{2,1,0:T(8,128)(2,1)S(1)}, u32[]{:S(2)}, u32[]{:S(2)}) collective-permute-start(bf16[2,128,320]{2,1,0:T(8,128)(2,1)S(1)} %get-tuple-element.59), channel_id=1, source_target_pairs={{0,8},{8,0},{16,24},{24,16},{32,40},{40,32},{48,56},{56,48},{64,72... | collective-permute-start | bytes 491528 | tf_op jit(solution)/shard_map/ppermute | solution.py:388
  15.6 1.1 %collective-permute-done.2.got = bf16[2,128,320]{2,1,0:T(8,128)(2,1)S(1)} collective-permute-done((bf16[2,128,320]{2,1,0:T(8,128)(2,1)S(1)}, bf16[2,128,320]{2,1,0:T(8,128)(2,1)S(1)}, u32[]{:S(2)}, u32[]{:S(2)}) %collective-permute-start.2) | collective-permute-done | bytes 163872 | tf_op jit(solution)/shard_map/ppermute | solution.py:388
  16.7 2.8 %collective-permute-start.3 = (bf16[2,128,320]{2,1,0:T(8,128)(2,1)S(1)}, bf16[2,128,320]{2,1,0:T(8,128)(2,1)S(1)}, u32[]{:S(2)}, u32[]{:S(2)}) collective-permute-start(bf16[2,128,320]{2,1,0:T(8,128)(2,1)S(1)} %get-tuple-element.67), channel_id=1, source_target_pairs={{0,16},{8,24},{16,0},{24,8},{32,48},{40,56},{48,32},{56,40},{64,80... | collective-permute-start | bytes 491528 | tf_op jit(solution)/shard_map/ppermute | solution.py:388
  19.5 5.6 %collective-permute-start.4 = (bf16[2,128,320]{2,1,0:T(8,128)(2,1)S(1)}, bf16[2,128,320]{2,1,0:T(8,128)(2,1)S(1)}, u32[]{:S(2)}, u32[]{:S(2)}) collective-permute-start(bf16[2,128,320]{2,1,0:T(8,128)(2,1)S(1)} %get-tuple-element.80.near), channel_id=1, source_target_pairs={{0,224},{8,232},{16,48},{24,56},{32,0},{40,8},{48,80},{56,88},{64,... | collective-permute-start | bytes 491528 | tf_op jit(solution)/shard_map/ppermute | solution.py:388
  25.1 0.0 copy-done
  25.1 0.0 copy-done.1
  25.1 4.9 %outer_rows.1 = (bf16[2,128,320]{2,1,0:T(8,128)(2,1)S(1)}, bf16[2,128,320]{2,1,0:T(8,128)(2,1)S(1)}, f32[4,128,320]{2,1,0:T(8,128)S(1)}, bf16[4,320,320]{2,1,0:T(8,128)(2,1)S(1)}, f32[64,256]{1,0:T(8,128)S(1)}) custom-call(s32[256]{0:T(256)S(1)} %copy-done.1, bf16[2,128,320]{2,1,0:T(8,128)(2,1)S(1)} %collective-permute-done.one, ...), custom_call_target="tpu_custom_call" | custom-call | tf_op jit(solution)/shard_map/outer_rows/pallas_call | solution.py:476
  30.0 0.0 collective-permute-done.3.across_x
  30.0 0.0 collective-permute-done.4.near_z
  30.0 1.0 %collective-permute-start.5 = (bf16[2,128,320]{2,1,0:T(8,128)(2,1)S(1)}, bf16[2,128,320]{2,1,0:T(8,128)(2,1)S(1)}, u32[]{:S(2)}, u32[]{:S(2)}) collective-permute-start(bf16[2,128,320]{2,1,0:T(8,128)(2,1)S(1)} %get-tuple-element.68), channel_id=1, source_target_pairs={{0,8},{8,0},{16,24},{24,16},{32,40},{40,32},{48,56},{56,48},{64,72... | collective-permute-start | bytes 491528 | tf_op jit(solution)/shard_map/ppermute | solution.py:388
  31.1 0.0 collective-permute-start.12
  31.1 1.1 %collective-permute-done.5.got = bf16[2,128,320]{2,1,0:T(8,128)(2,1)S(1)} collective-permute-done((bf16[2,128,320]{2,1,0:T(8,128)(2,1)S(1)}, bf16[2,128,320]{2,1,0:T(8,128)(2,1)S(1)}, u32[]{:S(2)}, u32[]{:S(2)}) %collective-permute-start.5) | collective-permute-done | bytes 163872 | tf_op jit(solution)/shard_map/ppermute | solution.py:388
  32.2 2.6 %collective-permute-start.7 = (bf16[2,128,320]{2,1,0:T(8,128)(2,1)S(1)}, bf16[2,128,320]{2,1,0:T(8,128)(2,1)S(1)}, u32[]{:S(2)}, u32[]{:S(2)}) collective-permute-start(bf16[2,128,320]{2,1,0:T(8,128)(2,1)S(1)} %get-tuple-element.71.near), channel_id=1, source_target_pairs={{0,224},{8,232},{16,48},{24,56},{32,0},{40,8},{48,80},{56,88},{64,... | collective-permute-start | bytes 491528 | tf_op jit(solution)/shard_map/ppermute | solution.py:388
  34.8 1.6 %collective-permute-start.8 = (bf16[2,128,320]{2,1,0:T(8,128)(2,1)S(1)}, bf16[2,128,320]{2,1,0:T(8,128)(2,1)S(1)}, u32[]{:S(2)}, u32[]{:S(2)}) collective-permute-start(bf16[2,128,320]{2,1,0:T(8,128)(2,1)S(1)} %get-tuple-element.72), channel_id=1, source_target_pairs={{0,240},{8,248},{16,32},{24,40},{32,16},{40,24},{48,64},{56,72},{6... | collective-permute-start | bytes 491528 | tf_op jit(solution)/shard_map/ppermute | solution.py:388
  36.4 0.0 collective-permute-start.6
  36.4 2.3 %collective-permute-done.12.across_z = bf16[2,128,320]{2,1,0:T(8,128)(2,1)S(1)} collective-permute-done((bf16[2,128,320]{2,1,0:T(8,128)(2,1)S(1)}, bf16[2,128,320]{2,1,0:T(8,128)(2,1)S(1)}, u32[]{:S(2)}, u32[]{:S(2)}) %collective-permute-start.12) | collective-permute-done | bytes 163872 | tf_op jit(solution)/shard_map/ppermute | solution.py:388
  38.7 3.1 %attend.3 = (bf16[128,320]{1,0:T(8,128)(2,1)S(1)}, bf16[128,320]{1,0:T(8,128)(2,1)S(1)}, bf16[128,320]{1,0:T(8,128)(2,1)S(1)}, bf16[128,320]{1,0:T(8,128)(2,1)S(1)}) custom-call(bf16[2,128,320]{2,1,0:T(8,128)(2,1)S(1)} %get-tuple-element.80.near, bf16[2,128,320]{2,1,0:T(8,128)(2,1)S(1)} %collective-permute-done.3.across_x, ...), custom_call_target="tpu_custom_call" | custom-call | tf_op jit(solution)/shard_map/attend/pallas_call | solution.py:504
  41.9 1.0 %collective-permute-start.13 = (bf16[128,320]{1,0:T(8,128)(2,1)S(1)}, bf16[128,320]{1,0:T(8,128)(2,1)S(1)}, u32[]{:S(2)}, u32[]{:S(2)}) collective-permute-start(bf16[128,320]{1,0:T(8,128)(2,1)S(1)} %get-tuple-element.85), channel_id=1, source_target_pairs={{0,8},{8,0},{16,24},{24,16},{32,40},{40,32},{48,56},{56,48},{64,72... | collective-permute-start | bytes 245768 | tf_op jit(solution)/shard_map/ppermute | solution.py:388
  42.8 0.9 %collective-permute-start.14 = (bf16[128,320]{1,0:T(8,128)(2,1)S(1)}, bf16[128,320]{1,0:T(8,128)(2,1)S(1)}, u32[]{:S(2)}, u32[]{:S(2)}) collective-permute-start(bf16[128,320]{1,0:T(8,128)(2,1)S(1)} %get-tuple-element.86), channel_id=1, source_target_pairs={{0,16},{8,24},{16,0},{24,8},{32,48},{40,56},{48,32},{56,40},{64,80... | collective-permute-start | bytes 245768 | tf_op jit(solution)/shard_map/ppermute | solution.py:388
  43.8 0.0 collective-permute-done.7.near_z
  43.8 2.3 %collective-permute-start.15 = (bf16[128,320]{1,0:T(8,128)(2,1)S(1)}, bf16[128,320]{1,0:T(8,128)(2,1)S(1)}, u32[]{:S(2)}, u32[]{:S(2)}) collective-permute-start(bf16[128,320]{1,0:T(8,128)(2,1)S(1)} %get-tuple-element.87), channel_id=1, source_target_pairs={{0,24},{8,16},{16,8},{24,0},{32,56},{40,48},{48,40},{56,32},{64,88... | collective-permute-start | bytes 245768 | tf_op jit(solution)/shard_map/ppermute | solution.py:388
  46.1 0.0 collective-permute-done.8.across_z
  46.1 2.0 %collective-permute-done.6.across_x = bf16[2,128,320]{2,1,0:T(8,128)(2,1)S(1)} collective-permute-done((bf16[2,128,320]{2,1,0:T(8,128)(2,1)S(1)}, bf16[2,128,320]{2,1,0:T(8,128)(2,1)S(1)}, u32[]{:S(2)}, u32[]{:S(2)}) %collective-permute-start.6) | collective-permute-done | bytes 163872 | tf_op jit(solution)/shard_map/ppermute | solution.py:388
  48.1 3.1 %attend.2 = (bf16[128,320]{1,0:T(8,128)(2,1)S(1)}, bf16[128,320]{1,0:T(8,128)(2,1)S(1)}, bf16[128,320]{1,0:T(8,128)(2,1)S(1)}, bf16[128,320]{1,0:T(8,128)(2,1)S(1)}) custom-call(bf16[2,128,320]{2,1,0:T(8,128)(2,1)S(1)} %get-tuple-element.71.near, bf16[2,128,320]{2,1,0:T(8,128)(2,1)S(1)} %collective-permute-done.6.across_x, ...), custom_call_target="tpu_custom_call" | custom-call | tf_op jit(solution)/shard_map/attend/pallas_call | solution.py:504
  51.2 2.4 %collective-permute-start.9 = (bf16[128,320]{1,0:T(8,128)(2,1)S(1)}, bf16[128,320]{1,0:T(8,128)(2,1)S(1)}, u32[]{:S(2)}, u32[]{:S(2)}) collective-permute-start(bf16[128,320]{1,0:T(8,128)(2,1)S(1)} %get-tuple-element.76), channel_id=1, source_target_pairs={{0,8},{8,0},{16,24},{24,16},{32,40},{40,32},{48,56},{56,48},{64,72... | collective-permute-start | bytes 245768 | tf_op jit(solution)/shard_map/ppermute | solution.py:388
  53.6 0.0 collective-permute-start.10
  53.7 0.0 collective-permute-done.13.refs_1_
  53.7 3.2 %collective-permute-start.11 = (bf16[128,320]{1,0:T(8,128)(2,1)S(1)}, bf16[128,320]{1,0:T(8,128)(2,1)S(1)}, u32[]{:S(2)}, u32[]{:S(2)}) collective-permute-start(bf16[128,320]{1,0:T(8,128)(2,1)S(1)} %get-tuple-element.78), channel_id=1, source_target_pairs={{0,24},{8,16},{16,8},{24,0},{32,56},{40,48},{48,40},{56,32},{64,88... | collective-permute-start | bytes 245768 | tf_op jit(solution)/shard_map/ppermute | solution.py:388
  56.9 0.0 collective-permute-done.14.refs_2_
  56.9 0.0 collective-permute-done.15.refs_3_
  56.9 1.0 %project_out.2.refs_5_ = f32[8,8,16,320]{3,2,1,0:T(8,128)} custom-call(bf16[128,320]{1,0:T(8,128)(2,1)S(1)} %get-tuple-element.84.refs_0_, bf16[128,320]{1,0:T(8,128)(2,1)S(1)} %collective-permute-done.13.refs_1_, bf16[128,320]{1,0:T(8,128)(2,1)S(1)} %collective-permute-done.14.refs_2_, bf16[128,320]{1,0:T(8,128)(2,1)S(1)} %collective-permute-done.15.refs_3_, ...), custom_call_target="tpu_custom_call" | custom-call | tf_op jit(solution)/shard_map/project_out/pallas_call | solution.py:533
  57.9 0.0 collective-permute-done.9.refs_1_
  57.9 1.6 %collective-permute-done.10.refs_2_ = bf16[128,320]{1,0:T(8,128)(2,1)S(1)} collective-permute-done((bf16[128,320]{1,0:T(8,128)(2,1)S(1)}, bf16[128,320]{1,0:T(8,128)(2,1)S(1)}, u32[]{:S(2)}, u32[]{:S(2)}) %collective-permute-start.10) | collective-permute-done | bytes 81952 | tf_op jit(solution)/shard_map/ppermute | solution.py:388
  59.5 2.3 %collective-permute-done.11.refs_3_ = bf16[128,320]{1,0:T(8,128)(2,1)S(1)} collective-permute-done((bf16[128,320]{1,0:T(8,128)(2,1)S(1)}, bf16[128,320]{1,0:T(8,128)(2,1)S(1)}, u32[]{:S(2)}, u32[]{:S(2)}) %collective-permute-start.11) | collective-permute-done | bytes 81952 | tf_op jit(solution)/shard_map/ppermute | solution.py:388
  61.8 1.0 %project_out.3 = f32[8,8,16,320]{3,2,1,0:T(8,128)} custom-call(bf16[128,320]{1,0:T(8,128)(2,1)S(1)} %get-tuple-element.75.refs_0_, bf16[128,320]{1,0:T(8,128)(2,1)S(1)} %collective-permute-done.9.refs_1_, bf16[128,320]{1,0:T(8,128)(2,1)S(1)} %collective-permute-done.10.refs_2_, ...), custom_call_target="tpu_custom_call", output_to_operand_aliasing={{}: (5, {})} | custom-call | tf_op jit(solution)/shard_map/project_out/pallas_call | solution.py:533
  (2 shorter events, 0.1 us)
Async XLA Ops:
  2.6 11.7 %collective-permute-start = (bf16[2,128,320]{2,1,0:T(8,128)(2,1)S(1)}, bf16[2,128,320]{2,1,0:T(8,128)(2,1)S(1)}, u32[]{:S(2)}, u32[]{:S(2)}) collective-permute-start(bf16[2,128,320]{2,1,0:T(8,128)(2,1)S(1)} %get-tuple-element.54), channel_id=1, source_target_pairs={{1,2},{3,4},{5,6},{2,1},{4,3},{6,5},{9,10},{11,12},{13,14},{10,9},... | collective-permute-start | bytes 491528 | tf_op jit(solution)/shard_map/ppermute | solution.py:430
  3.2 11.0 %collective-permute-start.1 = (bf16[2,128,320]{2,1,0:T(8,128)(2,1)S(1)}, bf16[2,128,320]{2,1,0:T(8,128)(2,1)S(1)}, u32[]{:S(2)}, u32[]{:S(2)}) collective-permute-start(bf16[2,128,320]{2,1,0:T(8,128)(2,1)S(1)} %get-tuple-element.55), channel_id=1, source_target_pairs={{0,1},{2,3},{4,5},{6,7},{1,0},{3,2},{5,4},{7,6},{8,9},{10,11},{12,... | collective-permute-start | bytes 491528 | tf_op jit(solution)/shard_map/ppermute | solution.py:431
  8.6 16.4 %copy-start = (f32[8,33]{1,0:T(8,128)S(1)}, f32[8,33]{1,0:T(8,128)}, u32[]{:S(2)}) copy-start(f32[8,33]{1,0:T(8,128)} %rel_bias.1) | copy-start | bytes 3172
  8.6 16.4 %copy-start.1 = (s32[256]{0:T(256)S(1)}, s32[256]{0:T(256)}, u32[]{:S(2)}) copy-start(s32[256]{0:T(256)} %reach.1) | copy-start | bytes 3076
  14.2 2.4 %collective-permute-start.2 = (bf16[2,128,320]{2,1,0:T(8,128)(2,1)S(1)}, bf16[2,128,320]{2,1,0:T(8,128)(2,1)S(1)}, u32[]{:S(2)}, u32[]{:S(2)}) collective-permute-start(bf16[2,128,320]{2,1,0:T(8,128)(2,1)S(1)} %get-tuple-element.59), channel_id=1, source_target_pairs={{0,8},{8,0},{16,24},{24,16},{32,40},{40,32},{48,56},{56,48},{64,72... | collective-permute-start | bytes 491528 | tf_op jit(solution)/shard_map/ppermute | solution.py:388
  16.7 13.4 %collective-permute-start.3 = (bf16[2,128,320]{2,1,0:T(8,128)(2,1)S(1)}, bf16[2,128,320]{2,1,0:T(8,128)(2,1)S(1)}, u32[]{:S(2)}, u32[]{:S(2)}) collective-permute-start(bf16[2,128,320]{2,1,0:T(8,128)(2,1)S(1)} %get-tuple-element.67), channel_id=1, source_target_pairs={{0,16},{8,24},{16,0},{24,8},{32,48},{40,56},{48,32},{56,40},{64,80... | collective-permute-start | bytes 491528 | tf_op jit(solution)/shard_map/ppermute | solution.py:388
  19.5 10.5 %collective-permute-start.4 = (bf16[2,128,320]{2,1,0:T(8,128)(2,1)S(1)}, bf16[2,128,320]{2,1,0:T(8,128)(2,1)S(1)}, u32[]{:S(2)}, u32[]{:S(2)}) collective-permute-start(bf16[2,128,320]{2,1,0:T(8,128)(2,1)S(1)} %get-tuple-element.80.near), channel_id=1, source_target_pairs={{0,224},{8,232},{16,48},{24,56},{32,0},{40,8},{48,80},{56,88},{64,... | collective-permute-start | bytes 491528 | tf_op jit(solution)/shard_map/ppermute | solution.py:388
  30.0 2.1 %collective-permute-start.5 = (bf16[2,128,320]{2,1,0:T(8,128)(2,1)S(1)}, bf16[2,128,320]{2,1,0:T(8,128)(2,1)S(1)}, u32[]{:S(2)}, u32[]{:S(2)}) collective-permute-start(bf16[2,128,320]{2,1,0:T(8,128)(2,1)S(1)} %get-tuple-element.68), channel_id=1, source_target_pairs={{0,8},{8,0},{16,24},{24,16},{32,40},{40,32},{48,56},{56,48},{64,72... | collective-permute-start | bytes 491528 | tf_op jit(solution)/shard_map/ppermute | solution.py:388
  31.1 7.7 %collective-permute-start.12 = (bf16[2,128,320]{2,1,0:T(8,128)(2,1)S(1)}, bf16[2,128,320]{2,1,0:T(8,128)(2,1)S(1)}, u32[]{:S(2)}, u32[]{:S(2)}) collective-permute-start(bf16[2,128,320]{2,1,0:T(8,128)(2,1)S(1)} %collective-permute-done.3.across_x), channel_id=1, source_target_pairs={{0,32},{8,40},{16,240},{24,248},{32,64},{40,72},{48,16},{56,24},{6... | collective-permute-start | bytes 491528 | tf_op jit(solution)/shard_map/ppermute | solution.py:388
  32.2 11.6 %collective-permute-start.7 = (bf16[2,128,320]{2,1,0:T(8,128)(2,1)S(1)}, bf16[2,128,320]{2,1,0:T(8,128)(2,1)S(1)}, u32[]{:S(2)}, u32[]{:S(2)}) collective-permute-start(bf16[2,128,320]{2,1,0:T(8,128)(2,1)S(1)} %get-tuple-element.71.near), channel_id=1, source_target_pairs={{0,224},{8,232},{16,48},{24,56},{32,0},{40,8},{48,80},{56,88},{64,... | collective-permute-start | bytes 491528 | tf_op jit(solution)/shard_map/ppermute | solution.py:388
  34.8 11.3 %collective-permute-start.8 = (bf16[2,128,320]{2,1,0:T(8,128)(2,1)S(1)}, bf16[2,128,320]{2,1,0:T(8,128)(2,1)S(1)}, u32[]{:S(2)}, u32[]{:S(2)}) collective-permute-start(bf16[2,128,320]{2,1,0:T(8,128)(2,1)S(1)} %get-tuple-element.72), channel_id=1, source_target_pairs={{0,240},{8,248},{16,32},{24,40},{32,16},{40,24},{48,64},{56,72},{6... | collective-permute-start | bytes 491528 | tf_op jit(solution)/shard_map/ppermute | solution.py:388
  36.4 11.7 %collective-permute-start.6 = (bf16[2,128,320]{2,1,0:T(8,128)(2,1)S(1)}, bf16[2,128,320]{2,1,0:T(8,128)(2,1)S(1)}, u32[]{:S(2)}, u32[]{:S(2)}) collective-permute-start(bf16[2,128,320]{2,1,0:T(8,128)(2,1)S(1)} %get-tuple-element.72), channel_id=1, source_target_pairs={{0,16},{8,24},{16,0},{24,8},{32,48},{40,56},{48,32},{56,40},{64,80... | collective-permute-start | bytes 491528 | tf_op jit(solution)/shard_map/ppermute | solution.py:388
  41.9 11.8 %collective-permute-start.13 = (bf16[128,320]{1,0:T(8,128)(2,1)S(1)}, bf16[128,320]{1,0:T(8,128)(2,1)S(1)}, u32[]{:S(2)}, u32[]{:S(2)}) collective-permute-start(bf16[128,320]{1,0:T(8,128)(2,1)S(1)} %get-tuple-element.85), channel_id=1, source_target_pairs={{0,8},{8,0},{16,24},{24,16},{32,40},{40,32},{48,56},{56,48},{64,72... | collective-permute-start | bytes 245768 | tf_op jit(solution)/shard_map/ppermute | solution.py:388
  42.8 14.0 %collective-permute-start.14 = (bf16[128,320]{1,0:T(8,128)(2,1)S(1)}, bf16[128,320]{1,0:T(8,128)(2,1)S(1)}, u32[]{:S(2)}, u32[]{:S(2)}) collective-permute-start(bf16[128,320]{1,0:T(8,128)(2,1)S(1)} %get-tuple-element.86), channel_id=1, source_target_pairs={{0,16},{8,24},{16,0},{24,8},{32,48},{40,56},{48,32},{56,40},{64,80... | collective-permute-start | bytes 245768 | tf_op jit(solution)/shard_map/ppermute | solution.py:388
  43.8 13.1 %collective-permute-start.15 = (bf16[128,320]{1,0:T(8,128)(2,1)S(1)}, bf16[128,320]{1,0:T(8,128)(2,1)S(1)}, u32[]{:S(2)}, u32[]{:S(2)}) collective-permute-start(bf16[128,320]{1,0:T(8,128)(2,1)S(1)} %get-tuple-element.87), channel_id=1, source_target_pairs={{0,24},{8,16},{16,8},{24,0},{32,56},{40,48},{48,40},{56,32},{64,88... | collective-permute-start | bytes 245768 | tf_op jit(solution)/shard_map/ppermute | solution.py:388
  51.2 6.6 %collective-permute-start.9 = (bf16[128,320]{1,0:T(8,128)(2,1)S(1)}, bf16[128,320]{1,0:T(8,128)(2,1)S(1)}, u32[]{:S(2)}, u32[]{:S(2)}) collective-permute-start(bf16[128,320]{1,0:T(8,128)(2,1)S(1)} %get-tuple-element.76), channel_id=1, source_target_pairs={{0,8},{8,0},{16,24},{24,16},{32,40},{40,32},{48,56},{56,48},{64,72... | collective-permute-start | bytes 245768 | tf_op jit(solution)/shard_map/ppermute | solution.py:388
  53.6 5.9 %collective-permute-start.10 = (bf16[128,320]{1,0:T(8,128)(2,1)S(1)}, bf16[128,320]{1,0:T(8,128)(2,1)S(1)}, u32[]{:S(2)}, u32[]{:S(2)}) collective-permute-start(bf16[128,320]{1,0:T(8,128)(2,1)S(1)} %get-tuple-element.77), channel_id=1, source_target_pairs={{0,16},{8,24},{16,0},{24,8},{32,48},{40,56},{48,32},{56,40},{64,80... | collective-permute-start | bytes 245768 | tf_op jit(solution)/shard_map/ppermute | solution.py:388
  53.7 8.1 %collective-permute-start.11 = (bf16[128,320]{1,0:T(8,128)(2,1)S(1)}, bf16[128,320]{1,0:T(8,128)(2,1)S(1)}, u32[]{:S(2)}, u32[]{:S(2)}) collective-permute-start(bf16[128,320]{1,0:T(8,128)(2,1)S(1)} %get-tuple-element.78), channel_id=1, source_target_pairs={{0,24},{8,16},{16,8},{24,0},{32,56},{40,48},{48,40},{56,32},{64,88... | collective-permute-start | bytes 245768 | tf_op jit(solution)/shard_map/ppermute | solution.py:388

commit v5 on v4

--- a/solution.py
+++ b/solution.py
@@ -96,6 +96,17 @@
         )
 
 
+def fold(dst, value):
+    dst[0:128] = value[:, 0:128]
+    dst[128:256] = value[:, 128:256]
+    dst[256:320] = jnp.concatenate([value[0:64, 256:], value[64:128, 256:]], axis=1)
+
+
+def unfold(value):
+    rest = jnp.concatenate([value[256:320, 0:64], value[256:320, 64:128]], axis=0)
+    return jnp.concatenate([value[0:128], value[128:256], rest], axis=1)
+
+
 def hand_out(me, normed, keep, give):
     keep[0] = normed[me]
     keep[1] = normed[me ^ 2]
@@ -127,8 +138,9 @@
             put(merged, m, f, fbuf[f, m].astype(F32) + cbuf[f, m].astype(F32))
         rows[m] = taken(merged, m).astype(BF)
     facing = jnp.where(odd_band(), 6, 0)
-    one[...] = rows[pl.ds(facing, 2)]
-    two[...] = rows[pl.ds(6 - facing, 2)]
+    for i in range(2):
+        fold(one.at[i], rows[facing + i])
+        fold(two.at[i], rows[6 - facing + i])
     loads[2].wait()
     arrange(wide, buf)
 
@@ -197,7 +209,7 @@
     for y in range(4):
         value = combine(prod, y) + rows[y + 2].astype(F32)
         flat[y] = value
-        normed[y] = layer_norm(value, gain)
+        fold(normed.at[y], layer_norm(value, gain))
     hand_out(me, normed, keep, give)
 
 
@@ -217,8 +229,8 @@
     odd = odd_band()
     embed = vectors[0:1]
     gain = vectors[1:2]
-    low = [jnp.where(odd, two[y], one[y]) for y in range(2)]
-    high = [jnp.where(odd, one[y], two[y]) for y in range(2)]
+    low = [unfold(jnp.where(odd, two[y], one[y])) for y in range(2)]
+    high = [unfold(jnp.where(odd, one[y], two[y])) for y in range(2)]
     rows = low + [merged[0], merged[1], merged[6], merged[7]] + high
     starts = (0, 1, 4, 5)
     for m in range(8):
@@ -240,7 +252,7 @@
     for y in range(4):
         value = combine(prod, y) + merged[(0, 1, 6, 7)[y]].astype(F32)
         flat[y] = value
-        normed[y] = layer_norm(value, gain)
+        fold(normed.at[y], layer_norm(value, gain))
     hand_out(me, normed, keep, give)
     bias_table(bias, rel_bias, reach)
     for load in loads:
@@ -266,10 +278,10 @@
         block = me ^ k
         own = (near, across_x)[k // 2]
         at = pl.multiple_of(16 + 8 * block, 8)
-        field[:, pl.ds(at, 8), :] = own[k % 2].astype(F32).reshape(pixels, 8, 320)
+        field[:, pl.ds(at, 8), :] = unfold(own[k % 2].astype(F32)).reshape(pixels, 8, 320)
         halo = (near_z, across_z)[k // 2]
         at = pl.multiple_of(jnp.where(block >= 2, 8 * block - 16, 48 + 8 * block), 8)
-        field[:, pl.ds(at, 8), :] = halo[k % 2].astype(F32).reshape(pixels, 8, 320)
+        field[:, pl.ds(at, 8), :] = unfold(halo[k % 2].astype(F32)).reshape(pixels, 8, 320)
 
     def project(x, i):
         return jnp.dot(x, weights[i], preferred_element_type=F32).astype(BF)
@@ -340,7 +352,7 @@
     each(softmax)
     each(attended)
     for k, out in enumerate((out0, out1, out2, out3)):
-        out[...] = project(back[me ^ k].reshape(pixels * 8, 320).astype(BF), 3)
+        fold(out, project(back[me ^ k].reshape(pixels * 8, 320).astype(BF), 3))
 
 
 def final_kernel(first_row, second_row, *refs):
@@ -351,7 +363,7 @@
     for k, a in enumerate((a0, a1, a2, a3)):
         q = me ^ k
         row = jnp.where(q >= 2, second_row + q - 2, first_row + q)
-        value = a[...].astype(F32) + flat[q]
+        value = unfold(a[...].astype(F32)) + flat[q]
         rest = jnp.concatenate([value[:, 256:], jnp.zeros((128, 64), F32)], axis=1)
         for j, part in enumerate((value[:, :128], value[:, 128:256], rest)):
             total[k, j] = part
@@ -393,7 +405,7 @@
 
     def params(mebibytes):
         return pltpu.CompilerParams(vmem_limit_bytes=mebibytes * MIB)
-    pair = jax.ShapeDtypeStruct((2, 128, 320), BF)
+    pair = jax.ShapeDtypeStruct((2, 320, 128), BF)
     chunk = pltpu.VMEM((4, 128, 320), F32)
 
     def cost(flops):
@@ -408,7 +420,7 @@
     rows_scratch = [
         pltpu.VMEM((4, 128, 960), BF),
         pltpu.VMEM((768, 960), F32),
-        pltpu.VMEM((4, 128, 320), BF),
+        pltpu.VMEM((4, 320, 128), BF),
     ]
     wide = pltpu.VMEM((960, 960), BF)
     one, two, merged, wide1 = pl.pallas_call(
@@ -500,7 +512,7 @@
     z_out = exchange(near_out, beside, 0)
 
     def attend(fields):
-        piece = jax.ShapeDtypeStruct((128, 320), BF)
+        piece = jax.ShapeDtypeStruct((320, 128), BF)
         outs = pl.pallas_call(
             attend_kernel,
             in_specs=[vmem] * 6,

time: 63.1 us -> 59.8 us (0.948)
  waiting for transfers between devices: 10.4 us -> 7.52 us
  starting transfers between devices: 30.2 us -> 29.2 us
  Pallas kernels: 21.3 us -> 22 us
    ppermute x14, waiting for transfers between devices: 10.4 us -> 7.51 us  [exchange(): return lax.ppermute(x, 'frame', [(i, to(i, k)) for i in range(count)])]
    ppermute x14, starting transfers between devices: 24.8 us -> 23.8 us  [exchange(): return lax.ppermute(x, 'frame', [(i, to(i, k)) for i in range(count)])]
  transfers between devices with their start and end apart: 16 -> 16, of which waited for: 6 -> 6; matrix products, arithmetic and copies ran while one was open for 0% -> 0% of each run, Pallas kernels for 28% -> 31%
where the time goes in v5:
time: 59.8 us; the launch traced here: 59.6 us
  starting transfers between devices  29.2 us (49%)
  Pallas kernels  22 us (37%)
  waiting for transfers between devices  7.52 us (13%)
  between operations  0.93 us (2%)
    ppermute x14, starting transfers between devices, exchange(): return lax.ppermute(x, 'frame', [(i, to(i, k)) for i in range(count)])  23.8 us
    ppermute x14, waiting for transfers between devices, exchange(): return lax.ppermute(x, 'frame', [(i, to(i, k)) for i in range(count)])  7.51 us
    pallas_call x2, Pallas kernels, attend(): pl.pallas_call(attend_kernel, in_specs=[vmem] * 6, out_specs=[vmem] * 4,...  6.48 us
    pallas_call x1, Pallas kernels, shards(): pl.pallas_call(inner_kernel, in_specs=[smem] + [vmem] * 2 + [anywhere] *...  5.6 us
    pallas_call x1, Pallas kernels, shards(): pl.pallas_call(outer_kernel, in_specs=[smem] + [vmem] * 8 + [anywhere] *...  5.1 us
    ppermute x1, starting transfers between devices, shards(): two = lax.ppermute(two, 'band', swaps(0))  4.75 us
    pallas_call x1, Pallas kernels, shards(): pl.pallas_call(merge_kernel, in_specs=[anywhere] * 3, out_specs=[vmem] *...  2.55 us
    pallas_call x2, Pallas kernels, finish(): pl.pallas_call(body, in_specs=[vmem] * 5 + [anywhere] * len(before), out_...  2.2 us
  transfers between devices with their start and end apart: 16, of which 6 were waited for; matrix products, arithmetic and copies ran while one was open for 0% of the time, Pallas kernels for 31%

profile of v5, /device:TPU:1, one launch (start us, length us, event | category | flops | bytes accessed | tf_op | source)
XLA Modules:
  0.0 59.6 jit_solution(16186011021995869016)
XLA Ops:
  0.0 2.5 %merge.1 = (bf16[2,320,128]{2,1,0:T(8,128)(2,1)S(1)}, bf16[2,320,128]{2,1,0:T(8,128)(2,1)S(1)}, bf16[8,128,320]{2,1,0:T(8,128)(2,1)S(1)}, bf16[960,960]{1,0:T(8,128)(2,1)S(1)}) custom-call(bf16[8,8,16,320]{3,2,1,0:T(8,128)(2,1)} %frames.1, bf16[8,8,16,320]{3,2,1,0:T(8,128)(2,1)} %control.1, bf16[3,3,320,320]{3,2,1,0:T(8,128)(2,1)} %first.1), custom_call_target="tpu_custom_call" | custom-call | tf_op jit(solution)/shard_map/merge/pallas_call | solution.py:426
  2.6 0.7 %collective-permute-start = (bf16[2,320,128]{2,1,0:T(8,128)(2,1)S(1)}, bf16[2,320,128]{2,1,0:T(8,128)(2,1)S(1)}, u32[]{:S(2)}, u32[]{:S(2)}) collective-permute-start(bf16[2,320,128]{2,1,0:T(8,128)(2,1)S(1)} %get-tuple-element.54), channel_id=1, source_target_pairs={{1,2},{3,4},{5,6},{2,1},{4,3},{6,5},{9,10},{11,12},{13,14},{10,9},... | collective-permute-start | bytes 491528 | tf_op jit(solution)/shard_map/ppermute | solution.py:442
  3.2 4.7 %collective-permute-start.1 = (bf16[2,320,128]{2,1,0:T(8,128)(2,1)S(1)}, bf16[2,320,128]{2,1,0:T(8,128)(2,1)S(1)}, u32[]{:S(2)}, u32[]{:S(2)}) collective-permute-start(bf16[2,320,128]{2,1,0:T(8,128)(2,1)S(1)} %get-tuple-element.55), channel_id=1, source_target_pairs={{0,1},{2,3},{4,5},{6,7},{1,0},{3,2},{5,4},{7,6},{8,9},{10,11},{12,... | collective-permute-start | bytes 491528 | tf_op jit(solution)/shard_map/ppermute | solution.py:443
  8.6 0.0 copy-start
  8.6 0.0 copy-start.1
  8.7 5.6 %inner_rows.1 = (bf16[2,320,128]{2,1,0:T(8,128)(2,1)S(1)}, bf16[2,320,128]{2,1,0:T(8,128)(2,1)S(1)}, f32[4,128,320]{2,1,0:T(8,128)S(1)}, bf16[4,128,320]{2,1,0:T...) custom-call(s32[1]{0:T(128)S(6)} %copy.16.step, ...), custom_call_target="tpu_custom_call" | custom-call | tf_op jit(solution)/shard_map/inner_rows/pallas_call | solution.py:445
  14.3 0.0 collective-permute-done.one
  14.3 0.0 collective-permute-done.1.two
  14.3 1.3 %collective-permute-start.2 = (bf16[2,320,128]{2,1,0:T(8,128)(2,1)S(1)}, bf16[2,320,128]{2,1,0:T(8,128)(2,1)S(1)}, u32[]{:S(2)}, u32[]{:S(2)}) collective-permute-start(bf16[2,320,128]{2,1,0:T(8,128)(2,1)S(1)} %get-tuple-element.59), channel_id=1, source_target_pairs={{0,8},{8,0},{16,24},{24,16},{32,40},{40,32},{48,56},{56,48},{64,72... | collective-permute-start | bytes 491528 | tf_op jit(solution)/shard_map/ppermute | solution.py:400
  15.6 1.0 %collective-permute-done.2.got = bf16[2,320,128]{2,1,0:T(8,128)(2,1)S(1)} collective-permute-done((bf16[2,320,128]{2,1,0:T(8,128)(2,1)S(1)}, bf16[2,320,128]{2,1,0:T(8,128)(2,1)S(1)}, u32[]{:S(2)}, u32[]{:S(2)}) %collective-permute-start.2) | collective-permute-done | bytes 163872 | tf_op jit(solution)/shard_map/ppermute | solution.py:400
  16.7 2.8 %collective-permute-start.3 = (bf16[2,320,128]{2,1,0:T(8,128)(2,1)S(1)}, bf16[2,320,128]{2,1,0:T(8,128)(2,1)S(1)}, u32[]{:S(2)}, u32[]{:S(2)}) collective-permute-start(bf16[2,320,128]{2,1,0:T(8,128)(2,1)S(1)} %get-tuple-element.67), channel_id=1, source_target_pairs={{0,16},{8,24},{16,0},{24,8},{32,48},{40,56},{48,32},{56,40},{64,80... | collective-permute-start | bytes 491528 | tf_op jit(solution)/shard_map/ppermute | solution.py:400
  19.5 5.6 %collective-permute-start.4 = (bf16[2,320,128]{2,1,0:T(8,128)(2,1)S(1)}, bf16[2,320,128]{2,1,0:T(8,128)(2,1)S(1)}, u32[]{:S(2)}, u32[]{:S(2)}) collective-permute-start(bf16[2,320,128]{2,1,0:T(8,128)(2,1)S(1)} %get-tuple-element.80.near), channel_id=1, source_target_pairs={{0,224},{8,232},{16,48},{24,56},{32,0},{40,8},{48,80},{56,88},{64,... | collective-permute-start | bytes 491528 | tf_op jit(solution)/shard_map/ppermute | solution.py:400
  25.1 0.0 copy-done
  25.1 0.0 copy-done.1
  25.1 5.1 %outer_rows.1 = (bf16[2,320,128]{2,1,0:T(8,128)(2,1)S(1)}, bf16[2,320,128]{2,1,0:T(8,128)(2,1)S(1)}, f32[4,128,320]{2,1,0:T(8,128)S(1)}, bf16[4,320,320]{2,1,0:T(8,128)(2,1)S(1)}, f32[64,256]{1,0:T(8,128)S(1)}) custom-call(s32[256]{0:T(256)S(1)} %copy-done.1, bf16[2,320,128]{2,1,0:T(8,128)(2,1)S(1)} %collective-permute-done.one, ...), custom_call_target="tpu_custom_call" | custom-call | tf_op jit(solution)/shard_map/outer_rows/pallas_call | solution.py:488
  30.2 0.0 collective-permute-done.3.across_x
  30.2 0.0 collective-permute-done.4.near_z
  30.2 1.0 %collective-permute-start.5 = (bf16[2,320,128]{2,1,0:T(8,128)(2,1)S(1)}, bf16[2,320,128]{2,1,0:T(8,128)(2,1)S(1)}, u32[]{:S(2)}, u32[]{:S(2)}) collective-permute-start(bf16[2,320,128]{2,1,0:T(8,128)(2,1)S(1)} %get-tuple-element.68), channel_id=1, source_target_pairs={{0,8},{8,0},{16,24},{24,16},{32,40},{40,32},{48,56},{56,48},{64,72... | collective-permute-start | bytes 491528 | tf_op jit(solution)/shard_map/ppermute | solution.py:400
  31.2 0.0 collective-permute-start.12
  31.2 1.0 %collective-permute-done.5.got = bf16[2,320,128]{2,1,0:T(8,128)(2,1)S(1)} collective-permute-done((bf16[2,320,128]{2,1,0:T(8,128)(2,1)S(1)}, bf16[2,320,128]{2,1,0:T(8,128)(2,1)S(1)}, u32[]{:S(2)}, u32[]{:S(2)}) %collective-permute-start.5) | collective-permute-done | bytes 163872 | tf_op jit(solution)/shard_map/ppermute | solution.py:400
  32.3 1.8 %collective-permute-start.7 = (bf16[2,320,128]{2,1,0:T(8,128)(2,1)S(1)}, bf16[2,320,128]{2,1,0:T(8,128)(2,1)S(1)}, u32[]{:S(2)}, u32[]{:S(2)}) collective-permute-start(bf16[2,320,128]{2,1,0:T(8,128)(2,1)S(1)} %get-tuple-element.71.near), channel_id=1, source_target_pairs={{0,224},{8,232},{16,48},{24,56},{32,0},{40,8},{48,80},{56,88},{64,... | collective-permute-start | bytes 491528 | tf_op jit(solution)/shard_map/ppermute | solution.py:400
  34.0 1.7 %collective-permute-start.8 = (bf16[2,320,128]{2,1,0:T(8,128)(2,1)S(1)}, bf16[2,320,128]{2,1,0:T(8,128)(2,1)S(1)}, u32[]{:S(2)}, u32[]{:S(2)}) collective-permute-start(bf16[2,320,128]{2,1,0:T(8,128)(2,1)S(1)} %get-tuple-element.72), channel_id=1, source_target_pairs={{0,240},{8,248},{16,32},{24,40},{32,16},{40,24},{48,64},{56,72},{6... | collective-permute-start | bytes 491528 | tf_op jit(solution)/shard_map/ppermute | solution.py:400
  35.7 0.8 %collective-permute-start.6 = (bf16[2,320,128]{2,1,0:T(8,128)(2,1)S(1)}, bf16[2,320,128]{2,1,0:T(8,128)(2,1)S(1)}, u32[]{:S(2)}, u32[]{:S(2)}) collective-permute-start(bf16[2,320,128]{2,1,0:T(8,128)(2,1)S(1)} %get-tuple-element.72), channel_id=1, source_target_pairs={{0,16},{8,24},{16,0},{24,8},{32,48},{40,56},{48,32},{56,40},{64,80... | collective-permute-start | bytes 491528 | tf_op jit(solution)/shard_map/ppermute | solution.py:400
  36.5 1.7 %collective-permute-done.12.across_z = bf16[2,320,128]{2,1,0:T(8,128)(2,1)S(1)} collective-permute-done((bf16[2,320,128]{2,1,0:T(8,128)(2,1)S(1)}, bf16[2,320,128]{2,1,0:T(8,128)(2,1)S(1)}, u32[]{:S(2)}, u32[]{:S(2)}) %collective-permute-start.12) | collective-permute-done | bytes 163872 | tf_op jit(solution)/shard_map/ppermute | solution.py:400
  38.2 3.2 %attend.3 = (bf16[320,128]{1,0:T(8,128)(2,1)S(1)}, bf16[320,128]{1,0:T(8,128)(2,1)S(1)}, bf16[320,128]{1,0:T(8,128)(2,1)S(1)}, bf16[320,128]{1,0:T(8,128)(2,1)S(1)}) custom-call(bf16[2,320,128]{2,1,0:T(8,128)(2,1)S(1)} %get-tuple-element.80.near, bf16[2,320,128]{2,1,0:T(8,128)(2,1)S(1)} %collective-permute-done.3.across_x, ...), custom_call_target="tpu_custom_call" | custom-call | tf_op jit(solution)/shard_map/attend/pallas_call | solution.py:516
  41.4 0.9 %collective-permute-start.13 = (bf16[320,128]{1,0:T(8,128)(2,1)S(1)}, bf16[320,128]{1,0:T(8,128)(2,1)S(1)}, u32[]{:S(2)}, u32[]{:S(2)}) collective-permute-start(bf16[320,128]{1,0:T(8,128)(2,1)S(1)} %get-tuple-element.85), channel_id=1, source_target_pairs={{0,8},{8,0},{16,24},{24,16},{32,40},{40,32},{48,56},{56,48},{64,72... | collective-permute-start | bytes 245768 | tf_op jit(solution)/shard_map/ppermute | solution.py:400
  42.3 0.8 %collective-permute-start.14 = (bf16[320,128]{1,0:T(8,128)(2,1)S(1)}, bf16[320,128]{1,0:T(8,128)(2,1)S(1)}, u32[]{:S(2)}, u32[]{:S(2)}) collective-permute-start(bf16[320,128]{1,0:T(8,128)(2,1)S(1)} %get-tuple-element.86), channel_id=1, source_target_pairs={{0,16},{8,24},{16,0},{24,8},{32,48},{40,56},{48,32},{56,40},{64,80... | collective-permute-start | bytes 245768 | tf_op jit(solution)/shard_map/ppermute | solution.py:400
  43.1 0.0 collective-permute-done.7.near_z
  43.1 2.5 %collective-permute-start.15 = (bf16[320,128]{1,0:T(8,128)(2,1)S(1)}, bf16[320,128]{1,0:T(8,128)(2,1)S(1)}, u32[]{:S(2)}, u32[]{:S(2)}) collective-permute-start(bf16[320,128]{1,0:T(8,128)(2,1)S(1)} %get-tuple-element.87), channel_id=1, source_target_pairs={{0,24},{8,16},{16,8},{24,0},{32,56},{40,48},{48,40},{56,32},{64,88... | collective-permute-start | bytes 245768 | tf_op jit(solution)/shard_map/ppermute | solution.py:400
  45.6 0.0 collective-permute-done.8.across_z
  45.6 0.7 %collective-permute-done.6.across_x = bf16[2,320,128]{2,1,0:T(8,128)(2,1)S(1)} collective-permute-done((bf16[2,320,128]{2,1,0:T(8,128)(2,1)S(1)}, bf16[2,320,128]{2,1,0:T(8,128)(2,1)S(1)}, u32[]{:S(2)}, u32[]{:S(2)}) %collective-permute-start.6) | collective-permute-done | bytes 163872 | tf_op jit(solution)/shard_map/ppermute | solution.py:400
  46.3 3.2 %attend.2 = (bf16[320,128]{1,0:T(8,128)(2,1)S(1)}, bf16[320,128]{1,0:T(8,128)(2,1)S(1)}, bf16[320,128]{1,0:T(8,128)(2,1)S(1)}, bf16[320,128]{1,0:T(8,128)(2,1)S(1)}) custom-call(bf16[2,320,128]{2,1,0:T(8,128)(2,1)S(1)} %get-tuple-element.71.near, bf16[2,320,128]{2,1,0:T(8,128)(2,1)S(1)} %collective-permute-done.6.across_x, ...), custom_call_target="tpu_custom_call" | custom-call | tf_op jit(solution)/shard_map/attend/pallas_call | solution.py:516
  49.5 1.4 %collective-permute-start.9 = (bf16[320,128]{1,0:T(8,128)(2,1)S(1)}, bf16[320,128]{1,0:T(8,128)(2,1)S(1)}, u32[]{:S(2)}, u32[]{:S(2)}) collective-permute-start(bf16[320,128]{1,0:T(8,128)(2,1)S(1)} %get-tuple-element.76), channel_id=1, source_target_pairs={{0,8},{8,0},{16,24},{24,16},{32,40},{40,32},{48,56},{56,48},{64,72... | collective-permute-start | bytes 245768 | tf_op jit(solution)/shard_map/ppermute | solution.py:400
  50.9 0.6 %collective-permute-start.10 = (bf16[320,128]{1,0:T(8,128)(2,1)S(1)}, bf16[320,128]{1,0:T(8,128)(2,1)S(1)}, u32[]{:S(2)}, u32[]{:S(2)}) collective-permute-start(bf16[320,128]{1,0:T(8,128)(2,1)S(1)} %get-tuple-element.77), channel_id=1, source_target_pairs={{0,16},{8,24},{16,0},{24,8},{32,48},{40,56},{48,32},{56,40},{64,80... | collective-permute-start | bytes 245768 | tf_op jit(solution)/shard_map/ppermute | solution.py:400
  51.5 0.0 collective-permute-done.13.refs_1_
  51.5 2.6 %collective-permute-start.11 = (bf16[320,128]{1,0:T(8,128)(2,1)S(1)}, bf16[320,128]{1,0:T(8,128)(2,1)S(1)}, u32[]{:S(2)}, u32[]{:S(2)}) collective-permute-start(bf16[320,128]{1,0:T(8,128)(2,1)S(1)} %get-tuple-element.78), channel_id=1, source_target_pairs={{0,24},{8,16},{16,8},{24,0},{32,56},{40,48},{48,40},{56,32},{64,88... | collective-permute-start | bytes 245768 | tf_op jit(solution)/shard_map/ppermute | solution.py:400
  54.2 0.0 collective-permute-done.14.refs_2_
  54.2 0.0 collective-permute-done.15.refs_3_
  54.2 1.1 %project_out.2.refs_5_ = f32[8,8,16,320]{3,2,1,0:T(8,128)} custom-call(bf16[320,128]{1,0:T(8,128)(2,1)S(1)} %get-tuple-element.84.refs_0_, bf16[320,128]{1,0:T(8,128)(2,1)S(1)} %collective-permute-done.13.refs_1_, bf16[320,128]{1,0:T(8,128)(2,1)S(1)} %collective-permute-done.14.refs_2_, bf16[320,128]{1,0:T(8,128)(2,1)S(1)} %collective-permute-done.15.refs_3_, ...), custom_call_target="tpu_custom_call" | custom-call | tf_op jit(solution)/shard_map/project_out/pallas_call | solution.py:545
  55.3 0.0 collective-permute-done.9.refs_1_
  55.3 1.1 %collective-permute-done.10.refs_2_ = bf16[320,128]{1,0:T(8,128)(2,1)S(1)} collective-permute-done((bf16[320,128]{1,0:T(8,128)(2,1)S(1)}, bf16[320,128]{1,0:T(8,128)(2,1)S(1)}, u32[]{:S(2)}, u32[]{:S(2)}) %collective-permute-start.10) | collective-permute-done | bytes 81952 | tf_op jit(solution)/shard_map/ppermute | solution.py:400
  56.4 1.9 %collective-permute-done.11.refs_3_ = bf16[320,128]{1,0:T(8,128)(2,1)S(1)} collective-permute-done((bf16[320,128]{1,0:T(8,128)(2,1)S(1)}, bf16[320,128]{1,0:T(8,128)(2,1)S(1)}, u32[]{:S(2)}, u32[]{:S(2)}) %collective-permute-start.11) | collective-permute-done | bytes 81952 | tf_op jit(solution)/shard_map/ppermute | solution.py:400
  58.4 1.1 %project_out.3 = f32[8,8,16,320]{3,2,1,0:T(8,128)} custom-call(bf16[320,128]{1,0:T(8,128)(2,1)S(1)} %get-tuple-element.75.refs_0_, bf16[320,128]{1,0:T(8,128)(2,1)S(1)} %collective-permute-done.9.refs_1_, bf16[320,128]{1,0:T(8,128)(2,1)S(1)} %collective-permute-done.10.refs_2_, ...), custom_call_target="tpu_custom_call", output_to_operand_aliasing={{}: (5, {})} | custom-call | tf_op jit(solution)/shard_map/project_out/pallas_call | solution.py:545
  (2 shorter events, 0.0 us)
Async XLA Ops:
  2.6 11.7 %collective-permute-start = (bf16[2,320,128]{2,1,0:T(8,128)(2,1)S(1)}, bf16[2,320,128]{2,1,0:T(8,128)(2,1)S(1)}, u32[]{:S(2)}, u32[]{:S(2)}) collective-permute-start(bf16[2,320,128]{2,1,0:T(8,128)(2,1)S(1)} %get-tuple-element.54), channel_id=1, source_target_pairs={{1,2},{3,4},{5,6},{2,1},{4,3},{6,5},{9,10},{11,12},{13,14},{10,9},... | collective-permute-start | bytes 491528 | tf_op jit(solution)/shard_map/ppermute | solution.py:442
  3.2 11.0 %collective-permute-start.1 = (bf16[2,320,128]{2,1,0:T(8,128)(2,1)S(1)}, bf16[2,320,128]{2,1,0:T(8,128)(2,1)S(1)}, u32[]{:S(2)}, u32[]{:S(2)}) collective-permute-start(bf16[2,320,128]{2,1,0:T(8,128)(2,1)S(1)} %get-tuple-element.55), channel_id=1, source_target_pairs={{0,1},{2,3},{4,5},{6,7},{1,0},{3,2},{5,4},{7,6},{8,9},{10,11},{12,... | collective-permute-start | bytes 491528 | tf_op jit(solution)/shard_map/ppermute | solution.py:443
  8.6 16.4 %copy-start = (f32[8,33]{1,0:T(8,128)S(1)}, f32[8,33]{1,0:T(8,128)}, u32[]{:S(2)}) copy-start(f32[8,33]{1,0:T(8,128)} %rel_bias.1) | copy-start | bytes 3172
  8.6 16.4 %copy-start.1 = (s32[256]{0:T(256)S(1)}, s32[256]{0:T(256)}, u32[]{:S(2)}) copy-start(s32[256]{0:T(256)} %reach.1) | copy-start | bytes 3076
  14.3 2.4 %collective-permute-start.2 = (bf16[2,320,128]{2,1,0:T(8,128)(2,1)S(1)}, bf16[2,320,128]{2,1,0:T(8,128)(2,1)S(1)}, u32[]{:S(2)}, u32[]{:S(2)}) collective-permute-start(bf16[2,320,128]{2,1,0:T(8,128)(2,1)S(1)} %get-tuple-element.59), channel_id=1, source_target_pairs={{0,8},{8,0},{16,24},{24,16},{32,40},{40,32},{48,56},{56,48},{64,72... | collective-permute-start | bytes 491528 | tf_op jit(solution)/shard_map/ppermute | solution.py:400
  16.7 13.5 %collective-permute-start.3 = (bf16[2,320,128]{2,1,0:T(8,128)(2,1)S(1)}, bf16[2,320,128]{2,1,0:T(8,128)(2,1)S(1)}, u32[]{:S(2)}, u32[]{:S(2)}) collective-permute-start(bf16[2,320,128]{2,1,0:T(8,128)(2,1)S(1)} %get-tuple-element.67), channel_id=1, source_target_pairs={{0,16},{8,24},{16,0},{24,8},{32,48},{40,56},{48,32},{56,40},{64,80... | collective-permute-start | bytes 491528 | tf_op jit(solution)/shard_map/ppermute | solution.py:400
  19.5 10.7 %collective-permute-start.4 = (bf16[2,320,128]{2,1,0:T(8,128)(2,1)S(1)}, bf16[2,320,128]{2,1,0:T(8,128)(2,1)S(1)}, u32[]{:S(2)}, u32[]{:S(2)}) collective-permute-start(bf16[2,320,128]{2,1,0:T(8,128)(2,1)S(1)} %get-tuple-element.80.near), channel_id=1, source_target_pairs={{0,224},{8,232},{16,48},{24,56},{32,0},{40,8},{48,80},{56,88},{64,... | collective-permute-start | bytes 491528 | tf_op jit(solution)/shard_map/ppermute | solution.py:400
  30.2 2.0 %collective-permute-start.5 = (bf16[2,320,128]{2,1,0:T(8,128)(2,1)S(1)}, bf16[2,320,128]{2,1,0:T(8,128)(2,1)S(1)}, u32[]{:S(2)}, u32[]{:S(2)}) collective-permute-start(bf16[2,320,128]{2,1,0:T(8,128)(2,1)S(1)} %get-tuple-element.68), channel_id=1, source_target_pairs={{0,8},{8,0},{16,24},{24,16},{32,40},{40,32},{48,56},{56,48},{64,72... | collective-permute-start | bytes 491528 | tf_op jit(solution)/shard_map/ppermute | solution.py:400
  31.2 7.0 %collective-permute-start.12 = (bf16[2,320,128]{2,1,0:T(8,128)(2,1)S(1)}, bf16[2,320,128]{2,1,0:T(8,128)(2,1)S(1)}, u32[]{:S(2)}, u32[]{:S(2)}) collective-permute-start(bf16[2,320,128]{2,1,0:T(8,128)(2,1)S(1)} %collective-permute-done.3.across_x), channel_id=1, source_target_pairs={{0,32},{8,40},{16,240},{24,248},{32,64},{40,72},{48,16},{56,24},{6... | collective-permute-start | bytes 491528 | tf_op jit(solution)/shard_map/ppermute | solution.py:400
  32.3 10.8 %collective-permute-start.7 = (bf16[2,320,128]{2,1,0:T(8,128)(2,1)S(1)}, bf16[2,320,128]{2,1,0:T(8,128)(2,1)S(1)}, u32[]{:S(2)}, u32[]{:S(2)}) collective-permute-start(bf16[2,320,128]{2,1,0:T(8,128)(2,1)S(1)} %get-tuple-element.71.near), channel_id=1, source_target_pairs={{0,224},{8,232},{16,48},{24,56},{32,0},{40,8},{48,80},{56,88},{64,... | collective-permute-start | bytes 491528 | tf_op jit(solution)/shard_map/ppermute | solution.py:400
  34.0 11.6 %collective-permute-start.8 = (bf16[2,320,128]{2,1,0:T(8,128)(2,1)S(1)}, bf16[2,320,128]{2,1,0:T(8,128)(2,1)S(1)}, u32[]{:S(2)}, u32[]{:S(2)}) collective-permute-start(bf16[2,320,128]{2,1,0:T(8,128)(2,1)S(1)} %get-tuple-element.72), channel_id=1, source_target_pairs={{0,240},{8,248},{16,32},{24,40},{32,16},{40,24},{48,64},{56,72},{6... | collective-permute-start | bytes 491528 | tf_op jit(solution)/shard_map/ppermute | solution.py:400
  35.7 10.6 %collective-permute-start.6 = (bf16[2,320,128]{2,1,0:T(8,128)(2,1)S(1)}, bf16[2,320,128]{2,1,0:T(8,128)(2,1)S(1)}, u32[]{:S(2)}, u32[]{:S(2)}) collective-permute-start(bf16[2,320,128]{2,1,0:T(8,128)(2,1)S(1)} %get-tuple-element.72), channel_id=1, source_target_pairs={{0,16},{8,24},{16,0},{24,8},{32,48},{40,56},{48,32},{56,40},{64,80... | collective-permute-start | bytes 491528 | tf_op jit(solution)/shard_map/ppermute | solution.py:400
  41.4 10.1 %collective-permute-start.13 = (bf16[320,128]{1,0:T(8,128)(2,1)S(1)}, bf16[320,128]{1,0:T(8,128)(2,1)S(1)}, u32[]{:S(2)}, u32[]{:S(2)}) collective-permute-start(bf16[320,128]{1,0:T(8,128)(2,1)S(1)} %get-tuple-element.85), channel_id=1, source_target_pairs={{0,8},{8,0},{16,24},{24,16},{32,40},{40,32},{48,56},{56,48},{64,72... | collective-permute-start | bytes 245768 | tf_op jit(solution)/shard_map/ppermute | solution.py:400
  42.3 11.8 %collective-permute-start.14 = (bf16[320,128]{1,0:T(8,128)(2,1)S(1)}, bf16[320,128]{1,0:T(8,128)(2,1)S(1)}, u32[]{:S(2)}, u32[]{:S(2)}) collective-permute-start(bf16[320,128]{1,0:T(8,128)(2,1)S(1)} %get-tuple-element.86), channel_id=1, source_target_pairs={{0,16},{8,24},{16,0},{24,8},{32,48},{40,56},{48,32},{56,40},{64,80... | collective-permute-start | bytes 245768 | tf_op jit(solution)/shard_map/ppermute | solution.py:400
  43.1 11.1 %collective-permute-start.15 = (bf16[320,128]{1,0:T(8,128)(2,1)S(1)}, bf16[320,128]{1,0:T(8,128)(2,1)S(1)}, u32[]{:S(2)}, u32[]{:S(2)}) collective-permute-start(bf16[320,128]{1,0:T(8,128)(2,1)S(1)} %get-tuple-element.87), channel_id=1, source_target_pairs={{0,24},{8,16},{16,8},{24,0},{32,56},{40,48},{48,40},{56,32},{64,88... | collective-permute-start | bytes 245768 | tf_op jit(solution)/shard_map/ppermute | solution.py:400
  49.5 5.8 %collective-permute-start.9 = (bf16[320,128]{1,0:T(8,128)(2,1)S(1)}, bf16[320,128]{1,0:T(8,128)(2,1)S(1)}, u32[]{:S(2)}, u32[]{:S(2)}) collective-permute-start(bf16[320,128]{1,0:T(8,128)(2,1)S(1)} %get-tuple-element.76), channel_id=1, source_target_pairs={{0,8},{8,0},{16,24},{24,16},{32,40},{40,32},{48,56},{56,48},{64,72... | collective-permute-start | bytes 245768 | tf_op jit(solution)/shard_map/ppermute | solution.py:400
  50.9 5.5 %collective-permute-start.10 = (bf16[320,128]{1,0:T(8,128)(2,1)S(1)}, bf16[320,128]{1,0:T(8,128)(2,1)S(1)}, u32[]{:S(2)}, u32[]{:S(2)}) collective-permute-start(bf16[320,128]{1,0:T(8,128)(2,1)S(1)} %get-tuple-element.77), channel_id=1, source_target_pairs={{0,16},{8,24},{16,0},{24,8},{32,48},{40,56},{48,32},{56,40},{64,80... | collective-permute-start | bytes 245768 | tf_op jit(solution)/shard_map/ppermute | solution.py:400
  51.5 6.8 %collective-permute-start.11 = (bf16[320,128]{1,0:T(8,128)(2,1)S(1)}, bf16[320,128]{1,0:T(8,128)(2,1)S(1)}, u32[]{:S(2)}, u32[]{:S(2)}) collective-permute-start(bf16[320,128]{1,0:T(8,128)(2,1)S(1)} %get-tuple-element.78), channel_id=1, source_target_pairs={{0,24},{8,16},{16,8},{24,0},{32,56},{40,48},{48,40},{56,32},{64,88... | collective-permute-start | bytes 245768 | tf_op jit(solution)/shard_map/ppermute | solution.py:400

commit v6 on v5

--- a/solution.py
+++ b/solution.py
@@ -123,14 +123,32 @@
 
 
 def merge_kernel(
-    frames, control, first, one, two, rows, wide, fbuf, cbuf, buf, merged, sems
+    step, frames, control, table, gain, one, two, rows, vectors,
+    line, column, tail, row, fbuf, cbuf, merged, sems,
 ):
     loads = [
         pltpu.make_async_copy(src, dst, sems.at[i])
-        for i, (src, dst) in enumerate(((frames, fbuf), (control, cbuf), (first, buf)))
+        for i, (src, dst) in enumerate(((frames, fbuf), (control, cbuf), (gain, line)))
     ]
     for load in loads:
         load.start()
+    block = step[0] // 128
+    whole_block = pltpu.make_async_copy(
+        table.at[:, pl.ds(pl.multiple_of(jnp.minimum(block, 6) * 128, 128), 128)],
+        column, sems.at[3],
+    )
+    last_block = pltpu.make_async_copy(
+        table.at[:, pl.ds(896, 104)], tail, sems.at[3]
+    )
+
+    @pl.when(block < 7)
+    def _():
+        whole_block.start()
+
+    @pl.when(block >= 7)
+    def _():
+        last_block.start()
+
     loads[0].wait()
     loads[1].wait()
     for m in range(8):
@@ -141,59 +159,40 @@
     for i in range(2):
         fold(one.at[i], rows[facing + i])
         fold(two.at[i], rows[6 - facing + i])
+
+    @pl.when(block < 7)
+    def _():
+        whole_block.wait()
+        row[...] = column[...].T
+
+    @pl.when(block >= 7)
+    def _():
+        last_block.wait()
+        row[0:104] = tail[...].T
+
+    vectors[0:1] = row[pl.ds(step[0] % 128, 1), :]
     loads[2].wait()
-    arrange(wide, buf)
+    vectors[1:2] = line[...].reshape(1, 320)
 
 
 def inner_kernel(
-    step, rows, wide1, second, table, gain,
-    keep, give, flat, edge, wide2, vectors,
-    line, column, tail, row, buf, taps1, taps2, prod, normed, sems,
+    rows, first, second, vectors,
+    keep, give, flat, edge, wide1, wide2,
+    buf, taps1, taps2, prod, normed, sems,
 ):
     loads = [pltpu.make_async_copy(second.at[i], buf.at[i], sems.at[i]) for i in range(3)]
-    load_gain = pltpu.make_async_copy(gain, line, sems.at[3])
-    me = in_group()
-    block = step[0] // 128
-    whole_block = pltpu.make_async_copy(
-        table.at[:, pl.ds(pl.multiple_of(jnp.minimum(block, 6) * 128, 128), 128)],
-        column, sems.at[4],
-    )
-    last_block = pltpu.make_async_copy(
-        table.at[:, pl.ds(896, 104)], tail, sems.at[4]
-    )
-
-    @pl.when(block < 7)
-    def _():
-        whole_block.start()
-
-    @pl.when(block >= 7)
-    def _():
-        last_block.start()
-
-    load_gain.start()
     for load in loads:
         load.start()
+    me = in_group()
     for m in range(8):
         value = rows[m]
         for dy in range(3):
             if 0 <= m - dy < 6:
                 tapped(taps1, m - dy, dy, value)
+    arrange(wide1, first)
     multiply(prod, taps1, wide1, 6)
 
-    @pl.when(block < 7)
-    def _():
-        whole_block.wait()
-        row[...] = column[...].T
-
-    @pl.when(block >= 7)
-    def _():
-        last_block.wait()
-        row[0:104] = tail[...].T
-
-    embed = row[pl.ds(step[0] % 128, 1), :]
-    vectors[0:1] = embed
-    load_gain.wait()
-    vectors[1:2] = line[...].reshape(1, 320)
+    embed = vectors[0:1]
     gain = vectors[1:2]
     for r in range(6):
         act = silu(combine(prod, r) + embed).astype(BF)
@@ -423,45 +422,43 @@
         pltpu.VMEM((4, 320, 128), BF),
     ]
     wide = pltpu.VMEM((960, 960), BF)
-    one, two, merged, wide1 = pl.pallas_call(
+    one, two, merged, vectors = pl.pallas_call(
         merge_kernel,
-        in_specs=[anywhere] * 3,
+        in_specs=[smem] + [anywhere] * 4,
         out_specs=[vmem] * 4,
-        out_shape=[pair, pair, pltpu.VMEM((8, 128, 320), BF), wide],
-        scratch_shapes=[
-            pltpu.VMEM((8, 8, 16, 320), BF),
-            pltpu.VMEM((8, 8, 16, 320), BF),
-            pltpu.VMEM((3, 3, 320, 320), BF),
-            pltpu.VMEM((3, 8, 128, 128), F32),
-            pltpu.SemaphoreType.DMA((3,)),
-        ],
-        compiler_params=params(8),
-        name="merge",
-    )(*stay(frames, control, conv_first))
-    one, two, step_index = lax.optimization_barrier((one, two, step_index))
-    one = lax.ppermute(one, "band", swaps(1))
-    two = lax.ppermute(two, "band", swaps(0))
-
-    keep, give, flat_in, edge, wide2, vectors = pl.pallas_call(
-        inner_kernel,
-        in_specs=[smem] + [vmem] * 2 + [anywhere] * 3,
-        out_specs=[vmem] * 6,
-        out_shape=[
-            pair, pair, chunk, pltpu.VMEM((4, 128, 320), BF), wide, pltpu.VMEM((2, 320), F32)
-        ],
+        out_shape=[pair, pair, pltpu.VMEM((8, 128, 320), BF), pltpu.VMEM((2, 320), F32)],
         scratch_shapes=[
             pltpu.VMEM((320,), F32),
             pltpu.VMEM((320, 128), F32),
             pltpu.VMEM((320, 104), F32),
             pltpu.VMEM((128, 320), F32),
+            pltpu.VMEM((8, 8, 16, 320), BF),
+            pltpu.VMEM((8, 8, 16, 320), BF),
+            pltpu.VMEM((3, 8, 128, 128), F32),
+            pltpu.SemaphoreType.DMA((4,)),
+        ],
+        compiler_params=params(8),
+        name="merge",
+    )(step_index, *stay(frames, control, time_table.T, norm_gain))
+    one, two, vectors = lax.optimization_barrier((one, two, vectors))
+    one = lax.ppermute(one, "band", swaps(1))
+    two = lax.ppermute(two, "band", swaps(0))
+
+    first = exchange(conv_first, plane, 1)
+    keep, give, flat_in, edge, wide1, wide2 = pl.pallas_call(
+        inner_kernel,
+        in_specs=[vmem] * 2 + [anywhere, vmem],
+        out_specs=[vmem] * 6,
+        out_shape=[pair, pair, chunk, pltpu.VMEM((4, 128, 320), BF), wide, wide],
+        scratch_shapes=[
             pltpu.VMEM((3, 3, 320, 320), BF),
             pltpu.VMEM((6, 128, 960), BF),
         ]
         + rows_scratch
-        + [pltpu.SemaphoreType.DMA((5,))],
+        + [pltpu.SemaphoreType.DMA((3,))],
         compiler_params=params(16),
         name="inner_rows",
-    )(step_index, *near_by(merged, wide1), *stay(conv_second, time_table.T, norm_gain))
+    )(*near_by(merged, first), *stay(conv_second), *near_by(vectors))
 
     keep, give, one, two = lax.optimization_barrier((keep, give, one, two))
 

time: 59.8 us -> 58.9 us (0.985)
  Pallas kernels: 22 us -> 21.1 us
    ppermute x14 -> x15, starting transfers between devices: 23.8 us -> 26.3 us  [exchange(): return lax.ppermute(x, 'frame', [(i, to(i, k)) for i in range(count)])]
    ppermute x1, starting transfers between devices: 4.75 us -> 2.18 us  [shards(): two = lax.ppermute(two, 'band', swaps(0))]
    pallas_call x2, Pallas kernels: 8.15 us -> 7.26 us  [the longest x1 5.24 us: shards(): pl.pallas_call(inner_kernel, in_specs=[vmem] * 2 + [anywhere, vmem], out_...]
    ppermute x14 -> x15, waiting for transfers between devices: 7.51 us -> 7.5 us  [exchange(): return lax.ppermute(x, 'frame', [(i, to(i, k)) for i in range(count)])]
  transfers between devices with their start and end apart: 16 -> 17, of which waited for: 6 -> 6; matrix products, arithmetic and copies ran while one was open for 0% -> 0% of each run, Pallas kernels for 31% -> 34%
where the time goes in v6:
time: 58.9 us; the launch traced here: 58.7 us
  starting transfers between devices  29.2 us (50%)
  Pallas kernels  21.1 us (36%)
  waiting for transfers between devices  7.5 us (13%)
  between operations  0.92 us (2%)
    ppermute x15, starting transfers between devices, exchange(): return lax.ppermute(x, 'frame', [(i, to(i, k)) for i in range(count)])  26.3 us
    ppermute x15, waiting for transfers between devices, exchange(): return lax.ppermute(x, 'frame', [(i, to(i, k)) for i in range(count)])  7.5 us
    pallas_call x2, Pallas kernels, attend(): pl.pallas_call(attend_kernel, in_specs=[vmem] * 6, out_specs=[vmem] * 4,...  6.47 us
    pallas_call x1, Pallas kernels, shards(): pl.pallas_call(inner_kernel, in_specs=[vmem] * 2 + [anywhere, vmem], out_...  5.24 us
    pallas_call x1, Pallas kernels, shards(): pl.pallas_call(outer_kernel, in_specs=[smem] + [vmem] * 8 + [anywhere] *...  5.11 us
    pallas_call x2, Pallas kernels, finish(): pl.pallas_call(body, in_specs=[vmem] * 5 + [anywhere] * len(before), out_...  2.2 us
    ppermute x1, starting transfers between devices, shards(): two = lax.ppermute(two, 'band', swaps(0))  2.18 us
    pallas_call x1, Pallas kernels, shards(): pl.pallas_call(merge_kernel, in_specs=[smem] + [anywhere] * 4, out_specs=...  2.02 us
  transfers between devices with their start and end apart: 17, of which 6 were waited for; matrix products, arithmetic and copies ran while one was open for 0% of the time, Pallas kernels for 34%

profile of v6, /device:TPU:1, one launch (start us, length us, event | category | flops | bytes accessed | tf_op | source)
XLA Modules:
  0.0 58.7 jit_solution(8970113272623303702)
XLA Ops:
  0.0 3.2 %collective-permute-start = (bf16[3,3,320,320]{3,2,1,0:T(8,128)(2,1)}, bf16[3,3,320,320]{3,2,1,0:T(8,128)(2,1)S(1)}, u32[]{:S(2)}, u32[]{:S(2)}) collective-permute-start(bf16[3,3,320,320]{3,2,1,0:T(8,128)(2,1)} %param.15), channel_id=1, source_target_pairs={{0,8},{8,0},{16,24},{24,16},{32,40},{40,32},{48,56},{56,48},{64,72... | collective-permute-start | bytes 5529608 | tf_op jit(solution)/shard_map/ppermute | solution.py:399
  3.9 2.0 %merge.1 = (bf16[2,320,128]{2,1,0:T(8,128)(2,1)S(1)}, bf16[2,320,128]{2,1,0:T(8,128)(2,1)S(1)}, bf16[8,128,320]{2,1,0:T(8,128)(2,1)S(1)}, f32[2,320]{1,0:T(2,128)S(1)}) custom-call(s32[1]{0:T(128)S(6)} %copy.16.step, bf16[8,8,16,320]{3,2,1,0:T(8,128)(2,1)} %frames.1, bf16[8,8,16,320]{3,2,1,0:T(8,128)(2,1)} %control.1, f32[320,1000]{1,0:T(8,128)} %bitcast.1, ...), custom_call_target="tpu_custom_call" | custom-call | tf_op jit(solution)/shard_map/merge/pallas_call | solution.py:425
  5.9 0.7 %collective-permute-start.1 = (bf16[2,320,128]{2,1,0:T(8,128)(2,1)S(1)}, bf16[2,320,128]{2,1,0:T(8,128)(2,1)S(1)}, u32[]{:S(2)}, u32[]{:S(2)}) collective-permute-start(bf16[2,320,128]{2,1,0:T(8,128)(2,1)S(1)} %get-tuple-element.54), channel_id=1, source_target_pairs={{1,2},{3,4},{5,6},{2,1},{4,3},{6,5},{9,10},{11,12},{13,14},{10,9},... | collective-permute-start | bytes 491528 | tf_op jit(solution)/shard_map/ppermute | solution.py:444
  6.6 2.2 %collective-permute-start.2 = (bf16[2,320,128]{2,1,0:T(8,128)(2,1)S(1)}, bf16[2,320,128]{2,1,0:T(8,128)(2,1)S(1)}, u32[]{:S(2)}, u32[]{:S(2)}) collective-permute-start(bf16[2,320,128]{2,1,0:T(8,128)(2,1)S(1)} %get-tuple-element.55), channel_id=1, source_target_pairs={{0,1},{2,3},{4,5},{6,7},{1,0},{3,2},{5,4},{7,6},{8,9},{10,11},{12,... | collective-permute-start | bytes 491528 | tf_op jit(solution)/shard_map/ppermute | solution.py:445
  8.8 0.0 collective-permute-done.first
  8.8 0.0 copy-start
  8.8 0.0 copy-start.1
  8.8 5.2 %inner_rows.1 = (bf16[2,320,128]{2,1,0:T(8,128)(2,1)S(1)}, bf16[2,320,128]{2,1,0:T(8,128)(2,1)S(1)}, f32[4,128,320]{2,1,0:T(8,128)S(1)}, bf16[4,128,320]{2,1,0:T...) custom-call(bf16[8,128,320]{2,1,0:T(8,128)(2,1)S(1)} %get-tuple-element.47.rows.merged, ...), custom_call_target="tpu_custom_call" | custom-call | tf_op jit(solution)/shard_map/inner_rows/pallas_call | solution.py:448
  14.0 0.0 collective-permute-done.1.one
  14.0 0.0 collective-permute-done.2.two
  14.1 0.7 %collective-permute-start.3 = (bf16[2,320,128]{2,1,0:T(8,128)(2,1)S(1)}, bf16[2,320,128]{2,1,0:T(8,128)(2,1)S(1)}, u32[]{:S(2)}, u32[]{:S(2)}) collective-permute-start(bf16[2,320,128]{2,1,0:T(8,128)(2,1)S(1)} %get-tuple-element.59), channel_id=1, source_target_pairs={{0,8},{8,0},{16,24},{24,16},{32,40},{40,32},{48,56},{56,48},{64,72... | collective-permute-start | bytes 491528 | tf_op jit(solution)/shard_map/ppermute | solution.py:399
  14.7 1.0 %collective-permute-done.3.got = bf16[2,320,128]{2,1,0:T(8,128)(2,1)S(1)} collective-permute-done((bf16[2,320,128]{2,1,0:T(8,128)(2,1)S(1)}, bf16[2,320,128]{2,1,0:T(8,128)(2,1)S(1)}, u32[]{:S(2)}, u32[]{:S(2)}) %collective-permute-start.3) | collective-permute-done | bytes 163872 | tf_op jit(solution)/shard_map/ppermute | solution.py:399
  15.8 2.8 %collective-permute-start.4 = (bf16[2,320,128]{2,1,0:T(8,128)(2,1)S(1)}, bf16[2,320,128]{2,1,0:T(8,128)(2,1)S(1)}, u32[]{:S(2)}, u32[]{:S(2)}) collective-permute-start(bf16[2,320,128]{2,1,0:T(8,128)(2,1)S(1)} %get-tuple-element.67), channel_id=1, source_target_pairs={{0,16},{8,24},{16,0},{24,8},{32,48},{40,56},{48,32},{56,40},{64,80... | collective-permute-start | bytes 491528 | tf_op jit(solution)/shard_map/ppermute | solution.py:399
  18.6 5.6 %collective-permute-start.5 = (bf16[2,320,128]{2,1,0:T(8,128)(2,1)S(1)}, bf16[2,320,128]{2,1,0:T(8,128)(2,1)S(1)}, u32[]{:S(2)}, u32[]{:S(2)}) collective-permute-start(bf16[2,320,128]{2,1,0:T(8,128)(2,1)S(1)} %get-tuple-element.80.near), channel_id=1, source_target_pairs={{0,224},{8,232},{16,48},{24,56},{32,0},{40,8},{48,80},{56,88},{64,... | collective-permute-start | bytes 491528 | tf_op jit(solution)/shard_map/ppermute | solution.py:399
  24.2 0.0 copy-done
  24.2 0.0 copy-done.1
  24.2 5.1 %outer_rows.1 = (bf16[2,320,128]{2,1,0:T(8,128)(2,1)S(1)}, bf16[2,320,128]{2,1,0:T(8,128)(2,1)S(1)}, f32[4,128,320]{2,1,0:T(8,128)S(1)}, bf16[4,320,320]{2,1,0:T(8,128)(2,1)S(1)}, f32[64,256]{1,0:T(8,128)S(1)}) custom-call(s32[256]{0:T(256)S(1)} %copy-done.1, bf16[2,320,128]{2,1,0:T(8,128)(2,1)S(1)} %collective-permute-done.1.one, ...), custom_call_target="tpu_custom_call" | custom-call | tf_op jit(solution)/shard_map/outer_rows/pallas_call | solution.py:485
  29.3 0.0 collective-permute-done.4.across_x
  29.3 0.0 collective-permute-done.5.near_z
  29.3 1.0 %collective-permute-start.6 = (bf16[2,320,128]{2,1,0:T(8,128)(2,1)S(1)}, bf16[2,320,128]{2,1,0:T(8,128)(2,1)S(1)}, u32[]{:S(2)}, u32[]{:S(2)}) collective-permute-start(bf16[2,320,128]{2,1,0:T(8,128)(2,1)S(1)} %get-tuple-element.68), channel_id=1, source_target_pairs={{0,8},{8,0},{16,24},{24,16},{32,40},{40,32},{48,56},{56,48},{64,72... | collective-permute-start | bytes 491528 | tf_op jit(solution)/shard_map/ppermute | solution.py:399
  30.3 0.0 collective-permute-start.13
  30.3 1.0 %collective-permute-done.6.got = bf16[2,320,128]{2,1,0:T(8,128)(2,1)S(1)} collective-permute-done((bf16[2,320,128]{2,1,0:T(8,128)(2,1)S(1)}, bf16[2,320,128]{2,1,0:T(8,128)(2,1)S(1)}, u32[]{:S(2)}, u32[]{:S(2)}) %collective-permute-start.6) | collective-permute-done | bytes 163872 | tf_op jit(solution)/shard_map/ppermute | solution.py:399
  31.4 1.7 %collective-permute-start.8 = (bf16[2,320,128]{2,1,0:T(8,128)(2,1)S(1)}, bf16[2,320,128]{2,1,0:T(8,128)(2,1)S(1)}, u32[]{:S(2)}, u32[]{:S(2)}) collective-permute-start(bf16[2,320,128]{2,1,0:T(8,128)(2,1)S(1)} %get-tuple-element.71.near), channel_id=1, source_target_pairs={{0,224},{8,232},{16,48},{24,56},{32,0},{40,8},{48,80},{56,88},{64,... | collective-permute-start | bytes 491528 | tf_op jit(solution)/shard_map/ppermute | solution.py:399
  33.1 1.7 %collective-permute-start.9 = (bf16[2,320,128]{2,1,0:T(8,128)(2,1)S(1)}, bf16[2,320,128]{2,1,0:T(8,128)(2,1)S(1)}, u32[]{:S(2)}, u32[]{:S(2)}) collective-permute-start(bf16[2,320,128]{2,1,0:T(8,128)(2,1)S(1)} %get-tuple-element.72), channel_id=1, source_target_pairs={{0,240},{8,248},{16,32},{24,40},{32,16},{40,24},{48,64},{56,72},{6... | collective-permute-start | bytes 491528 | tf_op jit(solution)/shard_map/ppermute | solution.py:399
  34.8 0.8 %collective-permute-start.7 = (bf16[2,320,128]{2,1,0:T(8,128)(2,1)S(1)}, bf16[2,320,128]{2,1,0:T(8,128)(2,1)S(1)}, u32[]{:S(2)}, u32[]{:S(2)}) collective-permute-start(bf16[2,320,128]{2,1,0:T(8,128)(2,1)S(1)} %get-tuple-element.72), channel_id=1, source_target_pairs={{0,16},{8,24},{16,0},{24,8},{32,48},{40,56},{48,32},{56,40},{64,80... | collective-permute-start | bytes 491528 | tf_op jit(solution)/shard_map/ppermute | solution.py:399
  35.6 1.7 %collective-permute-done.13.across_z = bf16[2,320,128]{2,1,0:T(8,128)(2,1)S(1)} collective-permute-done((bf16[2,320,128]{2,1,0:T(8,128)(2,1)S(1)}, bf16[2,320,128]{2,1,0:T(8,128)(2,1)S(1)}, u32[]{:S(2)}, u32[]{:S(2)}) %collective-permute-start.13) | collective-permute-done | bytes 163872 | tf_op jit(solution)/shard_map/ppermute | solution.py:399
  37.3 3.2 %attend.3 = (bf16[320,128]{1,0:T(8,128)(2,1)S(1)}, bf16[320,128]{1,0:T(8,128)(2,1)S(1)}, bf16[320,128]{1,0:T(8,128)(2,1)S(1)}, bf16[320,128]{1,0:T(8,128)(2,1)S(1)}) custom-call(bf16[2,320,128]{2,1,0:T(8,128)(2,1)S(1)} %get-tuple-element.80.near, bf16[2,320,128]{2,1,0:T(8,128)(2,1)S(1)} %collective-permute-done.4.across_x, ...), custom_call_target="tpu_custom_call" | custom-call | tf_op jit(solution)/shard_map/attend/pallas_call | solution.py:513
  40.5 0.9 %collective-permute-start.14 = (bf16[320,128]{1,0:T(8,128)(2,1)S(1)}, bf16[320,128]{1,0:T(8,128)(2,1)S(1)}, u32[]{:S(2)}, u32[]{:S(2)}) collective-permute-start(bf16[320,128]{1,0:T(8,128)(2,1)S(1)} %get-tuple-element.85), channel_id=1, source_target_pairs={{0,8},{8,0},{16,24},{24,16},{32,40},{40,32},{48,56},{56,48},{64,72... | collective-permute-start | bytes 245768 | tf_op jit(solution)/shard_map/ppermute | solution.py:399
  41.5 0.7 %collective-permute-start.15 = (bf16[320,128]{1,0:T(8,128)(2,1)S(1)}, bf16[320,128]{1,0:T(8,128)(2,1)S(1)}, u32[]{:S(2)}, u32[]{:S(2)}) collective-permute-start(bf16[320,128]{1,0:T(8,128)(2,1)S(1)} %get-tuple-element.86), channel_id=1, source_target_pairs={{0,16},{8,24},{16,0},{24,8},{32,48},{40,56},{48,32},{56,40},{64,80... | collective-permute-start | bytes 245768 | tf_op jit(solution)/shard_map/ppermute | solution.py:399
  42.2 0.0 collective-permute-done.8.near_z
  42.2 2.5 %collective-permute-start.16 = (bf16[320,128]{1,0:T(8,128)(2,1)S(1)}, bf16[320,128]{1,0:T(8,128)(2,1)S(1)}, u32[]{:S(2)}, u32[]{:S(2)}) collective-permute-start(bf16[320,128]{1,0:T(8,128)(2,1)S(1)} %get-tuple-element.87), channel_id=1, source_target_pairs={{0,24},{8,16},{16,8},{24,0},{32,56},{40,48},{48,40},{56,32},{64,88... | collective-permute-start | bytes 245768 | tf_op jit(solution)/shard_map/ppermute | solution.py:399
  44.7 0.0 collective-permute-done.9.across_z
  44.7 0.7 %collective-permute-done.7.across_x = bf16[2,320,128]{2,1,0:T(8,128)(2,1)S(1)} collective-permute-done((bf16[2,320,128]{2,1,0:T(8,128)(2,1)S(1)}, bf16[2,320,128]{2,1,0:T(8,128)(2,1)S(1)}, u32[]{:S(2)}, u32[]{:S(2)}) %collective-permute-start.7) | collective-permute-done | bytes 163872 | tf_op jit(solution)/shard_map/ppermute | solution.py:399
  45.4 3.2 %attend.2 = (bf16[320,128]{1,0:T(8,128)(2,1)S(1)}, bf16[320,128]{1,0:T(8,128)(2,1)S(1)}, bf16[320,128]{1,0:T(8,128)(2,1)S(1)}, bf16[320,128]{1,0:T(8,128)(2,1)S(1)}) custom-call(bf16[2,320,128]{2,1,0:T(8,128)(2,1)S(1)} %get-tuple-element.71.near, bf16[2,320,128]{2,1,0:T(8,128)(2,1)S(1)} %collective-permute-done.7.across_x, ...), custom_call_target="tpu_custom_call" | custom-call | tf_op jit(solution)/shard_map/attend/pallas_call | solution.py:513
  48.6 1.4 %collective-permute-start.10 = (bf16[320,128]{1,0:T(8,128)(2,1)S(1)}, bf16[320,128]{1,0:T(8,128)(2,1)S(1)}, u32[]{:S(2)}, u32[]{:S(2)}) collective-permute-start(bf16[320,128]{1,0:T(8,128)(2,1)S(1)} %get-tuple-element.76), channel_id=1, source_target_pairs={{0,8},{8,0},{16,24},{24,16},{32,40},{40,32},{48,56},{56,48},{64,72... | collective-permute-start | bytes 245768 | tf_op jit(solution)/shard_map/ppermute | solution.py:399
  50.0 0.7 %collective-permute-start.11 = (bf16[320,128]{1,0:T(8,128)(2,1)S(1)}, bf16[320,128]{1,0:T(8,128)(2,1)S(1)}, u32[]{:S(2)}, u32[]{:S(2)}) collective-permute-start(bf16[320,128]{1,0:T(8,128)(2,1)S(1)} %get-tuple-element.77), channel_id=1, source_target_pairs={{0,16},{8,24},{16,0},{24,8},{32,48},{40,56},{48,32},{56,40},{64,80... | collective-permute-start | bytes 245768 | tf_op jit(solution)/shard_map/ppermute | solution.py:399
  50.7 0.0 collective-permute-done.14.refs_1_
  50.7 2.6 %collective-permute-start.12 = (bf16[320,128]{1,0:T(8,128)(2,1)S(1)}, bf16[320,128]{1,0:T(8,128)(2,1)S(1)}, u32[]{:S(2)}, u32[]{:S(2)}) collective-permute-start(bf16[320,128]{1,0:T(8,128)(2,1)S(1)} %get-tuple-element.78), channel_id=1, source_target_pairs={{0,24},{8,16},{16,8},{24,0},{32,56},{40,48},{48,40},{56,32},{64,88... | collective-permute-start | bytes 245768 | tf_op jit(solution)/shard_map/ppermute | solution.py:399
  53.2 0.0 collective-permute-done.15.refs_2_
  53.2 0.0 collective-permute-done.16.refs_3_
  53.2 1.1 %project_out.2.refs_5_ = f32[8,8,16,320]{3,2,1,0:T(8,128)} custom-call(bf16[320,128]{1,0:T(8,128)(2,1)S(1)} %get-tuple-element.84.refs_0_, bf16[320,128]{1,0:T(8,128)(2,1)S(1)} %collective-permute-done.14.refs_1_, bf16[320,128]{1,0:T(8,128)(2,1)S(1)} %collective-permute-done.15.refs_2_, bf16[320,128]{1,0:T(8,128)(2,1)S(1)} %collective-permute-done.16.refs_3_, ...), custom_call_target="tpu_custom_call" | custom-call | tf_op jit(solution)/shard_map/project_out/pallas_call | solution.py:542
  54.4 0.0 collective-permute-done.10.refs_1_
  54.4 1.1 %collective-permute-done.11.refs_2_ = bf16[320,128]{1,0:T(8,128)(2,1)S(1)} collective-permute-done((bf16[320,128]{1,0:T(8,128)(2,1)S(1)}, bf16[320,128]{1,0:T(8,128)(2,1)S(1)}, u32[]{:S(2)}, u32[]{:S(2)}) %collective-permute-start.11) | collective-permute-done | bytes 81952 | tf_op jit(solution)/shard_map/ppermute | solution.py:399
  55.5 1.9 %collective-permute-done.12.refs_3_ = bf16[320,128]{1,0:T(8,128)(2,1)S(1)} collective-permute-done((bf16[320,128]{1,0:T(8,128)(2,1)S(1)}, bf16[320,128]{1,0:T(8,128)(2,1)S(1)}, u32[]{:S(2)}, u32[]{:S(2)}) %collective-permute-start.12) | collective-permute-done | bytes 81952 | tf_op jit(solution)/shard_map/ppermute | solution.py:399
  57.4 1.1 %project_out.3 = f32[8,8,16,320]{3,2,1,0:T(8,128)} custom-call(bf16[320,128]{1,0:T(8,128)(2,1)S(1)} %get-tuple-element.75.refs_0_, bf16[320,128]{1,0:T(8,128)(2,1)S(1)} %collective-permute-done.10.refs_1_, bf16[320,128]{1,0:T(8,128)(2,1)S(1)} %collective-permute-done.11.refs_2_, ...), custom_call_target="tpu_custom_call", output_to_operand_aliasing={{}: (5, {})} | custom-call | tf_op jit(solution)/shard_map/project_out/pallas_call | solution.py:542
  (2 shorter events, 0.0 us)
Async XLA Ops:
  0.0 8.8 %collective-permute-start = (bf16[3,3,320,320]{3,2,1,0:T(8,128)(2,1)}, bf16[3,3,320,320]{3,2,1,0:T(8,128)(2,1)S(1)}, u32[]{:S(2)}, u32[]{:S(2)}) collective-permute-start(bf16[3,3,320,320]{3,2,1,0:T(8,128)(2,1)} %param.15), channel_id=1, source_target_pairs={{0,8},{8,0},{16,24},{24,16},{32,40},{40,32},{48,56},{56,48},{64,72... | collective-permute-start | bytes 5529608 | tf_op jit(solution)/shard_map/ppermute | solution.py:399
  5.9 8.1 %collective-permute-start.1 = (bf16[2,320,128]{2,1,0:T(8,128)(2,1)S(1)}, bf16[2,320,128]{2,1,0:T(8,128)(2,1)S(1)}, u32[]{:S(2)}, u32[]{:S(2)}) collective-permute-start(bf16[2,320,128]{2,1,0:T(8,128)(2,1)S(1)} %get-tuple-element.54), channel_id=1, source_target_pairs={{1,2},{3,4},{5,6},{2,1},{4,3},{6,5},{9,10},{11,12},{13,14},{10,9},... | collective-permute-start | bytes 491528 | tf_op jit(solution)/shard_map/ppermute | solution.py:444
  6.6 7.4 %collective-permute-start.2 = (bf16[2,320,128]{2,1,0:T(8,128)(2,1)S(1)}, bf16[2,320,128]{2,1,0:T(8,128)(2,1)S(1)}, u32[]{:S(2)}, u32[]{:S(2)}) collective-permute-start(bf16[2,320,128]{2,1,0:T(8,128)(2,1)S(1)} %get-tuple-element.55), channel_id=1, source_target_pairs={{0,1},{2,3},{4,5},{6,7},{1,0},{3,2},{5,4},{7,6},{8,9},{10,11},{12,... | collective-permute-start | bytes 491528 | tf_op jit(solution)/shard_map/ppermute | solution.py:445
  8.8 15.4 %copy-start = (f32[8,33]{1,0:T(8,128)S(1)}, f32[8,33]{1,0:T(8,128)}, u32[]{:S(2)}) copy-start(f32[8,33]{1,0:T(8,128)} %rel_bias.1) | copy-start | bytes 3172
  8.8 15.4 %copy-start.1 = (s32[256]{0:T(256)S(1)}, s32[256]{0:T(256)}, u32[]{:S(2)}) copy-start(s32[256]{0:T(256)} %reach.1) | copy-start | bytes 3076
  14.1 1.7 %collective-permute-start.3 = (bf16[2,320,128]{2,1,0:T(8,128)(2,1)S(1)}, bf16[2,320,128]{2,1,0:T(8,128)(2,1)S(1)}, u32[]{:S(2)}, u32[]{:S(2)}) collective-permute-start(bf16[2,320,128]{2,1,0:T(8,128)(2,1)S(1)} %get-tuple-element.59), channel_id=1, source_target_pairs={{0,8},{8,0},{16,24},{24,16},{32,40},{40,32},{48,56},{56,48},{64,72... | collective-permute-start | bytes 491528 | tf_op jit(solution)/shard_map/ppermute | solution.py:399
  15.8 13.5 %collective-permute-start.4 = (bf16[2,320,128]{2,1,0:T(8,128)(2,1)S(1)}, bf16[2,320,128]{2,1,0:T(8,128)(2,1)S(1)}, u32[]{:S(2)}, u32[]{:S(2)}) collective-permute-start(bf16[2,320,128]{2,1,0:T(8,128)(2,1)S(1)} %get-tuple-element.67), channel_id=1, source_target_pairs={{0,16},{8,24},{16,0},{24,8},{32,48},{40,56},{48,32},{56,40},{64,80... | collective-permute-start | bytes 491528 | tf_op jit(solution)/shard_map/ppermute | solution.py:399
  18.6 10.7 %collective-permute-start.5 = (bf16[2,320,128]{2,1,0:T(8,128)(2,1)S(1)}, bf16[2,320,128]{2,1,0:T(8,128)(2,1)S(1)}, u32[]{:S(2)}, u32[]{:S(2)}) collective-permute-start(bf16[2,320,128]{2,1,0:T(8,128)(2,1)S(1)} %get-tuple-element.80.near), channel_id=1, source_target_pairs={{0,224},{8,232},{16,48},{24,56},{32,0},{40,8},{48,80},{56,88},{64,... | collective-permute-start | bytes 491528 | tf_op jit(solution)/shard_map/ppermute | solution.py:399
  29.3 2.0 %collective-permute-start.6 = (bf16[2,320,128]{2,1,0:T(8,128)(2,1)S(1)}, bf16[2,320,128]{2,1,0:T(8,128)(2,1)S(1)}, u32[]{:S(2)}, u32[]{:S(2)}) collective-permute-start(bf16[2,320,128]{2,1,0:T(8,128)(2,1)S(1)} %get-tuple-element.68), channel_id=1, source_target_pairs={{0,8},{8,0},{16,24},{24,16},{32,40},{40,32},{48,56},{56,48},{64,72... | collective-permute-start | bytes 491528 | tf_op jit(solution)/shard_map/ppermute | solution.py:399
  30.3 7.0 %collective-permute-start.13 = (bf16[2,320,128]{2,1,0:T(8,128)(2,1)S(1)}, bf16[2,320,128]{2,1,0:T(8,128)(2,1)S(1)}, u32[]{:S(2)}, u32[]{:S(2)}) collective-permute-start(bf16[2,320,128]{2,1,0:T(8,128)(2,1)S(1)} %collective-permute-done.4.across_x), channel_id=1, source_target_pairs={{0,32},{8,40},{16,240},{24,248},{32,64},{40,72},{48,16},{56,24},{6... | collective-permute-start | bytes 491528 | tf_op jit(solution)/shard_map/ppermute | solution.py:399
  31.4 10.8 %collective-permute-start.8 = (bf16[2,320,128]{2,1,0:T(8,128)(2,1)S(1)}, bf16[2,320,128]{2,1,0:T(8,128)(2,1)S(1)}, u32[]{:S(2)}, u32[]{:S(2)}) collective-permute-start(bf16[2,320,128]{2,1,0:T(8,128)(2,1)S(1)} %get-tuple-element.71.near), channel_id=1, source_target_pairs={{0,224},{8,232},{16,48},{24,56},{32,0},{40,8},{48,80},{56,88},{64,... | collective-permute-start | bytes 491528 | tf_op jit(solution)/shard_map/ppermute | solution.py:399
  33.1 11.6 %collective-permute-start.9 = (bf16[2,320,128]{2,1,0:T(8,128)(2,1)S(1)}, bf16[2,320,128]{2,1,0:T(8,128)(2,1)S(1)}, u32[]{:S(2)}, u32[]{:S(2)}) collective-permute-start(bf16[2,320,128]{2,1,0:T(8,128)(2,1)S(1)} %get-tuple-element.72), channel_id=1, source_target_pairs={{0,240},{8,248},{16,32},{24,40},{32,16},{40,24},{48,64},{56,72},{6... | collective-permute-start | bytes 491528 | tf_op jit(solution)/shard_map/ppermute | solution.py:399
  34.8 10.6 %collective-permute-start.7 = (bf16[2,320,128]{2,1,0:T(8,128)(2,1)S(1)}, bf16[2,320,128]{2,1,0:T(8,128)(2,1)S(1)}, u32[]{:S(2)}, u32[]{:S(2)}) collective-permute-start(bf16[2,320,128]{2,1,0:T(8,128)(2,1)S(1)} %get-tuple-element.72), channel_id=1, source_target_pairs={{0,16},{8,24},{16,0},{24,8},{32,48},{40,56},{48,32},{56,40},{64,80... | collective-permute-start | bytes 491528 | tf_op jit(solution)/shard_map/ppermute | solution.py:399
  40.5 10.1 %collective-permute-start.14 = (bf16[320,128]{1,0:T(8,128)(2,1)S(1)}, bf16[320,128]{1,0:T(8,128)(2,1)S(1)}, u32[]{:S(2)}, u32[]{:S(2)}) collective-permute-start(bf16[320,128]{1,0:T(8,128)(2,1)S(1)} %get-tuple-element.85), channel_id=1, source_target_pairs={{0,8},{8,0},{16,24},{24,16},{32,40},{40,32},{48,56},{56,48},{64,72... | collective-permute-start | bytes 245768 | tf_op jit(solution)/shard_map/ppermute | solution.py:399
  41.5 11.8 %collective-permute-start.15 = (bf16[320,128]{1,0:T(8,128)(2,1)S(1)}, bf16[320,128]{1,0:T(8,128)(2,1)S(1)}, u32[]{:S(2)}, u32[]{:S(2)}) collective-permute-start(bf16[320,128]{1,0:T(8,128)(2,1)S(1)} %get-tuple-element.86), channel_id=1, source_target_pairs={{0,16},{8,24},{16,0},{24,8},{32,48},{40,56},{48,32},{56,40},{64,80... | collective-permute-start | bytes 245768 | tf_op jit(solution)/shard_map/ppermute | solution.py:399
  42.2 11.1 %collective-permute-start.16 = (bf16[320,128]{1,0:T(8,128)(2,1)S(1)}, bf16[320,128]{1,0:T(8,128)(2,1)S(1)}, u32[]{:S(2)}, u32[]{:S(2)}) collective-permute-start(bf16[320,128]{1,0:T(8,128)(2,1)S(1)} %get-tuple-element.87), channel_id=1, source_target_pairs={{0,24},{8,16},{16,8},{24,0},{32,56},{40,48},{48,40},{56,32},{64,88... | collective-permute-start | bytes 245768 | tf_op jit(solution)/shard_map/ppermute | solution.py:399
  48.6 5.8 %collective-permute-start.10 = (bf16[320,128]{1,0:T(8,128)(2,1)S(1)}, bf16[320,128]{1,0:T(8,128)(2,1)S(1)}, u32[]{:S(2)}, u32[]{:S(2)}) collective-permute-start(bf16[320,128]{1,0:T(8,128)(2,1)S(1)} %get-tuple-element.76), channel_id=1, source_target_pairs={{0,8},{8,0},{16,24},{24,16},{32,40},{40,32},{48,56},{56,48},{64,72... | collective-permute-start | bytes 245768 | tf_op jit(solution)/shard_map/ppermute | solution.py:399
  50.0 5.5 %collective-permute-start.11 = (bf16[320,128]{1,0:T(8,128)(2,1)S(1)}, bf16[320,128]{1,0:T(8,128)(2,1)S(1)}, u32[]{:S(2)}, u32[]{:S(2)}) collective-permute-start(bf16[320,128]{1,0:T(8,128)(2,1)S(1)} %get-tuple-element.77), channel_id=1, source_target_pairs={{0,16},{8,24},{16,0},{24,8},{32,48},{40,56},{48,32},{56,40},{64,80... | collective-permute-start | bytes 245768 | tf_op jit(solution)/shard_map/ppermute | solution.py:399
  50.7 6.8 %collective-permute-start.12 = (bf16[320,128]{1,0:T(8,128)(2,1)S(1)}, bf16[320,128]{1,0:T(8,128)(2,1)S(1)}, u32[]{:S(2)}, u32[]{:S(2)}) collective-permute-start(bf16[320,128]{1,0:T(8,128)(2,1)S(1)} %get-tuple-element.78), channel_id=1, source_target_pairs={{0,24},{8,16},{16,8},{24,0},{32,56},{40,48},{48,40},{56,32},{64,88... | collective-permute-start | bytes 245768 | tf_op jit(solution)/shard_map/ppermute | solution.py:399

commit v7 on v6

--- a/solution.py
+++ b/solution.py
@@ -175,15 +175,8 @@
     vectors[1:2] = line[...].reshape(1, 320)
 
 
-def inner_kernel(
-    rows, first, second, vectors,
-    keep, give, flat, edge, wide1, wide2,
-    buf, taps1, taps2, prod, normed, sems,
-):
-    loads = [pltpu.make_async_copy(second.at[i], buf.at[i], sems.at[i]) for i in range(3)]
-    for load in loads:
-        load.start()
-    me = in_group()
+def inner_kernel(rows, first, vectors, edge, wide1, taps2, taps1, prod):
+    embed = vectors[0:1]
     for m in range(8):
         value = rows[m]
         for dy in range(3):
@@ -191,9 +184,6 @@
                 tapped(taps1, m - dy, dy, value)
     arrange(wide1, first)
     multiply(prod, taps1, wide1, 6)
-
-    embed = vectors[0:1]
-    gain = vectors[1:2]
     for r in range(6):
         act = silu(combine(prod, r) + embed).astype(BF)
         for dy in range(3):
@@ -201,15 +191,17 @@
                 tapped(taps2, r - dy, dy, act)
         if r in (0, 1, 4, 5):
             edge[(0, 1, None, None, 2, 3)[r]] = act
-    for load in loads:
-        load.wait()
-    arrange(wide2, buf)
+
+
+def second_kernel(rows, second, vectors, taps2, keep, give, flat, wide2, prod, normed):
+    gain = vectors[1:2]
+    arrange(wide2, second)
     multiply(prod, taps2, wide2, 4)
     for y in range(4):
         value = combine(prod, y) + rows[y + 2].astype(F32)
         flat[y] = value
         fold(normed.at[y], layer_norm(value, gain))
-    hand_out(me, normed, keep, give)
+    hand_out(in_group(), normed, keep, give)
 
 
 def outer_kernel(
@@ -445,20 +437,25 @@
     two = lax.ppermute(two, "band", swaps(0))
 
     first = exchange(conv_first, plane, 1)
-    keep, give, flat_in, edge, wide1, wide2 = pl.pallas_call(
+    second = exchange(conv_second, plane, 1)
+    edge, wide1, taps = pl.pallas_call(
         inner_kernel,
-        in_specs=[vmem] * 2 + [anywhere, vmem],
-        out_specs=[vmem] * 6,
-        out_shape=[pair, pair, chunk, pltpu.VMEM((4, 128, 320), BF), wide, wide],
-        scratch_shapes=[
-            pltpu.VMEM((3, 3, 320, 320), BF),
-            pltpu.VMEM((6, 128, 960), BF),
-        ]
-        + rows_scratch
-        + [pltpu.SemaphoreType.DMA((3,))],
-        compiler_params=params(16),
+        in_specs=[vmem] * 3,
+        out_specs=[vmem] * 3,
+        out_shape=[pltpu.VMEM((4, 128, 320), BF), wide, pltpu.VMEM((4, 128, 960), BF)],
+        scratch_shapes=[pltpu.VMEM((6, 128, 960), BF), pltpu.VMEM((768, 960), F32)],
+        compiler_params=params(10),
         name="inner_rows",
-    )(*near_by(merged, first), *stay(conv_second), *near_by(vectors))
+    )(*near_by(merged, first, vectors))
+    keep, give, flat_in, wide2 = pl.pallas_call(
+        second_kernel,
+        in_specs=[vmem] * 4,
+        out_specs=[vmem] * 4,
+        out_shape=[pair, pair, chunk, wide],
+        scratch_shapes=[pltpu.VMEM((512, 960), F32), pltpu.VMEM((4, 320, 128), BF)],
+        compiler_params=params(8),
+        name="inner_second",
+    )(*near_by(merged, second, vectors, taps))
 
     keep, give, one, two = lax.optimization_barrier((keep, give, one, two))
 

time: 58.9 us -> 58.5 us (level)
  Pallas kernels: 21.1 us -> 20.2 us
    pallas_call x1 -> x2, Pallas kernels: 5.24 us -> 4.34 us  [the longest x1 2.18 us: shards(): pl.pallas_call(inner_kernel, in_specs=[vmem] * 3, out_specs=[vmem] * 3, o...]
    ppermute x15 -> x16, starting transfers between devices: 26.3 us -> 26.8 us  [exchange(): return lax.ppermute(x, 'frame', [(i, to(i, k)) for i in range(count)])]
    ppermute x15 -> x16, waiting for transfers between devices: 7.5 us -> 7.51 us  [exchange(): return lax.ppermute(x, 'frame', [(i, to(i, k)) for i in range(count)])]
  transfers between devices with their start and end apart: 17 -> 18, of which waited for: 6 -> 6; matrix products, arithmetic and copies ran while one was open for 0% -> 0% of each run, Pallas kernels for 34% -> 33%
where the time goes in v7:
time: 58.5 us; the launch traced here: 58.4 us
  starting transfers between devices  29.7 us (51%)
  Pallas kernels  20.2 us (35%)
  waiting for transfers between devices  7.51 us (13%)
  between operations  0.94 us (2%)
    ppermute x16, starting transfers between devices, exchange(): return lax.ppermute(x, 'frame', [(i, to(i, k)) for i in range(count)])  26.8 us
    ppermute x16, waiting for transfers between devices, exchange(): return lax.ppermute(x, 'frame', [(i, to(i, k)) for i in range(count)])  7.51 us
    pallas_call x2, Pallas kernels, attend(): pl.pallas_call(attend_kernel, in_specs=[vmem] * 6, out_specs=[vmem] * 4,...  6.5 us
    pallas_call x1, Pallas kernels, shards(): pl.pallas_call(outer_kernel, in_specs=[smem] + [vmem] * 8 + [anywhere] *...  5.1 us
    pallas_call x2, Pallas kernels, finish(): pl.pallas_call(body, in_specs=[vmem] * 5 + [anywhere] * len(before), out_...  2.2 us
    pallas_call x1, Pallas kernels, shards(): pl.pallas_call(inner_kernel, in_specs=[vmem] * 3, out_specs=[vmem] * 3, o...  2.18 us
    ppermute x1, starting transfers between devices, shards(): two = lax.ppermute(two, 'band', swaps(0))  2.18 us
    pallas_call x1, Pallas kernels, shards(): pl.pallas_call(second_kernel, in_specs=[vmem] * 4, out_specs=[vmem] * 4,...  2.16 us
  transfers between devices with their start and end apart: 18, of which 6 were waited for; matrix products, arithmetic and copies ran while one was open for 0% of the time, Pallas kernels for 33%

profile of v7, /device:TPU:1, one launch (start us, length us, event | category | flops | bytes accessed | tf_op | source)
XLA Modules:
  0.0 58.4 jit_solution(15703789576604039218)
XLA Ops:
  0.0 3.2 %collective-permute-start.1 = (bf16[3,3,320,320]{3,2,1,0:T(8,128)(2,1)}, bf16[3,3,320,320]{3,2,1,0:T(8,128)(2,1)S(1)}, u32[]{:S(2)}, u32[]{:S(2)}) collective-permute-start(bf16[3,3,320,320]{3,2,1,0:T(8,128)(2,1)} %param.15), channel_id=1, source_target_pairs={{0,8},{8,0},{16,24},{24,16},{32,40},{40,32},{48,56},{56,48},{64,72... | collective-permute-start | bytes 5529608 | tf_op jit(solution)/shard_map/ppermute | solution.py:391
  3.2 0.0 collective-permute-start
  3.9 2.0 %merge.1 = (bf16[2,320,128]{2,1,0:T(8,128)(2,1)S(1)}, bf16[2,320,128]{2,1,0:T(8,128)(2,1)S(1)}, bf16[8,128,320]{2,1,0:T(8,128)(2,1)S(1)}, f32[2,320]{1,0:T(2,128)S(1)}) custom-call(s32[1]{0:T(128)S(6)} %copy.16.step, bf16[8,8,16,320]{3,2,1,0:T(8,128)(2,1)} %frames.1, bf16[8,8,16,320]{3,2,1,0:T(8,128)(2,1)} %control.1, f32[320,1000]{1,0:T(8,128)} %bitcast.1, ...), custom_call_target="tpu_custom_call" | custom-call | tf_op jit(solution)/shard_map/merge/pallas_call | solution.py:417
  5.9 0.7 %collective-permute-start.2 = (bf16[2,320,128]{2,1,0:T(8,128)(2,1)S(1)}, bf16[2,320,128]{2,1,0:T(8,128)(2,1)S(1)}, u32[]{:S(2)}, u32[]{:S(2)}) collective-permute-start(bf16[2,320,128]{2,1,0:T(8,128)(2,1)S(1)} %get-tuple-element.56), channel_id=1, source_target_pairs={{1,2},{3,4},{5,6},{2,1},{4,3},{6,5},{9,10},{11,12},{13,14},{10,9},... | collective-permute-start | bytes 491528 | tf_op jit(solution)/shard_map/ppermute | solution.py:436
  6.6 2.2 %collective-permute-start.3 = (bf16[2,320,128]{2,1,0:T(8,128)(2,1)S(1)}, bf16[2,320,128]{2,1,0:T(8,128)(2,1)S(1)}, u32[]{:S(2)}, u32[]{:S(2)}) collective-permute-start(bf16[2,320,128]{2,1,0:T(8,128)(2,1)S(1)} %get-tuple-element.57), channel_id=1, source_target_pairs={{0,1},{2,3},{4,5},{6,7},{1,0},{3,2},{5,4},{7,6},{8,9},{10,11},{12,... | collective-permute-start | bytes 491528 | tf_op jit(solution)/shard_map/ppermute | solution.py:437
  8.8 0.0 collective-permute-done.1.first
  8.8 2.2 %inner_rows.1 = (bf16[4,128,320]{2,1,0:T(8,128)(2,1)S(1)}, bf16[960,960]{1,0:T(8,128)(2,1)S(1)}, bf16[4,128,960]{2,1,0:T(8,128)(2,1)S(1)}) custom-call(bf16[8,128,320]{2,1,0:T(8,128)(2,1)S(1)} %get-tuple-element.48.rows.merged, bf16[3,3,320,320]{3,2,1,0:T(8,128)(2,1)S(1)} %collective-permute-done.1.first, f32[2,320]{1,0:T(2,128)S(1)} %get-tuple-element.52.vectors), custom_call_target="tpu_custom_call" | custom-call | tf_op jit(solution)/shard_map/inner_rows/pallas_call | solution.py:441
  11.0 0.0 collective-permute-done.second
  11.0 0.0 copy-start
  11.0 0.0 copy-start.1
  11.0 2.2 %inner_second.1 = (bf16[2,320,128]{2,1,0:T(8,128)(2,1)S(1)}, bf16[2,320,128]{2,1,0:T(8,128)(2,1)S(1)}, f32[4,128,320]{2,1,0:T(8,128)S(1)}, bf16[960,960]{1,0:T(8,128)(2,1)S(1)}) custom-call(bf16[8,128,320]{2,1,0:T(8,128)(2,1)S(1)} %get-tuple-element.48.rows.merged, bf16[3,3,320,320]{3,2,1,0:T(8,128)(2,1)S(1)} %collective-permute-done.second, ...), custom_call_target="tpu_custom_call" | custom-call | tf_op jit(solution)/shard_map/inner_second/pallas_call | solution.py:450
  13.2 0.0 collective-permute-done.2.one
  13.2 0.0 collective-permute-done.3.two
  13.2 1.2 %collective-permute-start.4 = (bf16[2,320,128]{2,1,0:T(8,128)(2,1)S(1)}, bf16[2,320,128]{2,1,0:T(8,128)(2,1)S(1)}, u32[]{:S(2)}, u32[]{:S(2)}) collective-permute-start(bf16[2,320,128]{2,1,0:T(8,128)(2,1)S(1)} %get-tuple-element.61), channel_id=1, source_target_pairs={{0,8},{8,0},{16,24},{24,16},{32,40},{40,32},{48,56},{56,48},{64,72... | collective-permute-start | bytes 491528 | tf_op jit(solution)/shard_map/ppermute | solution.py:391
  14.4 1.0 %collective-permute-done.4.got = bf16[2,320,128]{2,1,0:T(8,128)(2,1)S(1)} collective-permute-done((bf16[2,320,128]{2,1,0:T(8,128)(2,1)S(1)}, bf16[2,320,128]{2,1,0:T(8,128)(2,1)S(1)}, u32[]{:S(2)}, u32[]{:S(2)}) %collective-permute-start.4) | collective-permute-done | bytes 163872 | tf_op jit(solution)/shard_map/ppermute | solution.py:391
  15.4 2.8 %collective-permute-start.5 = (bf16[2,320,128]{2,1,0:T(8,128)(2,1)S(1)}, bf16[2,320,128]{2,1,0:T(8,128)(2,1)S(1)}, u32[]{:S(2)}, u32[]{:S(2)}) collective-permute-start(bf16[2,320,128]{2,1,0:T(8,128)(2,1)S(1)} %get-tuple-element.69), channel_id=1, source_target_pairs={{0,16},{8,24},{16,0},{24,8},{32,48},{40,56},{48,32},{56,40},{64,80... | collective-permute-start | bytes 491528 | tf_op jit(solution)/shard_map/ppermute | solution.py:391
  18.2 5.6 %collective-permute-start.6 = (bf16[2,320,128]{2,1,0:T(8,128)(2,1)S(1)}, bf16[2,320,128]{2,1,0:T(8,128)(2,1)S(1)}, u32[]{:S(2)}, u32[]{:S(2)}) collective-permute-start(bf16[2,320,128]{2,1,0:T(8,128)(2,1)S(1)} %get-tuple-element.82.near), channel_id=1, source_target_pairs={{0,224},{8,232},{16,48},{24,56},{32,0},{40,8},{48,80},{56,88},{64,... | collective-permute-start | bytes 491528 | tf_op jit(solution)/shard_map/ppermute | solution.py:391
  23.8 0.0 copy-done
  23.8 0.0 copy-done.1
  23.8 5.1 %outer_rows.1 = (bf16[2,320,128]{2,1,0:T(8,128)(2,1)S(1)}, bf16[2,320,128]{2,1,0:T(8,128)(2,1)S(1)}, f32[4,128,320]{2,1,0:T(8,128)S(1)}, bf16[4,320,320]{2,1,0:T(8,128)(2,1)S(1)}, f32[64,256]{1,0:T(8,128)S(1)}) custom-call(s32[256]{0:T(256)S(1)} %copy-done.1, bf16[2,320,128]{2,1,0:T(8,128)(2,1)S(1)} %collective-permute-done.2.one, ...), custom_call_target="tpu_custom_call" | custom-call | tf_op jit(solution)/shard_map/outer_rows/pallas_call | solution.py:482
  28.9 0.0 collective-permute-done.5.across_x
  28.9 0.0 collective-permute-done.6.near_z
  28.9 1.0 %collective-permute-start.7 = (bf16[2,320,128]{2,1,0:T(8,128)(2,1)S(1)}, bf16[2,320,128]{2,1,0:T(8,128)(2,1)S(1)}, u32[]{:S(2)}, u32[]{:S(2)}) collective-permute-start(bf16[2,320,128]{2,1,0:T(8,128)(2,1)S(1)} %get-tuple-element.70), channel_id=1, source_target_pairs={{0,8},{8,0},{16,24},{24,16},{32,40},{40,32},{48,56},{56,48},{64,72... | collective-permute-start | bytes 491528 | tf_op jit(solution)/shard_map/ppermute | solution.py:391
  30.0 0.0 collective-permute-start.14
  30.0 1.0 %collective-permute-done.7.got = bf16[2,320,128]{2,1,0:T(8,128)(2,1)S(1)} collective-permute-done((bf16[2,320,128]{2,1,0:T(8,128)(2,1)S(1)}, bf16[2,320,128]{2,1,0:T(8,128)(2,1)S(1)}, u32[]{:S(2)}, u32[]{:S(2)}) %collective-permute-start.7) | collective-permute-done | bytes 163872 | tf_op jit(solution)/shard_map/ppermute | solution.py:391
  31.0 1.8 %collective-permute-start.9 = (bf16[2,320,128]{2,1,0:T(8,128)(2,1)S(1)}, bf16[2,320,128]{2,1,0:T(8,128)(2,1)S(1)}, u32[]{:S(2)}, u32[]{:S(2)}) collective-permute-start(bf16[2,320,128]{2,1,0:T(8,128)(2,1)S(1)} %get-tuple-element.73.near), channel_id=1, source_target_pairs={{0,224},{8,232},{16,48},{24,56},{32,0},{40,8},{48,80},{56,88},{64,... | collective-permute-start | bytes 491528 | tf_op jit(solution)/shard_map/ppermute | solution.py:391
  32.8 1.7 %collective-permute-start.10 = (bf16[2,320,128]{2,1,0:T(8,128)(2,1)S(1)}, bf16[2,320,128]{2,1,0:T(8,128)(2,1)S(1)}, u32[]{:S(2)}, u32[]{:S(2)}) collective-permute-start(bf16[2,320,128]{2,1,0:T(8,128)(2,1)S(1)} %get-tuple-element.74), channel_id=1, source_target_pairs={{0,240},{8,248},{16,32},{24,40},{32,16},{40,24},{48,64},{56,72},{6... | collective-permute-start | bytes 491528 | tf_op jit(solution)/shard_map/ppermute | solution.py:391
  34.4 0.8 %collective-permute-start.8 = (bf16[2,320,128]{2,1,0:T(8,128)(2,1)S(1)}, bf16[2,320,128]{2,1,0:T(8,128)(2,1)S(1)}, u32[]{:S(2)}, u32[]{:S(2)}) collective-permute-start(bf16[2,320,128]{2,1,0:T(8,128)(2,1)S(1)} %get-tuple-element.74), channel_id=1, source_target_pairs={{0,16},{8,24},{16,0},{24,8},{32,48},{40,56},{48,32},{56,40},{64,80... | collective-permute-start | bytes 491528 | tf_op jit(solution)/shard_map/ppermute | solution.py:391
  35.2 1.7 %collective-permute-done.14.across_z = bf16[2,320,128]{2,1,0:T(8,128)(2,1)S(1)} collective-permute-done((bf16[2,320,128]{2,1,0:T(8,128)(2,1)S(1)}, bf16[2,320,128]{2,1,0:T(8,128)(2,1)S(1)}, u32[]{:S(2)}, u32[]{:S(2)}) %collective-permute-start.14) | collective-permute-done | bytes 163872 | tf_op jit(solution)/shard_map/ppermute | solution.py:391
  36.9 3.3 %attend.3 = (bf16[320,128]{1,0:T(8,128)(2,1)S(1)}, bf16[320,128]{1,0:T(8,128)(2,1)S(1)}, bf16[320,128]{1,0:T(8,128)(2,1)S(1)}, bf16[320,128]{1,0:T(8,128)(2,1)S(1)}) custom-call(bf16[2,320,128]{2,1,0:T(8,128)(2,1)S(1)} %get-tuple-element.82.near, bf16[2,320,128]{2,1,0:T(8,128)(2,1)S(1)} %collective-permute-done.5.across_x, ...), custom_call_target="tpu_custom_call" | custom-call | tf_op jit(solution)/shard_map/attend/pallas_call | solution.py:510
  40.2 0.9 %collective-permute-start.15 = (bf16[320,128]{1,0:T(8,128)(2,1)S(1)}, bf16[320,128]{1,0:T(8,128)(2,1)S(1)}, u32[]{:S(2)}, u32[]{:S(2)}) collective-permute-start(bf16[320,128]{1,0:T(8,128)(2,1)S(1)} %get-tuple-element.87), channel_id=1, source_target_pairs={{0,8},{8,0},{16,24},{24,16},{32,40},{40,32},{48,56},{56,48},{64,72... | collective-permute-start | bytes 245768 | tf_op jit(solution)/shard_map/ppermute | solution.py:391
  41.1 0.8 %collective-permute-start.16 = (bf16[320,128]{1,0:T(8,128)(2,1)S(1)}, bf16[320,128]{1,0:T(8,128)(2,1)S(1)}, u32[]{:S(2)}, u32[]{:S(2)}) collective-permute-start(bf16[320,128]{1,0:T(8,128)(2,1)S(1)} %get-tuple-element.88), channel_id=1, source_target_pairs={{0,16},{8,24},{16,0},{24,8},{32,48},{40,56},{48,32},{56,40},{64,80... | collective-permute-start | bytes 245768 | tf_op jit(solution)/shard_map/ppermute | solution.py:391
  41.9 0.0 collective-permute-done.9.near_z
  41.9 2.5 %collective-permute-start.17 = (bf16[320,128]{1,0:T(8,128)(2,1)S(1)}, bf16[320,128]{1,0:T(8,128)(2,1)S(1)}, u32[]{:S(2)}, u32[]{:S(2)}) collective-permute-start(bf16[320,128]{1,0:T(8,128)(2,1)S(1)} %get-tuple-element.89), channel_id=1, source_target_pairs={{0,24},{8,16},{16,8},{24,0},{32,56},{40,48},{48,40},{56,32},{64,88... | collective-permute-start | bytes 245768 | tf_op jit(solution)/shard_map/ppermute | solution.py:391
  44.3 0.0 collective-permute-done.10.across_z
  44.3 0.7 %collective-permute-done.8.across_x = bf16[2,320,128]{2,1,0:T(8,128)(2,1)S(1)} collective-permute-done((bf16[2,320,128]{2,1,0:T(8,128)(2,1)S(1)}, bf16[2,320,128]{2,1,0:T(8,128)(2,1)S(1)}, u32[]{:S(2)}, u32[]{:S(2)}) %collective-permute-start.8) | collective-permute-done | bytes 163872 | tf_op jit(solution)/shard_map/ppermute | solution.py:391
  45.0 3.2 %attend.2 = (bf16[320,128]{1,0:T(8,128)(2,1)S(1)}, bf16[320,128]{1,0:T(8,128)(2,1)S(1)}, bf16[320,128]{1,0:T(8,128)(2,1)S(1)}, bf16[320,128]{1,0:T(8,128)(2,1)S(1)}) custom-call(bf16[2,320,128]{2,1,0:T(8,128)(2,1)S(1)} %get-tuple-element.73.near, bf16[2,320,128]{2,1,0:T(8,128)(2,1)S(1)} %collective-permute-done.8.across_x, ...), custom_call_target="tpu_custom_call" | custom-call | tf_op jit(solution)/shard_map/attend/pallas_call | solution.py:510
  48.2 1.4 %collective-permute-start.11 = (bf16[320,128]{1,0:T(8,128)(2,1)S(1)}, bf16[320,128]{1,0:T(8,128)(2,1)S(1)}, u32[]{:S(2)}, u32[]{:S(2)}) collective-permute-start(bf16[320,128]{1,0:T(8,128)(2,1)S(1)} %get-tuple-element.78), channel_id=1, source_target_pairs={{0,8},{8,0},{16,24},{24,16},{32,40},{40,32},{48,56},{56,48},{64,72... | collective-permute-start | bytes 245768 | tf_op jit(solution)/shard_map/ppermute | solution.py:391
  49.7 0.6 %collective-permute-start.12 = (bf16[320,128]{1,0:T(8,128)(2,1)S(1)}, bf16[320,128]{1,0:T(8,128)(2,1)S(1)}, u32[]{:S(2)}, u32[]{:S(2)}) collective-permute-start(bf16[320,128]{1,0:T(8,128)(2,1)S(1)} %get-tuple-element.79), channel_id=1, source_target_pairs={{0,16},{8,24},{16,0},{24,8},{32,48},{40,56},{48,32},{56,40},{64,80... | collective-permute-start | bytes 245768 | tf_op jit(solution)/shard_map/ppermute | solution.py:391
  50.3 0.0 collective-permute-done.15.refs_1_
  50.3 2.6 %collective-permute-start.13 = (bf16[320,128]{1,0:T(8,128)(2,1)S(1)}, bf16[320,128]{1,0:T(8,128)(2,1)S(1)}, u32[]{:S(2)}, u32[]{:S(2)}) collective-permute-start(bf16[320,128]{1,0:T(8,128)(2,1)S(1)} %get-tuple-element.80), channel_id=1, source_target_pairs={{0,24},{8,16},{16,8},{24,0},{32,56},{40,48},{48,40},{56,32},{64,88... | collective-permute-start | bytes 245768 | tf_op jit(solution)/shard_map/ppermute | solution.py:391
  52.9 0.0 collective-permute-done.16.refs_2_
  52.9 0.0 collective-permute-done.17.refs_3_
  52.9 1.1 %project_out.2.refs_5_ = f32[8,8,16,320]{3,2,1,0:T(8,128)} custom-call(bf16[320,128]{1,0:T(8,128)(2,1)S(1)} %get-tuple-element.86.refs_0_, bf16[320,128]{1,0:T(8,128)(2,1)S(1)} %collective-permute-done.15.refs_1_, bf16[320,128]{1,0:T(8,128)(2,1)S(1)} %collective-permute-done.16.refs_2_, bf16[320,128]{1,0:T(8,128)(2,1)S(1)} %collective-permute-done.17.refs_3_, ...), custom_call_target="tpu_custom_call" | custom-call | tf_op jit(solution)/shard_map/project_out/pallas_call | solution.py:539
  54.0 0.0 collective-permute-done.11.refs_1_
  54.0 1.1 %collective-permute-done.12.refs_2_ = bf16[320,128]{1,0:T(8,128)(2,1)S(1)} collective-permute-done((bf16[320,128]{1,0:T(8,128)(2,1)S(1)}, bf16[320,128]{1,0:T(8,128)(2,1)S(1)}, u32[]{:S(2)}, u32[]{:S(2)}) %collective-permute-start.12) | collective-permute-done | bytes 81952 | tf_op jit(solution)/shard_map/ppermute | solution.py:391
  55.2 1.9 %collective-permute-done.13.refs_3_ = bf16[320,128]{1,0:T(8,128)(2,1)S(1)} collective-permute-done((bf16[320,128]{1,0:T(8,128)(2,1)S(1)}, bf16[320,128]{1,0:T(8,128)(2,1)S(1)}, u32[]{:S(2)}, u32[]{:S(2)}) %collective-permute-start.13) | collective-permute-done | bytes 81952 | tf_op jit(solution)/shard_map/ppermute | solution.py:391
  57.1 1.1 %project_out.3 = f32[8,8,16,320]{3,2,1,0:T(8,128)} custom-call(bf16[320,128]{1,0:T(8,128)(2,1)S(1)} %get-tuple-element.77.refs_0_, bf16[320,128]{1,0:T(8,128)(2,1)S(1)} %collective-permute-done.11.refs_1_, bf16[320,128]{1,0:T(8,128)(2,1)S(1)} %collective-permute-done.12.refs_2_, ...), custom_call_target="tpu_custom_call", output_to_operand_aliasing={{}: (5, {})} | custom-call | tf_op jit(solution)/shard_map/project_out/pallas_call | solution.py:539
  (2 shorter events, 0.0 us)
Async XLA Ops:
  0.0 8.8 %collective-permute-start.1 = (bf16[3,3,320,320]{3,2,1,0:T(8,128)(2,1)}, bf16[3,3,320,320]{3,2,1,0:T(8,128)(2,1)S(1)}, u32[]{:S(2)}, u32[]{:S(2)}) collective-permute-start(bf16[3,3,320,320]{3,2,1,0:T(8,128)(2,1)} %param.15), channel_id=1, source_target_pairs={{0,8},{8,0},{16,24},{24,16},{32,40},{40,32},{48,56},{56,48},{64,72... | collective-permute-start | bytes 5529608 | tf_op jit(solution)/shard_map/ppermute | solution.py:391
  3.2 7.7 %collective-permute-start = (bf16[3,3,320,320]{3,2,1,0:T(8,128)(2,1)}, bf16[3,3,320,320]{3,2,1,0:T(8,128)(2,1)S(1)}, u32[]{:S(2)}, u32[]{:S(2)}) collective-permute-start(bf16[3,3,320,320]{3,2,1,0:T(8,128)(2,1)} %param.16), channel_id=1, source_target_pairs={{0,8},{8,0},{16,24},{24,16},{32,40},{40,32},{48,56},{56,48},{64,72... | collective-permute-start | bytes 5529608 | tf_op jit(solution)/shard_map/ppermute | solution.py:391
  5.9 7.3 %collective-permute-start.2 = (bf16[2,320,128]{2,1,0:T(8,128)(2,1)S(1)}, bf16[2,320,128]{2,1,0:T(8,128)(2,1)S(1)}, u32[]{:S(2)}, u32[]{:S(2)}) collective-permute-start(bf16[2,320,128]{2,1,0:T(8,128)(2,1)S(1)} %get-tuple-element.56), channel_id=1, source_target_pairs={{1,2},{3,4},{5,6},{2,1},{4,3},{6,5},{9,10},{11,12},{13,14},{10,9},... | collective-permute-start | bytes 491528 | tf_op jit(solution)/shard_map/ppermute | solution.py:436
  6.6 6.6 %collective-permute-start.3 = (bf16[2,320,128]{2,1,0:T(8,128)(2,1)S(1)}, bf16[2,320,128]{2,1,0:T(8,128)(2,1)S(1)}, u32[]{:S(2)}, u32[]{:S(2)}) collective-permute-start(bf16[2,320,128]{2,1,0:T(8,128)(2,1)S(1)} %get-tuple-element.57), channel_id=1, source_target_pairs={{0,1},{2,3},{4,5},{6,7},{1,0},{3,2},{5,4},{7,6},{8,9},{10,11},{12,... | collective-permute-start | bytes 491528 | tf_op jit(solution)/shard_map/ppermute | solution.py:437
  11.0 12.8 %copy-start = (f32[8,33]{1,0:T(8,128)S(1)}, f32[8,33]{1,0:T(8,128)}, u32[]{:S(2)}) copy-start(f32[8,33]{1,0:T(8,128)} %rel_bias.1) | copy-start | bytes 3172
  11.0 12.8 %copy-start.1 = (s32[256]{0:T(256)S(1)}, s32[256]{0:T(256)}, u32[]{:S(2)}) copy-start(s32[256]{0:T(256)} %reach.1) | copy-start | bytes 3076
  13.2 2.2 %collective-permute-start.4 = (bf16[2,320,128]{2,1,0:T(8,128)(2,1)S(1)}, bf16[2,320,128]{2,1,0:T(8,128)(2,1)S(1)}, u32[]{:S(2)}, u32[]{:S(2)}) collective-permute-start(bf16[2,320,128]{2,1,0:T(8,128)(2,1)S(1)} %get-tuple-element.61), channel_id=1, source_target_pairs={{0,8},{8,0},{16,24},{24,16},{32,40},{40,32},{48,56},{56,48},{64,72... | collective-permute-start | bytes 491528 | tf_op jit(solution)/shard_map/ppermute | solution.py:391
  15.4 13.5 %collective-permute-start.5 = (bf16[2,320,128]{2,1,0:T(8,128)(2,1)S(1)}, bf16[2,320,128]{2,1,0:T(8,128)(2,1)S(1)}, u32[]{:S(2)}, u32[]{:S(2)}) collective-permute-start(bf16[2,320,128]{2,1,0:T(8,128)(2,1)S(1)} %get-tuple-element.69), channel_id=1, source_target_pairs={{0,16},{8,24},{16,0},{24,8},{32,48},{40,56},{48,32},{56,40},{64,80... | collective-permute-start | bytes 491528 | tf_op jit(solution)/shard_map/ppermute | solution.py:391
  18.2 10.7 %collective-permute-start.6 = (bf16[2,320,128]{2,1,0:T(8,128)(2,1)S(1)}, bf16[2,320,128]{2,1,0:T(8,128)(2,1)S(1)}, u32[]{:S(2)}, u32[]{:S(2)}) collective-permute-start(bf16[2,320,128]{2,1,0:T(8,128)(2,1)S(1)} %get-tuple-element.82.near), channel_id=1, source_target_pairs={{0,224},{8,232},{16,48},{24,56},{32,0},{40,8},{48,80},{56,88},{64,... | collective-permute-start | bytes 491528 | tf_op jit(solution)/shard_map/ppermute | solution.py:391
  28.9 2.0 %collective-permute-start.7 = (bf16[2,320,128]{2,1,0:T(8,128)(2,1)S(1)}, bf16[2,320,128]{2,1,0:T(8,128)(2,1)S(1)}, u32[]{:S(2)}, u32[]{:S(2)}) collective-permute-start(bf16[2,320,128]{2,1,0:T(8,128)(2,1)S(1)} %get-tuple-element.70), channel_id=1, source_target_pairs={{0,8},{8,0},{16,24},{24,16},{32,40},{40,32},{48,56},{56,48},{64,72... | collective-permute-start | bytes 491528 | tf_op jit(solution)/shard_map/ppermute | solution.py:391
  30.0 7.0 %collective-permute-start.14 = (bf16[2,320,128]{2,1,0:T(8,128)(2,1)S(1)}, bf16[2,320,128]{2,1,0:T(8,128)(2,1)S(1)}, u32[]{:S(2)}, u32[]{:S(2)}) collective-permute-start(bf16[2,320,128]{2,1,0:T(8,128)(2,1)S(1)} %collective-permute-done.5.across_x), channel_id=1, source_target_pairs={{0,32},{8,40},{16,240},{24,248},{32,64},{40,72},{48,16},{56,24},{6... | collective-permute-start | bytes 491528 | tf_op jit(solution)/shard_map/ppermute | solution.py:391
  31.0 10.8 %collective-permute-start.9 = (bf16[2,320,128]{2,1,0:T(8,128)(2,1)S(1)}, bf16[2,320,128]{2,1,0:T(8,128)(2,1)S(1)}, u32[]{:S(2)}, u32[]{:S(2)}) collective-permute-start(bf16[2,320,128]{2,1,0:T(8,128)(2,1)S(1)} %get-tuple-element.73.near), channel_id=1, source_target_pairs={{0,224},{8,232},{16,48},{24,56},{32,0},{40,8},{48,80},{56,88},{64,... | collective-permute-start | bytes 491528 | tf_op jit(solution)/shard_map/ppermute | solution.py:391
  32.8 11.6 %collective-permute-start.10 = (bf16[2,320,128]{2,1,0:T(8,128)(2,1)S(1)}, bf16[2,320,128]{2,1,0:T(8,128)(2,1)S(1)}, u32[]{:S(2)}, u32[]{:S(2)}) collective-permute-start(bf16[2,320,128]{2,1,0:T(8,128)(2,1)S(1)} %get-tuple-element.74), channel_id=1, source_target_pairs={{0,240},{8,248},{16,32},{24,40},{32,16},{40,24},{48,64},{56,72},{6... | collective-permute-start | bytes 491528 | tf_op jit(solution)/shard_map/ppermute | solution.py:391
  34.4 10.6 %collective-permute-start.8 = (bf16[2,320,128]{2,1,0:T(8,128)(2,1)S(1)}, bf16[2,320,128]{2,1,0:T(8,128)(2,1)S(1)}, u32[]{:S(2)}, u32[]{:S(2)}) collective-permute-start(bf16[2,320,128]{2,1,0:T(8,128)(2,1)S(1)} %get-tuple-element.74), channel_id=1, source_target_pairs={{0,16},{8,24},{16,0},{24,8},{32,48},{40,56},{48,32},{56,40},{64,80... | collective-permute-start | bytes 491528 | tf_op jit(solution)/shard_map/ppermute | solution.py:391
  40.2 10.1 %collective-permute-start.15 = (bf16[320,128]{1,0:T(8,128)(2,1)S(1)}, bf16[320,128]{1,0:T(8,128)(2,1)S(1)}, u32[]{:S(2)}, u32[]{:S(2)}) collective-permute-start(bf16[320,128]{1,0:T(8,128)(2,1)S(1)} %get-tuple-element.87), channel_id=1, source_target_pairs={{0,8},{8,0},{16,24},{24,16},{32,40},{40,32},{48,56},{56,48},{64,72... | collective-permute-start | bytes 245768 | tf_op jit(solution)/shard_map/ppermute | solution.py:391
  41.1 11.8 %collective-permute-start.16 = (bf16[320,128]{1,0:T(8,128)(2,1)S(1)}, bf16[320,128]{1,0:T(8,128)(2,1)S(1)}, u32[]{:S(2)}, u32[]{:S(2)}) collective-permute-start(bf16[320,128]{1,0:T(8,128)(2,1)S(1)} %get-tuple-element.88), channel_id=1, source_target_pairs={{0,16},{8,24},{16,0},{24,8},{32,48},{40,56},{48,32},{56,40},{64,80... | collective-permute-start | bytes 245768 | tf_op jit(solution)/shard_map/ppermute | solution.py:391
  41.9 11.0 %collective-permute-start.17 = (bf16[320,128]{1,0:T(8,128)(2,1)S(1)}, bf16[320,128]{1,0:T(8,128)(2,1)S(1)}, u32[]{:S(2)}, u32[]{:S(2)}) collective-permute-start(bf16[320,128]{1,0:T(8,128)(2,1)S(1)} %get-tuple-element.89), channel_id=1, source_target_pairs={{0,24},{8,16},{16,8},{24,0},{32,56},{40,48},{48,40},{56,32},{64,88... | collective-permute-start | bytes 245768 | tf_op jit(solution)/shard_map/ppermute | solution.py:391
  48.2 5.8 %collective-permute-start.11 = (bf16[320,128]{1,0:T(8,128)(2,1)S(1)}, bf16[320,128]{1,0:T(8,128)(2,1)S(1)}, u32[]{:S(2)}, u32[]{:S(2)}) collective-permute-start(bf16[320,128]{1,0:T(8,128)(2,1)S(1)} %get-tuple-element.78), channel_id=1, source_target_pairs={{0,8},{8,0},{16,24},{24,16},{32,40},{40,32},{48,56},{56,48},{64,72... | collective-permute-start | bytes 245768 | tf_op jit(solution)/shard_map/ppermute | solution.py:391
  49.7 5.5 %collective-permute-start.12 = (bf16[320,128]{1,0:T(8,128)(2,1)S(1)}, bf16[320,128]{1,0:T(8,128)(2,1)S(1)}, u32[]{:S(2)}, u32[]{:S(2)}) collective-permute-start(bf16[320,128]{1,0:T(8,128)(2,1)S(1)} %get-tuple-element.79), channel_id=1, source_target_pairs={{0,16},{8,24},{16,0},{24,8},{32,48},{40,56},{48,32},{56,40},{64,80... | collective-permute-start | bytes 245768 | tf_op jit(solution)/shard_map/ppermute | solution.py:391
  50.3 6.8 %collective-permute-start.13 = (bf16[320,128]{1,0:T(8,128)(2,1)S(1)}, bf16[320,128]{1,0:T(8,128)(2,1)S(1)}, u32[]{:S(2)}, u32[]{:S(2)}) collective-permute-start(bf16[320,128]{1,0:T(8,128)(2,1)S(1)} %get-tuple-element.80), channel_id=1, source_target_pairs={{0,24},{8,16},{16,8},{24,0},{32,56},{40,48},{48,40},{56,32},{64,88... | collective-permute-start | bytes 245768 | tf_op jit(solution)/shard_map/ppermute | solution.py:391
